TPU v7x, 32 devices: a whole 2x2x4 slice. The times are simulated.
32 devices in a mesh: segment: 4 (over x, core), graph: 8 (over z, y).
Axes of the slice: x: 2, y: 2, z: 4, core: 2. Of those that a mesh axis runs over, the one named last changes fastest.
Arguments:
- state: float32 [4, 4096, 1024], P('segment', 'graph'), may hold values from -6 to 6
- initial: float32 [4, 4096, 1024], P('segment', 'graph'), may hold values from -6 to 6
- fresh: float32 [4096, 1024], P('graph'), may hold values from -6 to 6
- weights: float32 [4, 1024, 1024], P('segment'), may hold values from -0.1875 to 0.1875
- wants: int32 [8, 4, 1], P('graph'), may hold values from 0 to 3
- adj_slot: int32 [32, 4], P('graph'), may hold values from 0 to 7, as said below
- adj_count: int32 [32], P('graph'), may hold values from 2 to 4, as said below
- adj_vals: float32 [32, 4, 128, 128], P('graph'), may hold values from -0.25 to 0.25
Outputs:
- handed: float32 [4, 4096, 1024], P('segment', 'graph')
- advanced: float32 [4, 4096, 1024], P('segment', 'graph')
Inputs may be any that keep to these rules, and one draw needn't show every extreme that they name: `adj_slot`: every entry of a destination block's row at k < 2 names a slot past the partition's own blocks, and every such slot of a partition is named at some k < 2 of one of its blocks. `adj_count`: each partition has a block with exactly 4 nonzero blocks.
All inputs are finite; a program needn't handle non-finite values.
Results may differ from a plain program's by a relative error of at most 0.0001.
Values sent between devices are 32-bit elements; how exact they have to be, the bound alone decides.
No kernel may reach another device: no remote copies, remote signals or barrier semaphores. Data moves between devices by JAX's collectives and lax.ppermute only.
A program may use at most 128 MiB of HBM per device.

v0:
```python
import jax
import jax.numpy as jnp
from jax import lax
from jax.sharding import PartitionSpec as P

D = 1024
BLK = 128
KMAX = 4
REACH = 2


def from_behind(value, axis, by):
    peers = lax.axis_size(axis)
    pairs = [(i, i + by) for i in range(peers) if 0 <= i + by < peers]
    return lax.ppermute(value, axis, pairs)


def offset_list():
    found = []
    for radius in range(1, REACH + 1):
        found.append(radius)
        found.append(-radius)
    return found


def local_layer(feats, first_feats, weight, layer_index, received, adj_slot, adj_count, adj_vals):
    nblocks = feats.shape[0] // BLK
    row_blocks = feats.reshape(nblocks, BLK, D)
    sources = jnp.concatenate([row_blocks, received], axis=0)
    selected = sources[adj_slot]
    live = (jnp.arange(KMAX, dtype=jnp.int32)[None, :] < adj_count[:, None]).astype(jnp.float32)
    values = adj_vals * live[:, :, None, None]
    agg = jnp.einsum("bkij,bkjd->bid", values, selected, precision=lax.Precision.HIGHEST).reshape(
        feats.shape[0], D
    )
    mixed = 0.9 * agg + 0.1 * first_feats
    beta = jnp.log(0.5 / (layer_index + 1.0) + 1.0)
    product = jnp.dot(
        mixed, weight, precision=lax.Precision.HIGHEST, preferred_element_type=jnp.float32
    )
    return jax.nn.relu((1.0 - beta) * mixed + beta * product)


def shards(state, initial, fresh, weights, wants, adj_slot, adj_count, adj_vals):
    section = lax.axis_index("segment")
    layer_index = section.astype(jnp.float32)
    weight = weights[0]
    offsets = offset_list()
    asked = [
        from_behind(wants[0, position], "graph", -shift_by)
        for position, shift_by in enumerate(offsets)
    ]

    def fetch(feats):
        row_blocks = feats.reshape(feats.shape[0] // BLK, BLK, D)
        pieces = [
            from_behind(row_blocks[asked[position]], "graph", shift_by)
            for position, shift_by in enumerate(offsets)
        ]
        return jnp.concatenate(pieces, axis=0)

    feats = state[0]
    first_feats = initial[0]
    first_out = local_layer(
        feats, first_feats, weight, layer_index, fetch(feats), adj_slot, adj_count, adj_vals
    )
    came_feats, came_first = from_behind((first_out, first_feats), "segment", 1)
    is_first = section == 0
    next_feats = jnp.where(is_first, fresh, came_feats)
    next_first = jnp.where(is_first, fresh, came_first)
    second_out = local_layer(
        next_feats,
        next_first,
        weight,
        layer_index,
        fetch(next_feats),
        adj_slot,
        adj_count,
        adj_vals,
    )
    return (first_out[None], second_out[None])


def solution(mesh):
    return jax.shard_map(
        shards,
        mesh=mesh,
        in_specs=(
            P("segment", "graph", None),
            P("segment", "graph", None),
            P("graph", None),
            P("segment", None, None),
            P("graph", None, None),
            P("graph", None),
            P("graph"),
            P("graph", None, None, None),
        ),
        out_specs=(P("segment", "graph", None), P("segment", "graph", None)),
        check_vma=False,
    )
```

profile of v0, /device:TPU:2, one launch (start us, length us, event | category | flops | bytes accessed | tf_op | source)
XLA Modules:
  0.0 156.7 jit_solution(16163748717954849814)
XLA Ops:
  0.6 1.5 fusion.16
  2.1 1.3 collective-permute-start
  3.4 5.1 %collective-permute-start.2 = (s32[1]{0:T(128)}, s32[1]{0:T(128)}, u32[]{:S(2)}, u32[]{:S(2)}) collective-permute-start(s32[1]{0:T(128)} %bitcast.3), channel_id=1, source_target_pairs={{0,1},{1,2},{2,3},{3,4},{4,5},{5,6},{6,7},{8,9},{9,10},{10,11},{11... | collective-permute-start | bytes 20 | tf_op jit(solution)/shard_map/ppermute | solution.py:15
  8.4 1.3 collective-permute-start.4
  9.8 5.2 %collective-permute-start.6 = (s32[1]{0:T(128)}, s32[1]{0:T(128)}, u32[]{:S(2)}, u32[]{:S(2)}) collective-permute-start(s32[1]{0:T(128)} %bitcast.7), channel_id=1, source_target_pairs={{0,2},{1,3},{2,4},{3,5},{4,6},{5,7},{8,10},{9,11},{10,12},{11,13},... | collective-permute-start | bytes 20 | tf_op jit(solution)/shard_map/ppermute | solution.py:15
  15.0 1.8 %broadcast_multiply_fusion = f32[1,512,1024]{2,1,0:T(8,128)S(1)} fusion(f32[1,512,1024]{2,1,0:T(8,128)} %param.9), kind=kLoop, calls=%fused_computation.14 | loop fusion | flops 524288 | bytes 4194304 | tf_op jit(solution)/shard_map/mul | solution.py:36
  24.5 1.2 constant_dynamic-slice_fusion.4
  25.7 3.9 %collective-permute-start.1 = (f32[1,128,1024]{2,1,0:T(8,128)}, f32[1,128,1024]{2,1,0:T(8,128)S(1)}, u32[]{:S(2)}, u32[]{:S(2)}) collective-permute-start(f32[1,128,1024]{2,1,0:T(8,128)} %get-tuple-element.97), channel_id=1, source_target_pairs={{0,1},{1,2},{2,3},{3,4},{4,5},{5,6},{6,7},{8,9},{9,10},{10,11},{11... | collective-permute-start | bytes 1572872 | tf_op jit(solution)/shard_map/ppermute | solution.py:15
  29.8 1.3 collective-permute-start.3
  31.2 4.1 %collective-permute-start.5 = (f32[1,128,1024]{2,1,0:T(8,128)}, f32[1,128,1024]{2,1,0:T(8,128)S(1)}, u32[]{:S(2)}, u32[]{:S(2)}) collective-permute-start(f32[1,128,1024]{2,1,0:T(8,128)} %get-tuple-element.95), channel_id=1, source_target_pairs={{0,2},{1,3},{2,4},{3,5},{4,6},{5,7},{8,10},{9,11},{10,12},{11,13},... | collective-permute-start | bytes 1572872 | tf_op jit(solution)/shard_map/ppermute | solution.py:15
  35.3 1.3 collective-permute-start.7
  36.6 3.2 %constant_dynamic-update-slice_fusion.4 = f32[8,128,1024]{2,1,0:T(8,128)} fusion(f32[4,128,1024]{2,1,0:T(8,128)} %bitcast.54), kind=kLoop, calls=%fused_computation.24 | loop fusion | bytes 4194304
  39.8 11.3 %collective-permute-done.1 = f32[1,128,1024]{2,1,0:T(8,128)S(1)} collective-permute-done((f32[1,128,1024]{2,1,0:T(8,128)}, f32[1,128,1024]{2,1,0:T(8,128)S(1)}, u32[]{:S(2)}, u32[]{:S(2)}) %collective-permute-start.1) | collective-permute-done | bytes 524320 | tf_op jit(solution)/shard_map/ppermute | solution.py:15
  53.6 1.5 collective-permute-done.7
  56.0 6.6 %gather_fusion = f32[16,128,1024]{2,1,0:T(8,128)} fusion(f32[8,128,1024]{2,1,0:T(8,128)} %constant_dynamic-update-slice_fusion, s32[1024]{0:T(1024)S(1)} %pad_clamp_fusion), kind=kCustom, calls=%fused_computation | custom fusion | bytes 16777280 | tf_op jit(solution)/shard_map/gather | solution.py:30
  62.6 7.4 %fusion.17 = (f32[4,128,1024]{2,1,0:T(8,128)S(1)}, f32[4,128,1024]{2,1,0:T(8,128)S(1)}) fusion(f32[4,128,1024]{2,1,0:T(8,128)S(1)} %bitcast.53, f32[4,4,128,1024]{3,2,1,0:T(8,128)} %bitcast.48, f32[4,4,128,128]{3,2,1,0:T(8,128)S(1)} %copy-done.4, f32[4,4]{1,0:T(4,128)S(1)} %fusion.15), kind=kOutput, calls=%fused_computation.43 | convolution fusion | flops 3222536192 | bytes 15728704 | tf_op jit(solution)/shard_map/bkij,bkjd->bid/dot_general | solution.py:33
  70.0 9.6 %fusion.6 = f32[512,1024]{1,0:T(8,128)} fusion(f32[4,128,1024]{2,1,0:T(8,128)S(1)} %get-tuple-element.103, f32[512,1024]{1,0:T(8,128)S(1)} %bitcast.52, f32[1,1024,1024]{2,1,0:T(8,128)S(1)} %copy-done, f32[]{:T(128)S(6)} %log.4, f32[]{:T(128)S(6)} %sub.4, f32[1,512,1024]{2,1,0:T(8,128)} %param.9), kind=kOutput, calls=%fused_computation.11 | convolution fusion | flops 6445596672 | bytes 12582920 | tf_op jit(solution)/shard_map/dot_general | solution.py:38
  79.5 1.9 %collective-permute-start.8 = (f32[512,1024]{1,0:T(8,128)}, f32[512,1024]{1,0:T(8,128)}, u32[]{:S(2)}, u32[]{:S(2)}) collective-permute-start(f32[512,1024]{1,0:T(8,128)} %fusion.6), channel_id=1, source_target_pairs={{0,8},{8,16},{16,24},{1,9},{9,17},{17,25},{2,10},{10,18},{18,26},{... | collective-permute-start | bytes 6291464 | tf_op jit(solution)/shard_map/ppermute | solution.py:15
  81.5 1.9 %collective-permute-start.13 = (f32[512,1024]{1,0:T(8,128)}, f32[512,1024]{1,0:T(8,128)}, u32[]{:S(2)}, u32[]{:S(2)}) collective-permute-start(f32[512,1024]{1,0:T(8,128)} %bitcast.13), channel_id=1, source_target_pairs={{0,8},{8,16},{16,24},{1,9},{9,17},{17,25},{2,10},{10,18},{18,26},{... | collective-permute-start | bytes 6291464 | tf_op jit(solution)/shard_map/ppermute | solution.py:15
  83.4 23.8 %collective-permute-done.8 = f32[512,1024]{1,0:T(8,128)} collective-permute-done((f32[512,1024]{1,0:T(8,128)}, f32[512,1024]{1,0:T(8,128)}, u32[]{:S(2)}, u32[]{:S(2)}) %collective-permute-start.8) | collective-permute-done | bytes 2097184 | tf_op jit(solution)/shard_map/ppermute | solution.py:15
  107.2 2.0 %broadcast_select_fusion = f32[512,1024]{1,0:T(8,128)S(1)} fusion(f32[512,1024]{1,0:T(8,128)S(1)} %copy-done.3, f32[512,1024]{1,0:T(8,128)} %collective-permute-done.8, pred[]{:T(512)S(6)} %eq.3), kind=kLoop, calls=%fused_computation.15 | loop fusion | flops 524288 | bytes 6291457 | tf_op jit(solution)/shard_map/jit(_where)/select_n | solution.py:69
  109.5 2.8 %collective-permute-start.9 = (f32[1,128,1024]{2,1,0:T(8,128)S(1)}, f32[1,128,1024]{2,1,0:T(8,128)S(1)}, u32[]{:S(2)}, u32[]{:S(2)}) collective-permute-start(f32[1,128,1024]{2,1,0:T(8,128)S(1)} %get-tuple-element.93), channel_id=1, source_target_pairs={{0,1},{1,2},{2,3},{3,4},{4,5},{5,6},{6,7},{8,9},{9,10},{10,11},{11... | collective-permute-start | bytes 1572872 | tf_op jit(solution)/shard_map/ppermute | solution.py:15
  112.3 1.3 collective-permute-start.10
  113.6 6.5 %collective-permute-start.11 = (f32[1,128,1024]{2,1,0:T(8,128)S(1)}, f32[1,128,1024]{2,1,0:T(8,128)S(1)}, u32[]{:S(2)}, u32[]{:S(2)}) collective-permute-start(f32[1,128,1024]{2,1,0:T(8,128)S(1)} %get-tuple-element.91), channel_id=1, source_target_pairs={{0,2},{1,3},{2,4},{3,5},{4,6},{5,7},{8,10},{9,11},{10,12},{11,13},... | collective-permute-start | bytes 1572872 | tf_op jit(solution)/shard_map/ppermute | solution.py:15
  120.1 1.5 collective-permute-start.12
  121.6 1.5 constant_dynamic-update-slice_fusion.9
  124.8 2.0 %collective-permute-done.11 = f32[1,128,1024]{2,1,0:T(8,128)S(1)} collective-permute-done((f32[1,128,1024]{2,1,0:T(8,128)S(1)}, f32[1,128,1024]{2,1,0:T(8,128)S(1)}, u32[]{:S(2)}, u32[]{:S(2)}) %collective-permute-start.11) | collective-permute-done | bytes 524320 | tf_op jit(solution)/shard_map/ppermute | solution.py:15
  127.6 3.6 %collective-permute-done.12 = f32[1,128,1024]{2,1,0:T(8,128)S(1)} collective-permute-done((f32[1,128,1024]{2,1,0:T(8,128)S(1)}, f32[1,128,1024]{2,1,0:T(8,128)S(1)}, u32[]{:S(2)}, u32[]{:S(2)}) %collective-permute-start.12) | collective-permute-done | bytes 524320 | tf_op jit(solution)/shard_map/ppermute | solution.py:15
  132.0 6.5 %gather_fusion.1 = f32[16,128,1024]{2,1,0:T(8,128)} fusion(f32[8,128,1024]{2,1,0:T(8,128)} %constant_dynamic-update-slice_fusion.5, s32[1024]{0:T(1024)S(1)} %pad_clamp_fusion), kind=kCustom, calls=%fused_computation.1 | custom fusion | bytes 16777280 | tf_op jit(solution)/shard_map/gather | solution.py:30
  138.6 7.1 %bitcast_multiply_fusion = f32[4,128,1024]{2,1,0:T(8,128)S(1)} fusion(f32[4,4,128,1024]{3,2,1,0:T(8,128)} %bitcast.49, f32[4,4,128,128]{3,2,1,0:T(8,128)S(1)} %copy-done.4, f32[4,4]{1,0:T(4,128)S(1)} %fusion.15), kind=kOutput, calls=%fused_computation.7 | convolution fusion | flops 3222011904 | bytes 11534400 | tf_op jit(solution)/shard_map/bkij,bkjd->bid/dot_general | solution.py:33
  145.7 2.4 %bitcast_add_fusion = f32[512,1024]{1,0:T(8,128)S(1)} fusion(f32[4,128,1024]{2,1,0:T(8,128)S(1)} %bitcast_multiply_fusion, f32[512,1024]{1,0:T(8,128)S(1)} %copy-done.3, f32[512,1024]{1,0:T(8,128)} %collective-permute-done.13, pred[]{:T(512)S(6)} %eq.3), kind=kLoop, calls=%fused_computation.6 | loop fusion | flops 1572864 | bytes 8388609 | tf_op jit(solution)/shard_map/add | solution.py:36
  148.5 8.3 %maximum_bitcast_fusion = f32[1,512,1024]{2,1,0:T(8,128)} fusion(f32[512,1024]{1,0:T(8,128)S(1)} %bitcast_add_fusion, f32[1,1024,1024]{2,1,0:T(8,128)S(1)} %copy-done.1, f32[]{:T(128)S(6)} %log.4, f32[]{:T(128)S(6)} %sub.4), kind=kOutput, calls=%fused_computation.13 | convolution fusion | flops 6444548096 | bytes 8388616 | tf_op jit(solution)/shard_map/dot_general | solution.py:38
  (36 shorter events, 7.5 us)
Async XLA Ops:
  2.1 14.7 %collective-permute-start = (s32[1]{0:T(128)}, s32[1]{0:T(128)}, u32[]{:S(2)}, u32[]{:S(2)}) collective-permute-start(s32[1]{0:T(128)} %bitcast.1), channel_id=1, source_target_pairs={{1,0},{2,1},{3,2},{4,3},{5,4},{6,5},{7,6},{9,8},{10,9},{11,10},{12... | collective-permute-start | bytes 20 | tf_op jit(solution)/shard_map/ppermute | solution.py:15
  3.4 14.7 %collective-permute-start.2 = (s32[1]{0:T(128)}, s32[1]{0:T(128)}, u32[]{:S(2)}, u32[]{:S(2)}) collective-permute-start(s32[1]{0:T(128)} %bitcast.3), channel_id=1, source_target_pairs={{0,1},{1,2},{2,3},{3,4},{4,5},{5,6},{6,7},{8,9},{9,10},{10,11},{11... | collective-permute-start | bytes 20 | tf_op jit(solution)/shard_map/ppermute | solution.py:15
  8.4 10.8 %collective-permute-start.4 = (s32[1]{0:T(128)}, s32[1]{0:T(128)}, u32[]{:S(2)}, u32[]{:S(2)}) collective-permute-start(s32[1]{0:T(128)} %bitcast.5), channel_id=1, source_target_pairs={{2,0},{3,1},{4,2},{5,3},{6,4},{7,5},{10,8},{11,9},{12,10},{13,11},... | collective-permute-start | bytes 20 | tf_op jit(solution)/shard_map/ppermute | solution.py:15
  9.7 14.7 %copy-start.2 = (f32[1,512,1024]{2,1,0:T(8,128)S(1)}, f32[1,512,1024]{2,1,0:T(8,128)}, u32[]{:S(2)}) copy-start(f32[1,512,1024]{2,1,0:T(8,128)} %param.8) | copy-start | bytes 6291460
  9.8 10.9 %collective-permute-start.6 = (s32[1]{0:T(128)}, s32[1]{0:T(128)}, u32[]{:S(2)}, u32[]{:S(2)}) collective-permute-start(s32[1]{0:T(128)} %bitcast.7), channel_id=1, source_target_pairs={{0,2},{1,3},{2,4},{3,5},{4,6},{5,7},{8,10},{9,11},{10,12},{11,13},... | collective-permute-start | bytes 20 | tf_op jit(solution)/shard_map/ppermute | solution.py:15
  24.5 5.1 %copy-start.5 = (s32[4,4]{1,0:T(4,128)S(1)}, s32[4,4]{1,0:T(4,128)}, u32[]{:S(2)}) copy-start(s32[4,4]{1,0:T(4,128)} %param.13) | copy-start | bytes 196
  24.5 6.6 %copy-start.6 = (s32[4]{0:T(128)S(1)}, s32[4]{0:T(128)}, u32[]{:S(2)}) copy-start(s32[4]{0:T(128)} %param.14) | copy-start | bytes 52
  25.7 25.4 %collective-permute-start.1 = (f32[1,128,1024]{2,1,0:T(8,128)}, f32[1,128,1024]{2,1,0:T(8,128)S(1)}, u32[]{:S(2)}, u32[]{:S(2)}) collective-permute-start(f32[1,128,1024]{2,1,0:T(8,128)} %get-tuple-element.97), channel_id=1, source_target_pairs={{0,1},{1,2},{2,3},{3,4},{4,5},{5,6},{6,7},{8,9},{9,10},{10,11},{11... | collective-permute-start | bytes 1572872 | tf_op jit(solution)/shard_map/ppermute | solution.py:15
  29.8 22.2 %collective-permute-start.3 = (f32[1,128,1024]{2,1,0:T(8,128)}, f32[1,128,1024]{2,1,0:T(8,128)S(1)}, u32[]{:S(2)}, u32[]{:S(2)}) collective-permute-start(f32[1,128,1024]{2,1,0:T(8,128)} %get-tuple-element.96), channel_id=1, source_target_pairs={{1,0},{2,1},{3,2},{4,3},{5,4},{6,5},{7,6},{9,8},{10,9},{11,10},{12... | collective-permute-start | bytes 1572872 | tf_op jit(solution)/shard_map/ppermute | solution.py:15
  31.2 21.7 %collective-permute-start.5 = (f32[1,128,1024]{2,1,0:T(8,128)}, f32[1,128,1024]{2,1,0:T(8,128)S(1)}, u32[]{:S(2)}, u32[]{:S(2)}) collective-permute-start(f32[1,128,1024]{2,1,0:T(8,128)} %get-tuple-element.95), channel_id=1, source_target_pairs={{0,2},{1,3},{2,4},{3,5},{4,6},{5,7},{8,10},{9,11},{10,12},{11,13},... | collective-permute-start | bytes 1572872 | tf_op jit(solution)/shard_map/ppermute | solution.py:15
  35.3 19.9 %collective-permute-start.7 = (f32[1,128,1024]{2,1,0:T(8,128)S(1)}, f32[1,128,1024]{2,1,0:T(8,128)S(1)}, u32[]{:S(2)}, u32[]{:S(2)}) collective-permute-start(f32[1,128,1024]{2,1,0:T(8,128)S(1)} %get-tuple-element.94), channel_id=1, source_target_pairs={{2,0},{3,1},{4,2},{5,3},{6,4},{7,5},{10,8},{11,9},{12,10},{13,11},... | collective-permute-start | bytes 1572872 | tf_op jit(solution)/shard_map/ppermute | solution.py:15
  56.0 6.6 %copy-start.4 = (f32[4,4,128,128]{3,2,1,0:T(8,128)S(1)}, f32[4,4,128,128]{3,2,1,0:T(8,128)}, u32[]{:S(2)}) copy-start(f32[4,4,128,128]{3,2,1,0:T(8,128)} %param.15) | copy-start | bytes 3145732
  62.6 7.4 %copy-start = (f32[1,1024,1024]{2,1,0:T(8,128)S(1)}, f32[1,1024,1024]{2,1,0:T(8,128)}, u32[]{:S(2)}) copy-start(f32[1,1024,1024]{2,1,0:T(8,128)} %param.11) | copy-start | bytes 12582916
  70.0 37.2 %copy-start.3 = (f32[512,1024]{1,0:T(8,128)S(1)}, f32[512,1024]{1,0:T(8,128)}, u32[]{:S(2)}) copy-start(f32[512,1024]{1,0:T(8,128)} %param.10) | copy-start | bytes 6291460
  79.5 27.7 %collective-permute-start.8 = (f32[512,1024]{1,0:T(8,128)}, f32[512,1024]{1,0:T(8,128)}, u32[]{:S(2)}, u32[]{:S(2)}) collective-permute-start(f32[512,1024]{1,0:T(8,128)} %fusion.6), channel_id=1, source_target_pairs={{0,8},{8,16},{16,24},{1,9},{9,17},{17,25},{2,10},{10,18},{18,26},{... | collective-permute-start | bytes 6291464 | tf_op jit(solution)/shard_map/ppermute | solution.py:15
  81.5 64.2 %collective-permute-start.13 = (f32[512,1024]{1,0:T(8,128)}, f32[512,1024]{1,0:T(8,128)}, u32[]{:S(2)}, u32[]{:S(2)}) collective-permute-start(f32[512,1024]{1,0:T(8,128)} %bitcast.13), channel_id=1, source_target_pairs={{0,8},{8,16},{16,24},{1,9},{9,17},{17,25},{2,10},{10,18},{18,26},{... | collective-permute-start | bytes 6291464 | tf_op jit(solution)/shard_map/ppermute | solution.py:15
  109.5 13.7 %collective-permute-start.9 = (f32[1,128,1024]{2,1,0:T(8,128)S(1)}, f32[1,128,1024]{2,1,0:T(8,128)S(1)}, u32[]{:S(2)}, u32[]{:S(2)}) collective-permute-start(f32[1,128,1024]{2,1,0:T(8,128)S(1)} %get-tuple-element.93), channel_id=1, source_target_pairs={{0,1},{1,2},{2,3},{3,4},{4,5},{5,6},{6,7},{8,9},{9,10},{10,11},{11... | collective-permute-start | bytes 1572872 | tf_op jit(solution)/shard_map/ppermute | solution.py:15
  112.3 11.7 %collective-permute-start.10 = (f32[1,128,1024]{2,1,0:T(8,128)S(1)}, f32[1,128,1024]{2,1,0:T(8,128)S(1)}, u32[]{:S(2)}, u32[]{:S(2)}) collective-permute-start(f32[1,128,1024]{2,1,0:T(8,128)S(1)} %get-tuple-element.92), channel_id=1, source_target_pairs={{1,0},{2,1},{3,2},{4,3},{5,4},{6,5},{7,6},{9,8},{10,9},{11,10},{12... | collective-permute-start | bytes 1572872 | tf_op jit(solution)/shard_map/ppermute | solution.py:15
  113.6 13.2 %collective-permute-start.11 = (f32[1,128,1024]{2,1,0:T(8,128)S(1)}, f32[1,128,1024]{2,1,0:T(8,128)S(1)}, u32[]{:S(2)}, u32[]{:S(2)}) collective-permute-start(f32[1,128,1024]{2,1,0:T(8,128)S(1)} %get-tuple-element.91), channel_id=1, source_target_pairs={{0,2},{1,3},{2,4},{3,5},{4,6},{5,7},{8,10},{9,11},{10,12},{11,13},... | collective-permute-start | bytes 1572872 | tf_op jit(solution)/shard_map/ppermute | solution.py:15
  120.1 11.1 %collective-permute-start.12 = (f32[1,128,1024]{2,1,0:T(8,128)S(1)}, f32[1,128,1024]{2,1,0:T(8,128)S(1)}, u32[]{:S(2)}, u32[]{:S(2)}) collective-permute-start(f32[1,128,1024]{2,1,0:T(8,128)S(1)} %get-tuple-element.90), channel_id=1, source_target_pairs={{2,0},{3,1},{4,2},{5,3},{6,4},{7,5},{10,8},{11,9},{12,10},{13,11},... | collective-permute-start | bytes 1572872 | tf_op jit(solution)/shard_map/ppermute | solution.py:15
  145.6 2.8 %copy-start.1 = (f32[1,1024,1024]{2,1,0:T(8,128)S(1)}, f32[1,1024,1024]{2,1,0:T(8,128)}, u32[]{:S(2)}) copy-start(f32[1,1024,1024]{2,1,0:T(8,128)} %param.11) | copy-start | bytes 12582916
where the time goes:
time: 157 us
  waiting for transfers between devices  42.2 us (27%)
  starting transfers between devices  39.3 us (25%)
  matrix products  32.3 us (21%)
  local copies, waits for them, and re-layouts  28 us (18%)
  between operations  8.68 us (6%)
  other arithmetic  6.28 us (4%)
    ppermute x14, waiting for transfers between devices, from_behind(): return lax.ppermute(value, axis, pairs)  42.2 us
    ppermute x14, starting transfers between devices, from_behind(): return lax.ppermute(value, axis, pairs)  39.3 us
    dot_general x2, matrix products, local_layer(): jnp.dot(mixed, weight, precision=lax.Precision.HIGHEST, preferred_element...  17.9 us
    dot_general x2, matrix products, local_layer(): jnp.einsum('bkij,bkjd->bid', values, selected, precision=lax.Precision.HI...  14.4 us
    gather x2, local copies, waits for them, and re-layouts, local_layer(): selected = sources[adj_slot]  13.1 us
    unnamed x22, local copies, waits for them, and re-layouts  10.2 us
  transfers between devices with their start and end apart: 14, of which 5 were waited for; matrix products, arithmetic and copies ran while one was open for 18% of the time, Pallas kernels for 0%

commit v1 on v0

v1 whole, which is shorter than its diff:
```python
import functools

import jax
import jax.numpy as jnp
from jax import lax
from jax.experimental import pallas as pl
from jax.experimental.pallas import tpu as pltpu
from jax.sharding import PartitionSpec as P

BLK = 128
REACH = 2
F32 = jnp.float32
BF16 = jnp.bfloat16
SWAPS = ((1, 0), (2, 0), (2, 1), (1, 1))
VMEM = pl.BlockSpec(memory_space=pltpu.VMEM)
SMEM = pl.BlockSpec(memory_space=pltpu.SMEM)
HBM = pl.BlockSpec(memory_space=pl.ANY)
ONE = pltpu.SemaphoreType.DMA


def swap(value, stride, phase):
    peers = lax.axis_size("graph")
    pairs = []
    for low in range(peers - stride):
        if (low // stride) % 2 == phase:
            pairs += [(low, low + stride), (low + stride, low)]
    return lax.ppermute(value, "graph", sorted(pairs))


def hand_on(value):
    peers = lax.axis_size("segment")
    return lax.ppermute(value, "segment", [(i, (i + 1) % peers) for i in range(peers)])


def halves(value):
    high = value.astype(BF16)
    return high, (value - high.astype(F32)).astype(BF16)


def dot3(a, b):
    times = functools.partial(jnp.dot, preferred_element_type=F32)
    return times(a[0], b[0]) + (times(a[0], b[1]) + times(a[1], b[0]))


def call(kernel, outs, in_specs, out_specs, flops=0, nbytes=0, scratch=(), grid=None, vmem=32):
    extra = {} if grid is None else {"grid": grid}
    return pl.pallas_call(
        kernel,
        out_shape=outs,
        in_specs=in_specs,
        out_specs=out_specs,
        scratch_shapes=list(scratch),
        cost_estimate=pl.CostEstimate(flops=flops, bytes_accessed=nbytes, transcendentals=0),
        compiler_params=pltpu.CompilerParams(vmem_limit_bytes=vmem * 2**20),
        **extra,
    )


def dense_kernel(place_ref, slot_ref, count_ref, vals_ref, high_ref, low_ref, total):
    total[...] = jnp.zeros_like(total)
    blocks, most = vals_ref.shape[:2]
    for b in range(blocks):
        for k in range(most):
            slot = slot_ref[b, k]
            past = jnp.maximum(slot - blocks, 0)
            column = jnp.where(slot < blocks, slot, blocks + place_ref[past])
            scale = jnp.where(k < count_ref[b], 0.9, 0.0).astype(F32)
            where = pl.ds(pl.multiple_of(column * BLK, BLK), BLK)
            total[b * BLK : (b + 1) * BLK, where] += scale * vals_ref[b, k]
    high, low = halves(total[...])
    high_ref[...] = high
    low_ref[...] = low


def dense(place, slots, counts, vals):
    rows = vals.shape[0] * BLK
    width = rows + 2 * REACH * BLK
    shape = jax.ShapeDtypeStruct((rows, width), BF16)
    return call(
        dense_kernel,
        (shape, shape),
        [SMEM, SMEM, SMEM, VMEM],
        (VMEM, VMEM),
        nbytes=4 * vals.size + 4 * rows * width,
        scratch=[pltpu.VMEM((rows, width), F32)],
    )(place, slots, counts, vals)


def pick_kernel(index_ref, *refs, count):
    got, source, outs, sem = refs[:count], refs[count], refs[count + 1 : -1], refs[-1]
    copies = []
    for i in range(count):
        row = pl.multiple_of(got[i][index_ref[i]] * BLK, BLK)
        copies.append(pltpu.make_async_copy(source.at[pl.ds(row, BLK)], outs[i], sem.at[i]))
    for copy in copies:
        copy.start()
    for copy in copies:
        copy.wait()


def pick(index, got, source):
    count = len(got)
    shape = jax.ShapeDtypeStruct((BLK, source.shape[1]), F32)
    return call(
        functools.partial(pick_kernel, count=count),
        (shape,) * count,
        [SMEM] * (1 + count) + [HBM],
        (HBM,) * count,
        nbytes=8 * count * BLK * source.shape[1],
        scratch=[ONE((count,))],
    )(index, *got, source)


def own_kernel(high_ref, low_ref, feats_ref, first_ref, out_ref):
    a = (high_ref[...], low_ref[...])
    out_ref[...] = dot3(a, halves(feats_ref[...])) + 0.1 * first_ref[...]


def own_part(adj, feats, first, column=0, width=None, tile=256):
    rows = feats.shape[0]
    width = feats.shape[1] if width is None else width
    start = column // tile
    spec = pl.BlockSpec((rows, rows), lambda i: (0, 0))
    cut = pl.BlockSpec((rows, tile), lambda i: (0, start + i))
    return call(
        own_kernel,
        jax.ShapeDtypeStruct((rows, width), F32),
        [spec, spec, cut, cut],
        pl.BlockSpec((rows, tile), lambda i: (0, i)),
        flops=6 * rows * rows * width,
        nbytes=12 * rows * width + 4 * rows * rows,
        grid=(width // tile,),
    )(*adj, feats, first)


def product_kernel(beta_ref, high_ref, low_ref, base_ref, weight_ref, *refs, near, relu):
    came, out_ref, mixed, total = refs[:near], refs[near], refs[near + 1], refs[near + 2]
    step, last = pl.program_id(0), pl.num_programs(0) - 1
    tile = weight_ref.shape[0]
    part = base_ref[...]
    if near:
        received = jnp.concatenate([r[...] for r in came], axis=0)
        part = part + dot3((high_ref[...], low_ref[...]), halves(received))
    mixed[:, pl.ds(pl.multiple_of(step * tile, tile), tile)] = part
    term = dot3(halves(part), halves(weight_ref[...]))

    @pl.when(step == 0)
    def _():
        total[...] = term

    @pl.when(step > 0)
    def _():
        total[...] += term

    @pl.when(step == last)
    def _():
        beta = beta_ref[0]
        value = (1.0 - beta) * mixed[...] + beta * total[...]
        out_ref[...] = jnp.maximum(value, 0.0) if relu else value


def product(beta, adj, base, weight, received, column, relu, tile=256):
    rows, depth = base.shape
    width = weight.shape[1]
    near = len(received)
    span = max(near, 1) * BLK
    at = column // span
    assert at * span == column
    spec = pl.BlockSpec((rows, span), lambda i: (0, at))
    return call(
        functools.partial(product_kernel, near=near, relu=relu),
        jax.ShapeDtypeStruct((rows, width), F32),
        [SMEM, spec, spec, pl.BlockSpec((rows, tile), lambda i: (0, i)), pl.BlockSpec((tile, width), lambda i: (i, 0))]
        + [pl.BlockSpec((BLK, tile), lambda i: (0, i))] * near,
        pl.BlockSpec((rows, width), lambda i: (0, 0)),
        flops=6 * rows * depth * width,
        nbytes=4 * (depth * width + 2 * rows * width),
        scratch=[pltpu.VMEM((rows, depth), F32), pltpu.VMEM((rows, width), F32)],
        grid=(depth // tile,),
        vmem=40,
    )(beta, *adj, base, weight, *received)


def add_kernel(high_ref, low_ref, base_ref, *refs):
    came, out_ref = refs[:-1], refs[-1]
    received = jnp.concatenate([r[...] for r in came], axis=0)
    out_ref[...] = base_ref[...] + dot3((high_ref[...], low_ref[...]), halves(received))


def add_received(adj, base, received, column, tile=256):
    rows, width = base.shape
    span = len(received) * BLK
    at = column // span
    spec = pl.BlockSpec((rows, span), lambda i: (0, at))
    return call(
        add_kernel,
        jax.ShapeDtypeStruct((rows, width), F32),
        [spec, spec, pl.BlockSpec((rows, tile), lambda i: (0, i))]
        + [pl.BlockSpec((BLK, tile), lambda i: (0, i))] * len(received),
        pl.BlockSpec((rows, tile), lambda i: (0, i)),
        flops=6 * rows * span * width,
        nbytes=8 * rows * width,
        grid=(width // tile,),
    )(*adj, base, *received)


def shards(state, initial, fresh, weights, wants, adj_slot, adj_count, adj_vals):
    section = lax.axis_index("segment")
    part = lax.axis_index("graph")
    beta = jnp.log(0.5 / (section.astype(F32) + 1.0) + 1.0).reshape(1)
    last = section == lax.axis_size("segment") - 1
    feats, first, weight = state[0], initial[0], weights[0]
    rows, depth = feats.shape
    half = depth // 2
    asks = wants.reshape(wants.shape[1])

    place = []
    for position in range(2 * REACH):
        stride = position // 2 + 1
        low = (part // stride) % 2 == 0
        phase = jnp.where(low, 1 - position % 2, position % 2)
        place.append(jnp.where(phase == 0, SWAPS.index((stride, 0)), SWAPS.index((stride, 1))))
    place = jnp.stack(place).astype(jnp.int32)
    index = []
    for stride, phase in SWAPS:
        low = (part // stride) % 2 == phase
        index.append(jnp.where(low, 2 * stride - 2, 2 * stride - 1))
    index = jnp.stack(index).astype(jnp.int32)

    got = [swap(asks, *kind) for kind in SWAPS]
    adj = dense(place, adj_slot, adj_count, adj_vals)

    sent = [pick(index[i : i + 1], got[i : i + 1], feats)[0] for i in range(len(SWAPS))]
    came = [swap(value, *kind) for value, kind in zip(sent, SWAPS)]
    next_first = jnp.where(last, fresh, first)
    first_left = hand_on(next_first[:, :half])
    mixed = own_part(adj, feats, first)
    first_out = product(beta, adj, mixed, weight, came, rows, True)

    next_feats = jnp.where(last, fresh, first_out)
    left = hand_on(next_feats[:, :half])
    right = next_feats[:, half:]
    came_right = [swap(value, *kind) for value, kind in zip(pick(index, got, right), SWAPS)]
    mixed_right = own_part(adj, right, next_first[:, half:])
    mixed_right = hand_on(add_received(adj, mixed_right, came_right, rows))
    came_left = [swap(value, *kind) for value, kind in zip(pick(index, got, left), SWAPS)]
    mixed_left = own_part(adj, left, first_left)
    mixed_left = add_received(adj, mixed_left, came_left, rows)
    base = jnp.concatenate([mixed_left, mixed_right], axis=1)
    second_out = product(beta, adj, base, weight, [], rows, True)
    return first_out[None], second_out[None]


def solution(mesh):
    return jax.shard_map(
        shards,
        mesh=mesh,
        in_specs=(
            P("segment", "graph", None),
            P("segment", "graph", None),
            P("graph", None),
            P("segment", None, None),
            P("graph", None, None),
            P("graph", None),
            P("graph"),
            P("graph", None, None, None),
        ),
        out_specs=(P("segment", "graph", None), P("segment", "graph", None)),
        check_vma=False,
    )
```

time: 157 us -> 103 us (0.66)
  the two profiles are of different devices: /device:TPU:2 before, /device:TPU:16 now
where the time goes in v1:
time: 103 us
  Pallas kernels  36.4 us (35%)
  starting transfers between devices  33.7 us (33%)
  waiting for transfers between devices  25.4 us (25%)
  local copies, waits for them, and re-layouts  3.58 us (3%)
  other arithmetic  2.62 us (3%)
  between operations  1.06 us (1%)
    ppermute x16, starting transfers between devices, swap(): return lax.ppermute(value, 'graph', sorted(pairs))  32 us
    ppermute x16, waiting for transfers between devices, swap(): return lax.ppermute(value, 'graph', sorted(pairs))  25.4 us
    pallas_call x2, Pallas kernels, product(): call(functools.partial(product_kernel, near=near, relu=relu), jax.ShapeDt...  19.1 us
    pallas_call x6, Pallas kernels, pick(): call(functools.partial(pick_kernel, count=count), (shape,) * count, [SMEM...  6.79 us
    pallas_call x3, Pallas kernels, own_part(): call(own_kernel, jax.ShapeDtypeStruct((rows, width), F32), [spec, spec, c...  5.96 us
    unnamed x18, local copies, waits for them, and re-layouts  3.22 us
    pallas_call x2, Pallas kernels, add_received(): call(add_kernel, jax.ShapeDtypeStruct((rows, width), F32), [spec, spec, p...  3 us
    select_n x1, other arithmetic, shards(): next_first = jnp.where(last, fresh, first)  2.28 us
  transfers between devices with their start and end apart: 19, of which 10 were waited for; matrix products, arithmetic and copies ran while one was open for 0% of the time, Pallas kernels for 16%

profile of v1, /device:TPU:16, one launch (start us, length us, event | category | flops | bytes accessed | tf_op | source)
XLA Modules:
  0.0 102.7 jit_solution(5989058135941600761)
XLA Ops:
  0.6 3.3 %collective-permute-start.6 = (s32[4]{0:T(128)}, s32[4]{0:T(128)S(1)}, u32[]{:S(2)}, u32[]{:S(2)}) collective-permute-start(s32[4]{0:T(128)} %bitcast.25), channel_id=1, source_target_pairs={{1,2},{2,1},{3,4},{4,3},{5,6},{6,5},{9,10},{10,9},{11,12},{12,11},... | collective-permute-start | bytes 56 | tf_op jit(solution)/shard_map/ppermute | solution.py:27
  4.0 2.4 %collective-permute-start.4 = (s32[4]{0:T(128)}, s32[4]{0:T(128)S(1)}, u32[]{:S(2)}, u32[]{:S(2)}) collective-permute-start(s32[4]{0:T(128)} %bitcast.26), channel_id=1, source_target_pairs={{2,4},{3,5},{4,2},{5,3},{10,12},{11,13},{12,10},{13,11},{18,20},{1... | collective-permute-start | bytes 56 | tf_op jit(solution)/shard_map/ppermute | solution.py:27
  6.4 1.7 %collective-permute-start = (s32[4]{0:T(128)}, s32[4]{0:T(128)S(1)}, u32[]{:S(2)}, u32[]{:S(2)}) collective-permute-start(s32[4]{0:T(128)} %bitcast.28), channel_id=1, source_target_pairs={{0,1},{1,0},{2,3},{3,2},{4,5},{5,4},{6,7},{7,6},{8,9},{9,8},{10,11... | collective-permute-start | bytes 56 | tf_op jit(solution)/shard_map/ppermute | solution.py:27
  8.1 1.6 %copy-done = f32[1,512,1024]{2,1,0:T(8,128)S(1)} copy-done((f32[1,512,1024]{2,1,0:T(8,128)S(1)}, f32[1,512,1024]{2,1,0:T(8,128)}, u32[]{:S(2)}) %copy-start) | copy-done | bytes 2097176
  9.7 1.4 %shard_map.100 = f32[128,1024]{1,0:T(8,128)} custom-call(s32[1]{0:T(128)} %bitcast.12.index_ref, s32[4]{0:T(128)S(1)} %collective-permute-done.6.refs_0_.refs_3_, f32[512,1024]{1,0:T(8,128)S(1)} %bitcast.16), custom_call_target="tpu_custom_call" | custom-call | bytes 1048576 | tf_op jit(solution)/shard_map/pallas_call | solution.py:104
  11.1 3.3 %collective-permute-start.7 = (f32[128,1024]{1,0:T(8,128)}, f32[128,1024]{1,0:T(8,128)}, u32[]{:S(2)}, u32[]{:S(2)}) collective-permute-start(f32[128,1024]{1,0:T(8,128)} %shard_map.100), channel_id=1, source_target_pairs={{1,2},{2,1},{3,4},{4,3},{5,6},{6,5},{9,10},{10,9},{11,12},{12,11},... | collective-permute-start | bytes 1572872 | tf_op jit(solution)/shard_map/ppermute | solution.py:27
  14.4 1.3 %shard_map.99 = f32[128,1024]{1,0:T(8,128)} custom-call(s32[1]{0:T(128)} %bitcast.11.index_ref, s32[4]{0:T(128)S(1)} %collective-permute-done.4.refs_0_.refs_2_, f32[512,1024]{1,0:T(8,128)S(1)} %bitcast.17), custom_call_target="tpu_custom_call" | custom-call | bytes 1048576 | tf_op jit(solution)/shard_map/pallas_call | solution.py:104
  15.7 3.9 %collective-permute-start.5 = (f32[128,1024]{1,0:T(8,128)}, f32[128,1024]{1,0:T(8,128)}, u32[]{:S(2)}, u32[]{:S(2)}) collective-permute-start(f32[128,1024]{1,0:T(8,128)} %shard_map.99), channel_id=1, source_target_pairs={{2,4},{3,5},{4,2},{5,3},{10,12},{11,13},{12,10},{13,11},{18,20},{1... | collective-permute-start | bytes 1572872 | tf_op jit(solution)/shard_map/ppermute | solution.py:27
  19.6 1.3 %shard_map.98 = f32[128,1024]{1,0:T(8,128)} custom-call(s32[1]{0:T(128)} %bitcast.10.index_ref, s32[4]{0:T(128)S(1)} %collective-permute-done.2.refs_0_.refs_1_, f32[512,1024]{1,0:T(8,128)S(1)} %bitcast.18), custom_call_target="tpu_custom_call" | custom-call | bytes 1048576 | tf_op jit(solution)/shard_map/pallas_call | solution.py:104
  21.1 1.3 %shard_map.97 = f32[128,1024]{1,0:T(8,128)} custom-call(s32[1]{0:T(128)} %bitcast.8.index_ref, s32[4]{0:T(128)S(1)} %collective-permute-done.refs_0_, f32[512,1024]{1,0:T(8,128)S(1)} %bitcast.19), custom_call_target="tpu_custom_call" | custom-call | bytes 1048576 | tf_op jit(solution)/shard_map/pallas_call | solution.py:104
  22.8 1.5 %shard_map.95 = (bf16[512,1024]{1,0:T(8,128)(2,1)S(1)}, bf16[512,1024]{1,0:T(8,128)(2,1)S(1)}) custom-call(s32[4]{0:T(128)S(1)} %pad_add_fusion.place_ref, s32[4,4]{1,0:T(4,128)S(1)} %copy-done.6, s32[4]{0:T(128)S(1)} %copy-done.7, f32[4,4,128,128]{3,2,1,0:T(8,128)S(1)} %copy-done.5), custom_call_target="tpu_custom_call" | custom-call | bytes 3145728 | tf_op jit(solution)/shard_map/pallas_call | solution.py:79
  24.4 1.6 %copy-done.2 = f32[1,512,1024]{2,1,0:T(8,128)S(1)} copy-done((f32[1,512,1024]{2,1,0:T(8,128)S(1)}, f32[1,512,1024]{2,1,0:T(8,128)}, u32[]{:S(2)}) %copy-start.2) | copy-done | bytes 2097176
  26.0 2.9 %shard_map.96.base_ref = f32[512,1024]{1,0:T(8,128)S(1)} custom-call(bf16[512,1024]{1,0:T(8,128)(2,1)S(1)} %get-tuple-element.12.high_ref, bf16[512,1024]{1,0:T(8,128)(2,1)S(1)} %get-tuple-element.13.low_ref, f32[512,1024]{1,0:T(8,128)S(1)} %bitcast.20, f32[512,1024]{1,0:T(8,128)S(1)} %bitcast.21), custom_call_target="tpu_custom_call" | custom-call | flops 1610612736 | bytes 7340032 | tf_op jit(solution)/shard_map/pallas_call | solution.py:125
  29.0 7.2 %collective-permute-done.5.refs_2_ = f32[128,1024]{1,0:T(8,128)} collective-permute-done((f32[128,1024]{1,0:T(8,128)}, f32[128,1024]{1,0:T(8,128)}, u32[]{:S(2)}, u32[]{:S(2)}) %collective-permute-start.5) | collective-permute-done | bytes 524320 | tf_op jit(solution)/shard_map/ppermute | solution.py:27
  36.2 1.0 collective-permute-done.3.refs_1_
  38.2 12.5 %shard_map.101 = f32[512,1024]{1,0:T(8,128)} custom-call(f32[1]{0:T(128)} %bitcast.beta_ref, bf16[512,1024]{1,0:T(8,128)(2,1)S(1)} %get-tuple-element.12.high_ref, bf16[512,1024]{1,0:T(8,128)(2,1)S(1)} %get-tuple-element.13.low_ref, f32[512,1024]{1,0:T(8,128)S(1)} %shard_map.96.base_ref, f32[1024,1024]{1,0:T(8,128)S(1)} %bitcast.22, ...), custom_call_target="tpu_custom_call" | custom-call | flops 3221225472 | bytes 8388608 | tf_op jit(solution)/shard_map/pallas_call | solution.py:170
  50.8 2.3 %broadcast_select_fusion = (f32[512,1024]{1,0:T(8,128)S(1)}, f32[512,1024]{1,0:T(8,128)S(1)}) fusion(f32[512,1024]{1,0:T(8,128)S(1)} %copy-done.8, pred[]{:T(512)S(6)} %eq.48, f32[1,512,1024]{2,1,0:T(8,128)S(1)} %copy-done.3, f32[512,1024]{1,0:T(8,128)} %shard_map.101), kind=kLoop, calls=%fused_computation.1 | loop fusion | flops 1048576 | bytes 10485761 | tf_op jit(solution)/shard_map/jit(_where)/select_n | solution.py:235
  54.8 1.7 %collective-permute-start.9 = (f32[512,512]{1,0:T(8,128)S(1)}, f32[512,512]{1,0:T(8,128)S(1)}, u32[]{:S(2)}, u32[]{:S(2)}) collective-permute-start(f32[512,512]{1,0:T(8,128)S(1)} %get-tuple-element.22), channel_id=1, source_target_pairs={{0,8},{8,16},{16,24},{24,0},{1,9},{9,17},{17,25},{25,1},{2,10},{10... | collective-permute-start | bytes 3145736 | tf_op jit(solution)/shard_map/ppermute | solution.py:32
  56.5 1.7 %collective-permute-start.15 = (f32[128,512]{1,0:T(8,128)S(1)}, f32[128,512]{1,0:T(8,128)S(1)}, u32[]{:S(2)}, u32[]{:S(2)}) collective-permute-start(f32[128,512]{1,0:T(8,128)S(1)} %get-tuple-element.19), channel_id=1, source_target_pairs={{0,2},{1,3},{2,0},{3,1},{4,6},{5,7},{6,4},{7,5},{8,10},{9,11},{10,... | collective-permute-start | bytes 786440 | tf_op jit(solution)/shard_map/ppermute | solution.py:27
  58.1 3.3 %collective-permute-start.16 = (f32[128,512]{1,0:T(8,128)S(1)}, f32[128,512]{1,0:T(8,128)S(1)}, u32[]{:S(2)}, u32[]{:S(2)}) collective-permute-start(f32[128,512]{1,0:T(8,128)S(1)} %get-tuple-element.20), channel_id=1, source_target_pairs={{2,4},{3,5},{4,2},{5,3},{10,12},{11,13},{12,10},{13,11},{18,20},{1... | collective-permute-start | bytes 786440 | tf_op jit(solution)/shard_map/ppermute | solution.py:27
  61.5 3.9 %collective-permute-start.17 = (f32[128,512]{1,0:T(8,128)S(1)}, f32[128,512]{1,0:T(8,128)S(1)}, u32[]{:S(2)}, u32[]{:S(2)}) collective-permute-start(f32[128,512]{1,0:T(8,128)S(1)} %get-tuple-element.21), channel_id=1, source_target_pairs={{1,2},{2,1},{3,4},{4,3},{5,6},{6,5},{9,10},{10,9},{11,12},{12,11},... | collective-permute-start | bytes 786440 | tf_op jit(solution)/shard_map/ppermute | solution.py:27
  65.4 1.5 %shard_map.105.base_ref = f32[512,512]{1,0:T(8,128)S(1)} custom-call(bf16[512,1024]{1,0:T(8,128)(2,1)S(1)} %get-tuple-element.12.high_ref, bf16[512,1024]{1,0:T(8,128)(2,1)S(1)} %get-tuple-element.13.low_ref, f32[512,512]{1,0:T(8,128)S(1)} %get-tuple-element.25.feats_ref.refs_4_, f32[512,512]{1,0:T(8,128)S(1)} %get-tuple-element.23.first_ref), custom_call_target="tpu_custom_call" | custom-call | flops 805306368 | bytes 4194304 | tf_op jit(solution)/shard_map/pallas_call | solution.py:125
  67.0 1.1 %collective-permute-done.16.refs_2_ = f32[128,512]{1,0:T(8,128)S(1)} collective-permute-done((f32[128,512]{1,0:T(8,128)S(1)}, f32[128,512]{1,0:T(8,128)S(1)}, u32[]{:S(2)}, u32[]{:S(2)}) %collective-permute-start.16) | collective-permute-done | bytes 262176 | tf_op jit(solution)/shard_map/ppermute | solution.py:27
  68.1 6.4 %collective-permute-done.17.refs_3_ = f32[128,512]{1,0:T(8,128)S(1)} collective-permute-done((f32[128,512]{1,0:T(8,128)S(1)}, f32[128,512]{1,0:T(8,128)S(1)}, u32[]{:S(2)}, u32[]{:S(2)}) %collective-permute-start.17) | collective-permute-done | bytes 262176 | tf_op jit(solution)/shard_map/ppermute | solution.py:27
  74.5 1.5 %shard_map.107 = f32[512,512]{1,0:T(8,128)S(1)} custom-call(bf16[512,1024]{1,0:T(8,128)(2,1)S(1)} %get-tuple-element.12.high_ref, bf16[512,1024]{1,0:T(8,128)(2,1)S(1)} %get-tuple-element.13.low_ref, f32[512,512]{1,0:T(8,128)S(1)} %shard_map.105.base_ref, f32[128,512]{1,0:T(8,128)S(1)} %collective-permute-done.14.refs_0_, ...), custom_call_target="tpu_custom_call" | custom-call | flops 805306368 | bytes 2097152 | tf_op jit(solution)/shard_map/pallas_call | solution.py:195
  76.9 3.8 %collective-permute-start.12 = (f32[128,512]{1,0:T(8,128)S(1)}, f32[128,512]{1,0:T(8,128)S(1)}, u32[]{:S(2)}, u32[]{:S(2)}) collective-permute-start(f32[128,512]{1,0:T(8,128)S(1)} %get-tuple-element.16), channel_id=1, source_target_pairs={{2,4},{3,5},{4,2},{5,3},{10,12},{11,13},{12,10},{13,11},{18,20},{1... | collective-permute-start | bytes 786440 | tf_op jit(solution)/shard_map/ppermute | solution.py:27
  80.7 3.7 %collective-permute-start.13 = (f32[128,512]{1,0:T(8,128)S(1)}, f32[128,512]{1,0:T(8,128)S(1)}, u32[]{:S(2)}, u32[]{:S(2)}) collective-permute-start(f32[128,512]{1,0:T(8,128)S(1)} %get-tuple-element.17), channel_id=1, source_target_pairs={{1,2},{2,1},{3,4},{4,3},{5,6},{6,5},{9,10},{10,9},{11,12},{12,11},... | collective-permute-start | bytes 786440 | tf_op jit(solution)/shard_map/ppermute | solution.py:27
  84.4 1.5 %shard_map.102.base_ref = f32[512,512]{1,0:T(8,128)S(1)} custom-call(bf16[512,1024]{1,0:T(8,128)(2,1)S(1)} %get-tuple-element.12.high_ref, bf16[512,1024]{1,0:T(8,128)(2,1)S(1)} %get-tuple-element.13.low_ref, f32[512,512]{1,0:T(8,128)S(1)} %collective-permute-done.8.feats_ref.refs_4_, f32[512,512]{1,0:T(8,128)S(1)} %collective-permute-done.9.first_ref), custom_call_target="tpu_custom_call" | custom-call | flops 805306368 | bytes 4194304 | tf_op jit(solution)/shard_map/pallas_call | solution.py:125
  86.1 1.6 %collective-permute-done.12.refs_2_ = f32[128,512]{1,0:T(8,128)S(1)} collective-permute-done((f32[128,512]{1,0:T(8,128)S(1)}, f32[128,512]{1,0:T(8,128)S(1)}, u32[]{:S(2)}, u32[]{:S(2)}) %collective-permute-start.12) | collective-permute-done | bytes 262176 | tf_op jit(solution)/shard_map/ppermute | solution.py:27
  87.7 6.7 %collective-permute-done.13.refs_3_ = f32[128,512]{1,0:T(8,128)S(1)} collective-permute-done((f32[128,512]{1,0:T(8,128)S(1)}, f32[128,512]{1,0:T(8,128)S(1)}, u32[]{:S(2)}, u32[]{:S(2)}) %collective-permute-start.13) | collective-permute-done | bytes 262176 | tf_op jit(solution)/shard_map/ppermute | solution.py:27
  94.4 1.5 %shard_map.104 = f32[512,512]{1,0:T(8,128)S(1)} custom-call(bf16[512,1024]{1,0:T(8,128)(2,1)S(1)} %get-tuple-element.12.high_ref, bf16[512,1024]{1,0:T(8,128)(2,1)S(1)} %get-tuple-element.13.low_ref, f32[512,512]{1,0:T(8,128)S(1)} %shard_map.102.base_ref, f32[128,512]{1,0:T(8,128)S(1)} %collective-permute-done.10.refs_0_, ...), custom_call_target="tpu_custom_call" | custom-call | flops 805306368 | bytes 2097152 | tf_op jit(solution)/shard_map/pallas_call | solution.py:195
  96.1 6.6 %shard_map.108 = f32[512,1024]{1,0:T(8,128)} custom-call(f32[1]{0:T(128)} %bitcast.beta_ref, bf16[512,1024]{1,0:T(8,128)(2,1)S(1)} %get-tuple-element.12.high_ref, bf16[512,1024]{1,0:T(8,128)(2,1)S(1)} %get-tuple-element.13.low_ref, f32[512,1024]{1,0:T(8,128)S(1)} %pad_maximum_fusion.base_ref, f32[1024,1024]{1,0:T(8,128)S(1)} %bitcast.23), custom_call_target="tpu_custom_call" | custom-call | flops 3221225472 | bytes 8388608 | tf_op jit(solution)/shard_map/pallas_call | solution.py:170
  (44 shorter events, 4.7 us)
Async XLA Ops:
  0.6 7.5 %collective-permute-start.6 = (s32[4]{0:T(128)}, s32[4]{0:T(128)S(1)}, u32[]{:S(2)}, u32[]{:S(2)}) collective-permute-start(s32[4]{0:T(128)} %bitcast.25), channel_id=1, source_target_pairs={{1,2},{2,1},{3,4},{4,3},{5,6},{6,5},{9,10},{10,9},{11,12},{12,11},... | collective-permute-start | bytes 56 | tf_op jit(solution)/shard_map/ppermute | solution.py:27
  4.0 10.4 %collective-permute-start.4 = (s32[4]{0:T(128)}, s32[4]{0:T(128)S(1)}, u32[]{:S(2)}, u32[]{:S(2)}) collective-permute-start(s32[4]{0:T(128)} %bitcast.26), channel_id=1, source_target_pairs={{2,4},{3,5},{4,2},{5,3},{10,12},{11,13},{12,10},{13,11},{18,20},{1... | collective-permute-start | bytes 56 | tf_op jit(solution)/shard_map/ppermute | solution.py:27
  6.3 13.3 %collective-permute-start.2 = (s32[4]{0:T(128)}, s32[4]{0:T(128)S(1)}, u32[]{:S(2)}, u32[]{:S(2)}) collective-permute-start(s32[4]{0:T(128)} %bitcast.27), channel_id=1, source_target_pairs={{0,2},{1,3},{2,0},{3,1},{4,6},{5,7},{6,4},{7,5},{8,10},{9,11},{10,... | collective-permute-start | bytes 56 | tf_op jit(solution)/shard_map/ppermute | solution.py:27
  6.4 14.7 %collective-permute-start = (s32[4]{0:T(128)}, s32[4]{0:T(128)S(1)}, u32[]{:S(2)}, u32[]{:S(2)}) collective-permute-start(s32[4]{0:T(128)} %bitcast.28), channel_id=1, source_target_pairs={{0,1},{1,0},{2,3},{3,2},{4,5},{5,4},{6,7},{7,6},{8,9},{9,8},{10,11... | collective-permute-start | bytes 56 | tf_op jit(solution)/shard_map/ppermute | solution.py:27
  8.1 1.6 %copy-start = (f32[1,512,1024]{2,1,0:T(8,128)S(1)}, f32[1,512,1024]{2,1,0:T(8,128)}, u32[]{:S(2)}) copy-start(f32[1,512,1024]{2,1,0:T(8,128)} %param.8) | copy-start | bytes 6291460
  11.1 18.0 %collective-permute-start.7 = (f32[128,1024]{1,0:T(8,128)}, f32[128,1024]{1,0:T(8,128)}, u32[]{:S(2)}, u32[]{:S(2)}) collective-permute-start(f32[128,1024]{1,0:T(8,128)} %shard_map.100), channel_id=1, source_target_pairs={{1,2},{2,1},{3,4},{4,3},{5,6},{6,5},{9,10},{10,9},{11,12},{12,11},... | collective-permute-start | bytes 1572872 | tf_op jit(solution)/shard_map/ppermute | solution.py:27
  15.7 20.5 %collective-permute-start.5 = (f32[128,1024]{1,0:T(8,128)}, f32[128,1024]{1,0:T(8,128)}, u32[]{:S(2)}, u32[]{:S(2)}) collective-permute-start(f32[128,1024]{1,0:T(8,128)} %shard_map.99), channel_id=1, source_target_pairs={{2,4},{3,5},{4,2},{5,3},{10,12},{11,13},{12,10},{13,11},{18,20},{1... | collective-permute-start | bytes 1572872 | tf_op jit(solution)/shard_map/ppermute | solution.py:27
  19.6 3.2 %copy-start.5 = (f32[4,4,128,128]{3,2,1,0:T(8,128)S(1)}, f32[4,4,128,128]{3,2,1,0:T(8,128)}, u32[]{:S(2)}) copy-start(f32[4,4,128,128]{3,2,1,0:T(8,128)} %vals_ref.1) | copy-start | bytes 3145732
  19.6 3.2 %copy-start.6 = (s32[4,4]{1,0:T(4,128)S(1)}, s32[4,4]{1,0:T(4,128)}, u32[]{:S(2)}) copy-start(s32[4,4]{1,0:T(4,128)} %slot_ref.1) | copy-start | bytes 196
  19.6 3.2 %copy-start.7 = (s32[4]{0:T(128)S(1)}, s32[4]{0:T(128)}, u32[]{:S(2)}) copy-start(s32[4]{0:T(128)} %count_ref.1) | copy-start | bytes 52
  21.0 3.4 %copy-start.1 = (f32[1,512,1024]{2,1,0:T(8,128)S(1)}, f32[1,512,1024]{2,1,0:T(8,128)}, u32[]{:S(2)}) copy-start(f32[1,512,1024]{2,1,0:T(8,128)} %param.8) | copy-start | bytes 6291460
  21.0 16.2 %collective-permute-start.3 = (f32[128,1024]{1,0:T(8,128)}, f32[128,1024]{1,0:T(8,128)}, u32[]{:S(2)}, u32[]{:S(2)}) collective-permute-start(f32[128,1024]{1,0:T(8,128)} %shard_map.98), channel_id=1, source_target_pairs={{0,2},{1,3},{2,0},{3,1},{4,6},{5,7},{6,4},{7,5},{8,10},{9,11},{10,... | collective-permute-start | bytes 1572872 | tf_op jit(solution)/shard_map/ppermute | solution.py:27
  22.5 15.8 %collective-permute-start.1 = (f32[128,1024]{1,0:T(8,128)}, f32[128,1024]{1,0:T(8,128)}, u32[]{:S(2)}, u32[]{:S(2)}) collective-permute-start(f32[128,1024]{1,0:T(8,128)} %shard_map.97), channel_id=1, source_target_pairs={{0,1},{1,0},{2,3},{3,2},{4,5},{5,4},{6,7},{7,6},{8,9},{9,8},{10,11... | collective-permute-start | bytes 1572872 | tf_op jit(solution)/shard_map/ppermute | solution.py:27
  24.4 1.6 %copy-start.2 = (f32[1,512,1024]{2,1,0:T(8,128)S(1)}, f32[1,512,1024]{2,1,0:T(8,128)}, u32[]{:S(2)}) copy-start(f32[1,512,1024]{2,1,0:T(8,128)} %param.9) | copy-start | bytes 6291460
  26.0 12.2 %copy-start.4 = (f32[1,1024,1024]{2,1,0:T(8,128)S(1)}, f32[1,1024,1024]{2,1,0:T(8,128)}, u32[]{:S(2)}) copy-start(f32[1,1024,1024]{2,1,0:T(8,128)} %param.11) | copy-start | bytes 12582916
  38.2 12.5 %copy-start.3 = (f32[1,512,1024]{2,1,0:T(8,128)S(1)}, f32[1,512,1024]{2,1,0:T(8,128)}, u32[]{:S(2)}) copy-start(f32[1,512,1024]{2,1,0:T(8,128)} %param.9) | copy-start | bytes 6291460
  38.2 12.5 %copy-start.8 = (f32[512,1024]{1,0:T(8,128)S(1)}, f32[512,1024]{1,0:T(8,128)}, u32[]{:S(2)}) copy-start(f32[512,1024]{1,0:T(8,128)} %param.10) | copy-start | bytes 6291460
  53.9 7.6 %collective-permute-start.14 = (f32[128,512]{1,0:T(8,128)S(1)}, f32[128,512]{1,0:T(8,128)S(1)}, u32[]{:S(2)}, u32[]{:S(2)}) collective-permute-start(f32[128,512]{1,0:T(8,128)S(1)} %get-tuple-element.18), channel_id=1, source_target_pairs={{0,1},{1,0},{2,3},{3,2},{4,5},{5,4},{6,7},{7,6},{8,9},{9,8},{10,11... | collective-permute-start | bytes 786440 | tf_op jit(solution)/shard_map/ppermute | solution.py:27
  54.6 21.5 %collective-permute-start.8 = (f32[512,512]{1,0:T(8,128)S(1)}, f32[512,512]{1,0:T(8,128)S(1)}, u32[]{:S(2)}, u32[]{:S(2)}) collective-permute-start(f32[512,512]{1,0:T(8,128)S(1)} %get-tuple-element.24), channel_id=1, source_target_pairs={{0,8},{8,16},{16,24},{24,0},{1,9},{9,17},{17,25},{25,1},{2,10},{10... | collective-permute-start | bytes 3145736 | tf_op jit(solution)/shard_map/ppermute | solution.py:32
  54.8 25.9 %collective-permute-start.9 = (f32[512,512]{1,0:T(8,128)S(1)}, f32[512,512]{1,0:T(8,128)S(1)}, u32[]{:S(2)}, u32[]{:S(2)}) collective-permute-start(f32[512,512]{1,0:T(8,128)S(1)} %get-tuple-element.22), channel_id=1, source_target_pairs={{0,8},{8,16},{16,24},{24,0},{1,9},{9,17},{17,25},{25,1},{2,10},{10... | collective-permute-start | bytes 3145736 | tf_op jit(solution)/shard_map/ppermute | solution.py:32
  56.5 10.5 %collective-permute-start.15 = (f32[128,512]{1,0:T(8,128)S(1)}, f32[128,512]{1,0:T(8,128)S(1)}, u32[]{:S(2)}, u32[]{:S(2)}) collective-permute-start(f32[128,512]{1,0:T(8,128)S(1)} %get-tuple-element.19), channel_id=1, source_target_pairs={{0,2},{1,3},{2,0},{3,1},{4,6},{5,7},{6,4},{7,5},{8,10},{9,11},{10,... | collective-permute-start | bytes 786440 | tf_op jit(solution)/shard_map/ppermute | solution.py:27
  58.1 10.0 %collective-permute-start.16 = (f32[128,512]{1,0:T(8,128)S(1)}, f32[128,512]{1,0:T(8,128)S(1)}, u32[]{:S(2)}, u32[]{:S(2)}) collective-permute-start(f32[128,512]{1,0:T(8,128)S(1)} %get-tuple-element.20), channel_id=1, source_target_pairs={{2,4},{3,5},{4,2},{5,3},{10,12},{11,13},{12,10},{13,11},{18,20},{1... | collective-permute-start | bytes 786440 | tf_op jit(solution)/shard_map/ppermute | solution.py:27
  61.5 13.0 %collective-permute-start.17 = (f32[128,512]{1,0:T(8,128)S(1)}, f32[128,512]{1,0:T(8,128)S(1)}, u32[]{:S(2)}, u32[]{:S(2)}) collective-permute-start(f32[128,512]{1,0:T(8,128)S(1)} %get-tuple-element.21), channel_id=1, source_target_pairs={{1,2},{2,1},{3,4},{4,3},{5,6},{6,5},{9,10},{10,9},{11,12},{12,11},... | collective-permute-start | bytes 786440 | tf_op jit(solution)/shard_map/ppermute | solution.py:27
  76.0 19.9 %collective-permute-start.18 = (f32[512,512]{1,0:T(8,128)S(1)}, f32[512,512]{1,0:T(8,128)S(1)}, u32[]{:S(2)}, u32[]{:S(2)}) collective-permute-start(f32[512,512]{1,0:T(8,128)S(1)} %shard_map.107), channel_id=1, source_target_pairs={{0,8},{8,16},{16,24},{24,0},{1,9},{9,17},{17,25},{25,1},{2,10},{10... | collective-permute-start | bytes 3145736 | tf_op jit(solution)/shard_map/ppermute | solution.py:32
  76.8 9.1 %collective-permute-start.10 = (f32[128,512]{1,0:T(8,128)S(1)}, f32[128,512]{1,0:T(8,128)S(1)}, u32[]{:S(2)}, u32[]{:S(2)}) collective-permute-start(f32[128,512]{1,0:T(8,128)S(1)} %get-tuple-element.14), channel_id=1, source_target_pairs={{0,1},{1,0},{2,3},{3,2},{4,5},{5,4},{6,7},{7,6},{8,9},{9,8},{10,11... | collective-permute-start | bytes 786440 | tf_op jit(solution)/shard_map/ppermute | solution.py:27
  76.9 9.2 %collective-permute-start.11 = (f32[128,512]{1,0:T(8,128)S(1)}, f32[128,512]{1,0:T(8,128)S(1)}, u32[]{:S(2)}, u32[]{:S(2)}) collective-permute-start(f32[128,512]{1,0:T(8,128)S(1)} %get-tuple-element.15), channel_id=1, source_target_pairs={{0,2},{1,3},{2,0},{3,1},{4,6},{5,7},{6,4},{7,5},{8,10},{9,11},{10,... | collective-permute-start | bytes 786440 | tf_op jit(solution)/shard_map/ppermute | solution.py:27
  76.9 10.7 %collective-permute-start.12 = (f32[128,512]{1,0:T(8,128)S(1)}, f32[128,512]{1,0:T(8,128)S(1)}, u32[]{:S(2)}, u32[]{:S(2)}) collective-permute-start(f32[128,512]{1,0:T(8,128)S(1)} %get-tuple-element.16), channel_id=1, source_target_pairs={{2,4},{3,5},{4,2},{5,3},{10,12},{11,13},{12,10},{13,11},{18,20},{1... | collective-permute-start | bytes 786440 | tf_op jit(solution)/shard_map/ppermute | solution.py:27
  80.7 13.6 %collective-permute-start.13 = (f32[128,512]{1,0:T(8,128)S(1)}, f32[128,512]{1,0:T(8,128)S(1)}, u32[]{:S(2)}, u32[]{:S(2)}) collective-permute-start(f32[128,512]{1,0:T(8,128)S(1)} %get-tuple-element.17), channel_id=1, source_target_pairs={{1,2},{2,1},{3,4},{4,3},{5,6},{6,5},{9,10},{10,9},{11,12},{12,11},... | collective-permute-start | bytes 786440 | tf_op jit(solution)/shard_map/ppermute | solution.py:27

commit v2 on v0

v2 whole, which is shorter than its diff:
```python
import functools

import jax
import jax.numpy as jnp
from jax import lax
from jax.experimental import pallas as pl
from jax.experimental.pallas import tpu as pltpu
from jax.sharding import PartitionSpec as P

BLK = 128
REACH = 2
F32 = jnp.float32
BF16 = jnp.bfloat16
SWAPS = ((1, 0), (2, 0), (2, 1), (1, 1))
VMEM = pl.BlockSpec(memory_space=pltpu.VMEM)
SMEM = pl.BlockSpec(memory_space=pltpu.SMEM)
HBM = pl.BlockSpec(memory_space=pltpu.HBM)
ONE = pltpu.SemaphoreType.DMA


def swap(value, stride, phase):
    peers = lax.axis_size("graph")
    pairs = []
    for low in range(peers - stride):
        if (low // stride) % 2 == phase:
            pairs += [(low, low + stride), (low + stride, low)]
    return lax.ppermute(value, "graph", sorted(pairs))


def hand_on(value):
    peers = lax.axis_size("segment")
    return lax.ppermute(value, "segment", [(i, (i + 1) % peers) for i in range(peers)])


def halves(value):
    high = value.astype(BF16)
    return high, (value - high.astype(F32)).astype(BF16)


def dot3(a, b):
    times = functools.partial(jnp.dot, preferred_element_type=F32)
    return times(a[0], b[0]) + (times(a[0], b[1]) + times(a[1], b[0]))


def call(kernel, args, in_specs, outs, flops=0, nbytes=0, scratch=(), after=(), vmem=16):
    count = len(args)

    def body(*refs):
        kernel(*refs[:count], *refs[count + len(after) :])

    return pl.pallas_call(
        body,
        out_shape=outs,
        in_specs=list(in_specs) + [VMEM] * len(after),
        out_specs=tuple(VMEM if isinstance(out, jax.ShapeDtypeStruct) else HBM for out in outs),
        scratch_shapes=list(scratch),
        cost_estimate=pl.CostEstimate(flops=flops, bytes_accessed=nbytes, transcendentals=0),
        compiler_params=pltpu.CompilerParams(vmem_limit_bytes=vmem * 2**20),
    )(*args, *after)


def vmem(*shape, dtype=F32):
    return jax.ShapeDtypeStruct(shape, dtype)


def prepare_kernel(place_ref, slot_ref, count_ref, index_ref, got_ref, *refs, kind):
    vals_ref, feats_ref, high_ref, low_ref, sent_ref, held, total, sem = refs
    copies = [pltpu.make_async_copy(vals_ref, held, sem.at[0])]
    row = pl.multiple_of(got_ref[index_ref[kind]] * BLK, BLK)
    copies.append(pltpu.make_async_copy(feats_ref.at[pl.ds(row, BLK)], sent_ref, sem.at[1]))
    for copy in copies:
        copy.start()
    total[...] = jnp.zeros_like(total)
    blocks, most = held.shape[:2]
    copies[0].wait()
    for b in range(blocks):
        for k in range(most):
            slot = slot_ref[b, k]
            past = jnp.maximum(slot - blocks, 0)
            column = jnp.where(slot < blocks, slot, blocks + place_ref[past])
            scale = jnp.where(k < count_ref[b], 0.9, 0.0).astype(F32)
            where = pl.ds(pl.multiple_of(column * BLK, BLK), BLK)
            total[b * BLK : (b + 1) * BLK, where] += scale * held[b, k]
    high, low = halves(total[...])
    high_ref[...] = high
    low_ref[...] = low
    copies[1].wait()


def in_hbm(value):
    return pltpu.with_memory_space_constraint(value, pltpu.HBM)


def prepare(kind, place, slots, counts, index, got, vals, feats, after=()):
    rows, width = feats.shape
    span = rows + 2 * REACH * BLK
    return call(
        functools.partial(prepare_kernel, kind=kind),
        (place, slots, counts, index, got[kind], in_hbm(vals), in_hbm(feats)),
        [SMEM] * 5 + [HBM] * 2,
        (vmem(rows, span, dtype=BF16),) * 2 + (vmem(BLK, width),),
        nbytes=4 * vals.size + 4 * rows * span,
        scratch=[pltpu.VMEM(vals.shape, F32), pltpu.VMEM((rows, span), F32), ONE((2,))],
        after=after,
    )


def pick_kernel(index_ref, *refs, kinds):
    count = len(kinds)
    got, source, outs, sem = refs[:count], refs[count], refs[count + 1 : -1], refs[-1]
    copies = []
    for i, kind in enumerate(kinds):
        row = pl.multiple_of(got[i][index_ref[kind]] * BLK, BLK)
        copies.append(pltpu.make_async_copy(source.at[pl.ds(row, BLK)], outs[i], sem.at[i]))
        copies[-1].start()
    for copy in copies:
        copy.wait()


def pick(kinds, index, got, source, after=()):
    return call(
        functools.partial(pick_kernel, kinds=kinds),
        (index, *[got[k] for k in kinds], in_hbm(source)),
        [SMEM] * (1 + len(kinds)) + [HBM],
        (vmem(BLK, source.shape[1]),) * len(kinds),
        nbytes=8 * BLK * source.shape[1] * len(kinds),
        scratch=[ONE((len(kinds),))],
        after=after,
    )


def wanted(kinds, index_ref, got, source_ref, outs):
    for kind, got_ref, out_ref in zip(kinds, got, outs):
        row = pl.multiple_of(got_ref[index_ref[kind]] * BLK, BLK)
        out_ref[...] = source_ref[pl.ds(row, BLK), :]


def choose_kernel(index_ref, *refs, kinds):
    count = len(kinds)
    wanted(kinds, index_ref, refs[:count], refs[count], refs[count + 1 :])


def choose(kinds, index, got, source, after=()):
    return call(
        functools.partial(choose_kernel, kinds=kinds),
        (index, *[got[k] for k in kinds], source),
        [SMEM] * (1 + len(kinds)) + [VMEM],
        (vmem(BLK, source.shape[1]),) * len(kinds),
        nbytes=8 * len(kinds) * BLK * source.shape[1],
        after=after,
    )


def times_adj(high_ref, low_ref, at, value):
    cut = slice(at, at + value.shape[0])
    return dot3((high_ref[:, cut], low_ref[:, cut]), halves(value))


def stacked(refs):
    return jnp.concatenate([ref[...] for ref in refs], axis=0)


def early_kernel(beta_ref, last_ref, high_ref, low_ref, weight_ref, *refs):
    came, sources, (out_ref, left_ref, right_ref), refs = refs[:-10], refs[-10:-7], refs[-7:-4], refs[-4:]
    held, sem = refs[:3], refs[3]
    feats_ref, first_ref, fresh_ref = held
    copies = [pltpu.make_async_copy(s, h, sem.at[i]) for i, (s, h) in enumerate(zip(sources, held))]
    for copy in copies:
        copy.start()
    rows, half = left_ref.shape
    mixed = times_adj(high_ref, low_ref, rows, stacked(came))
    copies[0].wait()
    mixed = mixed + times_adj(high_ref, low_ref, 0, feats_ref[...])
    copies[1].wait()
    mixed = mixed + 0.1 * first_ref[...]
    beta = beta_ref[0]
    out_ref[...] = (1.0 - beta) * mixed + beta * dot3(halves(mixed), halves(weight_ref[...]))
    copies[2].wait()
    last = last_ref[0] != 0
    left_ref[...] = jnp.where(last, fresh_ref[:, :half], first_ref[:, :half])
    right_ref[...] = jnp.where(last, fresh_ref[:, half:], first_ref[:, half:])


def early(beta, last, adj, weight, came, feats, first, fresh):
    rows, width = feats.shape
    arrays = (feats, first, fresh)
    return call(
        early_kernel,
        (beta, last, *adj, weight, *came, *[in_hbm(v) for v in arrays]),
        [SMEM] * 2 + [VMEM] * (3 + len(came)) + [HBM] * 3,
        (vmem(rows, width),) + (vmem(rows, width // 2),) * 2,
        flops=6 * rows * width * (width + rows + len(came) * BLK),
        nbytes=4 * (width * width + 5 * rows * width),
        scratch=[pltpu.VMEM(v.shape, F32) for v in arrays] + [ONE((len(arrays),))],
    )


def late_kernel(beta_ref, last_ref, index_ref, *refs, kinds):
    count = len(kinds)
    got, refs = refs[:count], refs[count:]
    (high_ref, low_ref, base_ref, weight_ref, first_left_ref, first_right_ref, came_ref), refs = refs[:7], refs[7:]
    out_left_ref, out_right_ref, left_ref, right_ref, sent = refs[0], refs[1], refs[2], refs[3], refs[4:]
    half = left_ref.shape[1]
    beta = beta_ref[0]
    last = last_ref[0] != 0
    came = came_ref[...]
    pair = halves(came)
    column = high_ref.shape[1] - BLK
    for at, out_ref, first_ref, next_ref in (
        (half, out_right_ref, first_right_ref, right_ref),
        (0, out_left_ref, first_left_ref, left_ref),
    ):
        cut = slice(at, at + half)
        through = (1.0 - beta) * came[:, cut] + beta * dot3(pair, halves(weight_ref[:, cut]))
        value = jnp.maximum(base_ref[:, cut] + times_adj(high_ref, low_ref, column, through), 0.0)
        out_ref[...] = value
        next_ref[...] = jnp.where(last, first_ref[...], value)
    wanted(kinds, index_ref, got, right_ref, sent)


def late(kinds, beta, last, index, got, adj, base, weight, firsts, came, after=()):
    rows, width = base.shape
    half = width // 2
    return call(
        functools.partial(late_kernel, kinds=kinds),
        (beta, last, index, *[got[k] for k in kinds], *adj, base, weight, *firsts, came),
        [SMEM] * (3 + len(kinds)) + [VMEM] * 7,
        (vmem(rows, half),) * 4 + (vmem(BLK, half),) * len(kinds),
        flops=6 * BLK * width * (width + rows),
        nbytes=4 * width * width + 24 * rows * width,
        after=after,
    )


def right_kernel(high_ref, low_ref, feats_ref, first_ref, left_ref, right_ref, out_ref, handed_ref, sem):
    half = left_ref.shape[1]
    copies = [
        pltpu.make_async_copy(left_ref, handed_ref.at[:, :half], sem.at[0]),
        pltpu.make_async_copy(right_ref, handed_ref.at[:, half:], sem.at[1]),
    ]
    for copy in copies:
        copy.start()
    out_ref[...] = times_adj(high_ref, low_ref, 0, feats_ref[...]) + 0.1 * first_ref[...]
    for copy in copies:
        copy.wait()


def own_right(adj, feats, first, left, right):
    rows, half = feats.shape
    return call(
        right_kernel,
        (*adj, feats, first, left, right),
        [VMEM] * 6,
        (vmem(rows, half), pltpu.HBM((rows, 2 * half), F32)),
        flops=6 * rows * rows * half,
        nbytes=28 * rows * half,
        scratch=[ONE((2,))],
    )


def left_kernel(high_ref, low_ref, feats_ref, first_ref, out_ref):
    out_ref[...] = times_adj(high_ref, low_ref, 0, feats_ref[...]) + 0.1 * first_ref[...]


def own_left(adj, feats, first):
    rows, half = feats.shape
    return call(
        left_kernel,
        (*adj, feats, first),
        [VMEM] * 4,
        (vmem(rows, half),),
        flops=6 * rows * rows * half,
        nbytes=12 * rows * half,
    )[0]


def add_kernel(high_ref, low_ref, base_ref, *refs):
    rows = base_ref.shape[0]
    refs[-1][...] = base_ref[...] + times_adj(high_ref, low_ref, rows, stacked(refs[:-1]))


def add_received(adj, base, came, after=()):
    rows, width = base.shape
    return call(
        add_kernel,
        (*adj, base, *came),
        [VMEM] * (3 + len(came)),
        (vmem(rows, width),),
        flops=6 * rows * len(came) * BLK * width,
        nbytes=8 * rows * width,
        after=after,
    )[0]


def second_kernel(beta_ref, high_ref, low_ref, left_ref, right_ref, weight_ref, *refs, tile):
    came, (out_ref, held, sem) = refs[:-3], refs[-3:]
    rows, half = left_ref.shape
    width = weight_ref.shape[1]
    left = left_ref[...] + times_adj(high_ref, low_ref, rows, stacked(came))
    mixed = (left, right_ref[...])
    pair = halves(jnp.concatenate(mixed, axis=1))
    beta = beta_ref[0]
    copies = []
    for i, at in enumerate(range(0, width, tile)):
        cut = slice(at, at + tile)
        own = mixed[at // half][:, at % half : at % half + tile]
        value = (1.0 - beta) * own + beta * dot3(pair, halves(weight_ref[:, cut]))
        held[:, cut] = jnp.maximum(value, 0.0)
        copies.append(pltpu.make_async_copy(held.at[:, cut], out_ref.at[:, cut], sem.at[i]))
        copies[-1].start()
    for copy in copies:
        copy.wait()


def second_layer(beta, adj, left, right, weight, came, tile=256):
    rows, half = left.shape
    width = weight.shape[1]
    return call(
        functools.partial(second_kernel, tile=tile),
        (beta, *adj, left, right, weight, *came),
        [SMEM] + [VMEM] * (5 + len(came)),
        (pltpu.HBM((rows, width), F32),),
        flops=6 * rows * width * (width + len(came) * BLK // 2),
        nbytes=4 * (width * width + 3 * rows * width),
        scratch=[pltpu.VMEM((rows, width), F32), ONE((width // tile,))],
        vmem=16,
    )[0]


def shards(state, initial, fresh, weights, wants, adj_slot, adj_count, adj_vals):
    section = lax.axis_index("segment")
    part = lax.axis_index("graph")
    beta = jnp.log(0.5 / (section.astype(F32) + 1.0) + 1.0).reshape(1)
    last = (section == lax.axis_size("segment") - 1).astype(jnp.int32).reshape(1)
    feats, first, weight = state[0], initial[0], weights[0]
    half = feats.shape[1] // 2
    asks = wants.reshape(wants.shape[1])

    place = []
    for position in range(2 * REACH):
        stride = position // 2 + 1
        low = (part // stride) % 2 == 0
        phase = jnp.where(low, 1 - position % 2, position % 2)
        place.append(jnp.where(phase == 0, SWAPS.index((stride, 0)), SWAPS.index((stride, 1))))
    place = jnp.stack(place).astype(jnp.int32)
    index = []
    for stride, phase in SWAPS:
        low = (part // stride) % 2 == phase
        index.append(jnp.where(low, 2 * stride - 2, 2 * stride - 1))
    index = jnp.stack(index).astype(jnp.int32)

    got = [swap(asks, *kind) for kind in SWAPS]
    final = len(SWAPS) - 1
    others = tuple(range(final))
    every = tuple(range(len(SWAPS)))

    sent = pick(others, index, got, feats, after=got[final:])
    came = [swap(value, *SWAPS[k]) for k, value in enumerate(sent)]
    *adj, sent = prepare(final, place, adj_slot, adj_count, index, got, adj_vals, feats, after=sent[:1])
    crossing = swap(sent, *SWAPS[final])
    known, first_left, first_right = early(beta, last, adj, weight, came, feats, first, fresh)
    handed_left = hand_on(first_left)
    out_left, out_right, left, right, *sent = late(
        every, beta, last, index, got, adj, known, weight, (first_left, first_right), crossing
    )

    left = hand_on(left)
    came = [swap(value, *kind) for value, kind in zip(sent, SWAPS)]
    mixed, first_out = own_right(adj, right, first_right, out_left, out_right)
    sent = choose(every, index, got, left)
    right = hand_on(add_received(adj, mixed, came, after=sent[:1]))
    came = [swap(value, *kind) for value, kind in zip(sent, SWAPS)]
    mixed = own_left(adj, left, handed_left)
    second_out = second_layer(beta, adj, mixed, right, weight, came)
    return first_out[None], second_out[None]


def solution(mesh):
    return jax.shard_map(
        shards,
        mesh=mesh,
        in_specs=(
            P("segment", "graph", None),
            P("segment", "graph", None),
            P("graph", None),
            P("segment", None, None),
            P("graph", None, None),
            P("graph", None),
            P("graph"),
            P("graph", None, None, None),
        ),
        out_specs=(P("segment", "graph", None), P("segment", "graph", None)),
        check_vma=False,
    )
```

time: 157 us -> 91.4 us (0.58)
  the two profiles are of different devices: /device:TPU:2 before, /device:TPU:10 now
where the time goes in v2:
time: 91.4 us; the launch traced here: 91 us
  waiting for transfers between devices  33.1 us (36%)
  starting transfers between devices  28.6 us (31%)
  Pallas kernels  25.8 us (28%)
  local copies, waits for them, and re-layouts  2.2 us (2%)
  between operations  1.22 us (1%)
    ppermute x16, starting transfers between devices, swap(): return lax.ppermute(value, 'graph', sorted(pairs))  27.8 us
    pallas_call x9, Pallas kernels, call(): pl.pallas_call(body, out_shape=outs, in_specs=list(in_specs) + [VMEM] * l...  25.8 us
    ppermute x3, waiting for transfers between devices, hand_on(): lax.ppermute(value, 'segment', [(i, (i + 1) % peers) for i in range(peers)])  16.6 us
    ppermute x16, waiting for transfers between devices, swap(): return lax.ppermute(value, 'graph', sorted(pairs))  16.5 us
    unnamed x8, local copies, waits for them, and re-layouts  2.2 us
  transfers between devices with their start and end apart: 19, of which 8 were waited for; matrix products, arithmetic and copies ran while one was open for 0% of the time, Pallas kernels for 17%

profile of v2, /device:TPU:10, one launch (start us, length us, event | category | flops | bytes accessed | tf_op | source)
XLA Modules:
  0.0 91.0 jit_solution(15196096551698915846)
XLA Ops:
  0.7 3.4 %collective-permute-start = (s32[4]{0:T(128)}, s32[4]{0:T(128)S(1)}, u32[]{:S(2)}, u32[]{:S(2)}) collective-permute-start(s32[4]{0:T(128)} %bitcast.24), channel_id=1, source_target_pairs={{1,2},{2,1},{3,4},{4,3},{5,6},{6,5},{9,10},{10,9},{11,12},{12,11},... | collective-permute-start | bytes 56 | tf_op jit(solution)/shard_map/ppermute | solution.py:27
  4.1 1.7 %collective-permute-start.1 = (s32[4]{0:T(128)}, s32[4]{0:T(128)S(1)}, u32[]{:S(2)}, u32[]{:S(2)}) collective-permute-start(s32[4]{0:T(128)} %bitcast.25), channel_id=1, source_target_pairs={{0,1},{1,0},{2,3},{3,2},{4,5},{5,4},{6,7},{7,6},{8,9},{9,8},{10,11... | collective-permute-start | bytes 56 | tf_op jit(solution)/shard_map/ppermute | solution.py:27
  5.8 0.4 collective-permute-start.2
  6.3 3.0 %collective-permute-start.3 = (s32[4]{0:T(128)}, s32[4]{0:T(128)S(1)}, u32[]{:S(2)}, u32[]{:S(2)}) collective-permute-start(s32[4]{0:T(128)} %bitcast.27), channel_id=1, source_target_pairs={{2,4},{3,5},{4,2},{5,3},{10,12},{11,13},{12,10},{13,11},{18,20},{1... | collective-permute-start | bytes 56 | tf_op jit(solution)/shard_map/ppermute | solution.py:27
  9.4 0.1 pad_add_fusion
  9.5 2.3 %collective-permute-done.3.refs_3_.refs_5_ = s32[4]{0:T(128)S(1)} collective-permute-done((s32[4]{0:T(128)}, s32[4]{0:T(128)S(1)}, u32[]{:S(2)}, u32[]{:S(2)}) %collective-permute-start.3) | collective-permute-done | bytes 48 | tf_op jit(solution)/shard_map/ppermute | solution.py:27
  11.8 2.0 %shard_map.95 = (f32[128,1024]{1,0:T(8,128)S(1)}, f32[128,1024]{1,0:T(8,128)S(1)}, f32[128,1024]{1,0:T(8,128)S(1)}) custom-call(s32[4]{0:T(128)S(1)} %get-tuple-element.49.refs_0_.refs_3_.refs_2_, s32[4]{0:T(128)S(1)} %collective-permute-done.1.refs_1_.refs_3_, s32[4]{0:T(128)S(1)} %collective-permute-done.2.refs_2_.refs_4_, ...), custom_call_target="tpu_custom_call" | custom-call | bytes 3145728 | tf_op jit(solution)/shard_map/pallas_call | solution.py:51
  13.8 1.1 %collective-permute-start.4 = (f32[128,1024]{1,0:T(8,128)S(1)}, f32[128,1024]{1,0:T(8,128)S(1)}, u32[]{:S(2)}, u32[]{:S(2)}) collective-permute-start(f32[128,1024]{1,0:T(8,128)S(1)} %get-tuple-element.25.refs_7_), channel_id=1, source_target_pairs={{0,1},{1,0},{2,3},{3,2},{4,5},{5,4},{6,7},{7,6},{8,9},{9,8},{10,11... | collective-permute-start | bytes 1572872 | tf_op jit(solution)/shard_map/ppermute | solution.py:27
  14.9 3.9 %collective-permute-start.6 = (f32[128,1024]{1,0:T(8,128)S(1)}, f32[128,1024]{1,0:T(8,128)S(1)}, u32[]{:S(2)}, u32[]{:S(2)}) collective-permute-start(f32[128,1024]{1,0:T(8,128)S(1)} %get-tuple-element.29), channel_id=1, source_target_pairs={{2,4},{3,5},{4,2},{5,3},{10,12},{11,13},{12,10},{13,11},{18,20},{1... | collective-permute-start | bytes 1572872 | tf_op jit(solution)/shard_map/ppermute | solution.py:27
  18.9 2.6 %shard_map.96 = (bf16[512,1024]{1,0:T(8,128)(2,1)S(1)}, bf16[512,1024]{1,0:T(8,128)(2,1)S(1)}, f32[128,1024]{1,0:T(8,128)S(1)}) custom-call(s32[4]{0:T(128)S(1)} %get-tuple-element.48.refs_0_, s32[4,4]{1,0:T(4,128)S(1)} %copy-done.2, s32[4]{0:T(128)S(1)} %copy-done.3, s32[4]{0:T(128)S(1)} %get-tuple-element.49.refs_0_.refs_3_.refs_2_, ...), custom_call_target="tpu_custom_call" | custom-call | bytes 3145728 | tf_op jit(solution)/shard_map/pallas_call | solution.py:51
  21.6 1.9 %collective-permute-start.7 = (f32[128,1024]{1,0:T(8,128)S(1)}, f32[128,1024]{1,0:T(8,128)S(1)}, u32[]{:S(2)}, u32[]{:S(2)}) collective-permute-start(f32[128,1024]{1,0:T(8,128)S(1)} %get-tuple-element.33), channel_id=1, source_target_pairs={{1,2},{2,1},{3,4},{4,3},{5,6},{6,5},{9,10},{10,9},{11,12},{12,11},... | collective-permute-start | bytes 1572872 | tf_op jit(solution)/shard_map/ppermute | solution.py:27
  23.5 3.2 %collective-permute-done.4.refs_5_ = f32[128,1024]{1,0:T(8,128)S(1)} collective-permute-done((f32[128,1024]{1,0:T(8,128)S(1)}, f32[128,1024]{1,0:T(8,128)S(1)}, u32[]{:S(2)}, u32[]{:S(2)}) %collective-permute-start.4) | collective-permute-done | bytes 524320 | tf_op jit(solution)/shard_map/ppermute | solution.py:27
  26.7 0.6 collective-permute-done.5.refs_6_
  27.3 4.4 %collective-permute-done.6.refs_7_ = f32[128,1024]{1,0:T(8,128)S(1)} collective-permute-done((f32[128,1024]{1,0:T(8,128)S(1)}, f32[128,1024]{1,0:T(8,128)S(1)}, u32[]{:S(2)}, u32[]{:S(2)}) %collective-permute-start.6) | collective-permute-done | bytes 524320 | tf_op jit(solution)/shard_map/ppermute | solution.py:27
  31.7 2.2 %copy-done = f32[1,1024,1024]{2,1,0:T(8,128)S(1)} copy-done((f32[1,1024,1024]{2,1,0:T(8,128)S(1)}, f32[1,1024,1024]{2,1,0:T(8,128)}, u32[]{:S(2)}) %copy-start) | copy-done | bytes 4194328
  33.9 8.5 %shard_map.97 = (f32[512,1024]{1,0:T(8,128)S(1)}, f32[512,512]{1,0:T(8,128)S(1)}, f32[512,512]{1,0:T(8,128)S(1)}) custom-call(f32[1]{0:T(128)} %bitcast.10.refs_0_, s32[1]{0:T(128)} %bitcast.11.refs_1_, bf16[512,1024]{1,0:T(8,128)(2,1)S(1)} %get-tuple-element.26.refs_2_.refs_7_.refs_0_.refs_1_, ...), custom_call_target="tpu_custom_call" | custom-call | flops 6039797760 | bytes 14680064 | tf_op jit(solution)/shard_map/pallas_call | solution.py:51
  42.4 3.3 %shard_map.98 = (f32[512,512]{1,0:T(8,128)S(1)}, f32[512,512]{1,0:T(8,128)S(1)}, f32[512,512]{1,0:T(8,128)S(1)}, f32[512,512]{1,0:T(8,128)S(1)}, f32[128,512]{1,...) custom-call(f32[1]{0:T(128)} %bitcast.10.refs_0_, s32[1]{0:T(128)} %bitcast.11.refs_1_, ...), custom_call_target="tpu_custom_call" | custom-call | flops 1207959552 | bytes 16777216 | tf_op jit(solution)/shard_map/pallas_call | solution.py:51
  45.9 3.9 %collective-permute-start.12 = (f32[128,512]{1,0:T(8,128)S(1)}, f32[128,512]{1,0:T(8,128)S(1)}, u32[]{:S(2)}, u32[]{:S(2)}) collective-permute-start(f32[128,512]{1,0:T(8,128)S(1)} %get-tuple-element.42), channel_id=1, source_target_pairs={{2,4},{3,5},{4,2},{5,3},{10,12},{11,13},{12,10},{13,11},{18,20},{1... | collective-permute-start | bytes 786440 | tf_op jit(solution)/shard_map/ppermute | solution.py:27
  49.8 2.1 %collective-permute-start.13 = (f32[128,512]{1,0:T(8,128)S(1)}, f32[128,512]{1,0:T(8,128)S(1)}, u32[]{:S(2)}, u32[]{:S(2)}) collective-permute-start(f32[128,512]{1,0:T(8,128)S(1)} %get-tuple-element.43), channel_id=1, source_target_pairs={{1,2},{2,1},{3,4},{4,3},{5,6},{6,5},{9,10},{10,9},{11,12},{12,11},... | collective-permute-start | bytes 786440 | tf_op jit(solution)/shard_map/ppermute | solution.py:27
  51.8 8.1 %collective-permute-done.8.refs_2_.refs_5_ = f32[512,512]{1,0:T(8,128)S(1)} collective-permute-done((f32[512,512]{1,0:T(8,128)S(1)}, f32[512,512]{1,0:T(8,128)S(1)}, u32[]{:S(2)}, u32[]{:S(2)}) %collective-permute-start.8) | collective-permute-done | bytes 1048608 | tf_op jit(solution)/shard_map/ppermute | solution.py:32
  59.9 1.4 %shard_map.99 = (f32[512,512]{1,0:T(8,128)S(1)}, f32[512,1024]{1,0:T(8,128)}) custom-call(bf16[512,1024]{1,0:T(8,128)(2,1)S(1)} %get-tuple-element.26.refs_2_.refs_7_.refs_0_.refs_1_, bf16[512,1024]{1,0:T(8,128)(2,1)S(1)} %get-tuple-element.27.refs_3_.refs_8_.refs_1_.refs_2_, f32[512,512]{1,0:T(8,128)S(1)} %get-tuple-element.34.refs_2_, ...), custom_call_target="tpu_custom_call" | custom-call | flops 805306368 | bytes 7340032 | tf_op jit(solution)/shard_map/pallas_call | solution.py:51
  61.3 0.6 shard_map.101
  62.0 1.0 %shard_map.102 = f32[512,512]{1,0:T(8,128)S(1)} custom-call(bf16[512,1024]{1,0:T(8,128)(2,1)S(1)} %get-tuple-element.26.refs_2_.refs_7_.refs_0_.refs_1_, bf16[512,1024]{1,0:T(8,128)(2,1)S(1)} %get-tuple-element.27.refs_3_.refs_8_.refs_1_.refs_2_, f32[512,512]{1,0:T(8,128)S(1)} %get-tuple-element.39.refs_2_, f32[128,512]{1,0:T(8,128)S(1)} %collective-permute-done.10.refs_3_, ...), custom_call_target="tpu_custom_call" | custom-call | flops 805306368 | bytes 2097152 | tf_op jit(solution)/shard_map/pallas_call | solution.py:51
  63.0 0.7 collective-permute-start.14
  63.7 1.1 %collective-permute-start.15 = (f32[128,512]{1,0:T(8,128)S(1)}, f32[128,512]{1,0:T(8,128)S(1)}, u32[]{:S(2)}, u32[]{:S(2)}) collective-permute-start(f32[128,512]{1,0:T(8,128)S(1)} %get-tuple-element.44.refs_7_), channel_id=1, source_target_pairs={{0,1},{1,0},{2,3},{3,2},{4,5},{5,4},{6,7},{7,6},{8,9},{9,8},{10,11... | collective-permute-start | bytes 786440 | tf_op jit(solution)/shard_map/ppermute | solution.py:27
  64.7 2.9 %collective-permute-start.17 = (f32[128,512]{1,0:T(8,128)S(1)}, f32[128,512]{1,0:T(8,128)S(1)}, u32[]{:S(2)}, u32[]{:S(2)}) collective-permute-start(f32[128,512]{1,0:T(8,128)S(1)} %get-tuple-element.46), channel_id=1, source_target_pairs={{2,4},{3,5},{4,2},{5,3},{10,12},{11,13},{12,10},{13,11},{18,20},{1... | collective-permute-start | bytes 786440 | tf_op jit(solution)/shard_map/ppermute | solution.py:27
  67.7 6.4 %collective-permute-done.9.refs_3_ = f32[512,512]{1,0:T(8,128)S(1)} collective-permute-done((f32[512,512]{1,0:T(8,128)S(1)}, f32[512,512]{1,0:T(8,128)S(1)}, u32[]{:S(2)}, u32[]{:S(2)}) %collective-permute-start.9) | collective-permute-done | bytes 1048608 | tf_op jit(solution)/shard_map/ppermute | solution.py:32
  74.1 2.1 %collective-permute-start.18 = (f32[128,512]{1,0:T(8,128)S(1)}, f32[128,512]{1,0:T(8,128)S(1)}, u32[]{:S(2)}, u32[]{:S(2)}) collective-permute-start(f32[128,512]{1,0:T(8,128)S(1)} %get-tuple-element.47), channel_id=1, source_target_pairs={{1,2},{2,1},{3,4},{4,3},{5,6},{6,5},{9,10},{10,9},{11,12},{12,11},... | collective-permute-start | bytes 786440 | tf_op jit(solution)/shard_map/ppermute | solution.py:27
  76.2 1.0 %shard_map.100.refs_3_ = f32[512,512]{1,0:T(8,128)S(1)} custom-call(bf16[512,1024]{1,0:T(8,128)(2,1)S(1)} %get-tuple-element.26.refs_2_.refs_7_.refs_0_.refs_1_, bf16[512,1024]{1,0:T(8,128)(2,1)S(1)} %get-tuple-element.27.refs_3_.refs_8_.refs_1_.refs_2_, f32[512,512]{1,0:T(8,128)S(1)} %collective-permute-done.8.refs_2_.refs_5_, ...), custom_call_target="tpu_custom_call" | custom-call | flops 805306368 | bytes 3145728 | tf_op jit(solution)/shard_map/pallas_call | solution.py:51
  77.3 6.0 %collective-permute-done.18.refs_9_ = f32[128,512]{1,0:T(8,128)S(1)} collective-permute-done((f32[128,512]{1,0:T(8,128)S(1)}, f32[128,512]{1,0:T(8,128)S(1)}, u32[]{:S(2)}, u32[]{:S(2)}) %collective-permute-start.18) | collective-permute-done | bytes 262176 | tf_op jit(solution)/shard_map/ppermute | solution.py:27
  83.3 2.1 %collective-permute-done.14.refs_4_ = f32[512,512]{1,0:T(8,128)S(1)} collective-permute-done((f32[512,512]{1,0:T(8,128)S(1)}, f32[512,512]{1,0:T(8,128)S(1)}, u32[]{:S(2)}, u32[]{:S(2)}) %collective-permute-start.14) | collective-permute-done | bytes 1048608 | tf_op jit(solution)/shard_map/ppermute | solution.py:32
  85.4 5.5 %shard_map.103 = f32[512,1024]{1,0:T(8,128)} custom-call(f32[1]{0:T(128)} %bitcast.10.refs_0_, bf16[512,1024]{1,0:T(8,128)(2,1)S(1)} %get-tuple-element.26.refs_2_.refs_7_.refs_0_.refs_1_, bf16[512,1024]{1,0:T(8,128)(2,1)S(1)} %get-tuple-element.27.refs_3_.refs_8_.refs_1_.refs_2_, f32[512,512]{1,0:T(8,128)S(1)} %shard_map.100.refs_3_, ...), custom_call_target="tpu_custom_call" | custom-call | flops 4026531840 | bytes 10485760 | tf_op jit(solution)/shard_map/pallas_call | solution.py:51
  (24 shorter events, 0.3 us)
Async XLA Ops:
  0.6 18.3 %copy-start.2 = (s32[4,4]{1,0:T(4,128)S(1)}, s32[4,4]{1,0:T(4,128)}, u32[]{:S(2)}) copy-start(s32[4,4]{1,0:T(4,128)} %refs_1_.1) | copy-start | bytes 196
  0.6 18.3 %copy-start.3 = (s32[4]{0:T(128)S(1)}, s32[4]{0:T(128)}, u32[]{:S(2)}) copy-start(s32[4]{0:T(128)} %refs_2_.1) | copy-start | bytes 52
  0.7 8.8 %collective-permute-start = (s32[4]{0:T(128)}, s32[4]{0:T(128)S(1)}, u32[]{:S(2)}, u32[]{:S(2)}) collective-permute-start(s32[4]{0:T(128)} %bitcast.24), channel_id=1, source_target_pairs={{1,2},{2,1},{3,4},{4,3},{5,6},{6,5},{9,10},{10,9},{11,12},{12,11},... | collective-permute-start | bytes 56 | tf_op jit(solution)/shard_map/ppermute | solution.py:27
  4.1 5.4 %collective-permute-start.1 = (s32[4]{0:T(128)}, s32[4]{0:T(128)S(1)}, u32[]{:S(2)}, u32[]{:S(2)}) collective-permute-start(s32[4]{0:T(128)} %bitcast.25), channel_id=1, source_target_pairs={{0,1},{1,0},{2,3},{3,2},{4,5},{5,4},{6,7},{7,6},{8,9},{9,8},{10,11... | collective-permute-start | bytes 56 | tf_op jit(solution)/shard_map/ppermute | solution.py:27
  5.8 3.7 %collective-permute-start.2 = (s32[4]{0:T(128)}, s32[4]{0:T(128)S(1)}, u32[]{:S(2)}, u32[]{:S(2)}) collective-permute-start(s32[4]{0:T(128)} %bitcast.26), channel_id=1, source_target_pairs={{0,2},{1,3},{2,0},{3,1},{4,6},{5,7},{6,4},{7,5},{8,10},{9,11},{10,... | collective-permute-start | bytes 56 | tf_op jit(solution)/shard_map/ppermute | solution.py:27
  6.3 5.6 %collective-permute-start.3 = (s32[4]{0:T(128)}, s32[4]{0:T(128)S(1)}, u32[]{:S(2)}, u32[]{:S(2)}) collective-permute-start(s32[4]{0:T(128)} %bitcast.27), channel_id=1, source_target_pairs={{2,4},{3,5},{4,2},{5,3},{10,12},{11,13},{12,10},{13,11},{18,20},{1... | collective-permute-start | bytes 56 | tf_op jit(solution)/shard_map/ppermute | solution.py:27
  13.8 12.9 %collective-permute-start.4 = (f32[128,1024]{1,0:T(8,128)S(1)}, f32[128,1024]{1,0:T(8,128)S(1)}, u32[]{:S(2)}, u32[]{:S(2)}) collective-permute-start(f32[128,1024]{1,0:T(8,128)S(1)} %get-tuple-element.25.refs_7_), channel_id=1, source_target_pairs={{0,1},{1,0},{2,3},{3,2},{4,5},{5,4},{6,7},{7,6},{8,9},{9,8},{10,11... | collective-permute-start | bytes 1572872 | tf_op jit(solution)/shard_map/ppermute | solution.py:27
  14.9 12.4 %collective-permute-start.5 = (f32[128,1024]{1,0:T(8,128)S(1)}, f32[128,1024]{1,0:T(8,128)S(1)}, u32[]{:S(2)}, u32[]{:S(2)}) collective-permute-start(f32[128,1024]{1,0:T(8,128)S(1)} %get-tuple-element.28), channel_id=1, source_target_pairs={{0,2},{1,3},{2,0},{3,1},{4,6},{5,7},{6,4},{7,5},{8,10},{9,11},{10,... | collective-permute-start | bytes 1572872 | tf_op jit(solution)/shard_map/ppermute | solution.py:27
  14.9 16.7 %collective-permute-start.6 = (f32[128,1024]{1,0:T(8,128)S(1)}, f32[128,1024]{1,0:T(8,128)S(1)}, u32[]{:S(2)}, u32[]{:S(2)}) collective-permute-start(f32[128,1024]{1,0:T(8,128)S(1)} %get-tuple-element.29), channel_id=1, source_target_pairs={{2,4},{3,5},{4,2},{5,3},{10,12},{11,13},{12,10},{13,11},{18,20},{1... | collective-permute-start | bytes 1572872 | tf_op jit(solution)/shard_map/ppermute | solution.py:27
  21.6 20.8 %collective-permute-start.7 = (f32[128,1024]{1,0:T(8,128)S(1)}, f32[128,1024]{1,0:T(8,128)S(1)}, u32[]{:S(2)}, u32[]{:S(2)}) collective-permute-start(f32[128,1024]{1,0:T(8,128)S(1)} %get-tuple-element.33), channel_id=1, source_target_pairs={{1,2},{2,1},{3,4},{4,3},{5,6},{6,5},{9,10},{10,9},{11,12},{12,11},... | collective-permute-start | bytes 1572872 | tf_op jit(solution)/shard_map/ppermute | solution.py:27
  31.7 2.2 %copy-start = (f32[1,1024,1024]{2,1,0:T(8,128)S(1)}, f32[1,1024,1024]{2,1,0:T(8,128)}, u32[]{:S(2)}) copy-start(f32[1,1024,1024]{2,1,0:T(8,128)} %param.11) | copy-start | bytes 12582916
  33.9 8.5 %copy-start.1 = (f32[1,1024,1024]{2,1,0:T(8,128)S(1)}, f32[1,1024,1024]{2,1,0:T(8,128)}, u32[]{:S(2)}) copy-start(f32[1,1024,1024]{2,1,0:T(8,128)} %param.11) | copy-start | bytes 12582916
  45.6 14.3 %collective-permute-start.8 = (f32[512,512]{1,0:T(8,128)S(1)}, f32[512,512]{1,0:T(8,128)S(1)}, u32[]{:S(2)}, u32[]{:S(2)}) collective-permute-start(f32[512,512]{1,0:T(8,128)S(1)} %get-tuple-element.38), channel_id=1, source_target_pairs={{0,8},{8,16},{16,24},{24,0},{1,9},{9,17},{17,25},{25,1},{2,10},{10... | collective-permute-start | bytes 3145736 | tf_op jit(solution)/shard_map/ppermute | solution.py:32
  45.7 16.2 %collective-permute-start.10 = (f32[128,512]{1,0:T(8,128)S(1)}, f32[128,512]{1,0:T(8,128)S(1)}, u32[]{:S(2)}, u32[]{:S(2)}) collective-permute-start(f32[128,512]{1,0:T(8,128)S(1)} %get-tuple-element.40), channel_id=1, source_target_pairs={{0,1},{1,0},{2,3},{3,2},{4,5},{5,4},{6,7},{7,6},{8,9},{9,8},{10,11... | collective-permute-start | bytes 786440 | tf_op jit(solution)/shard_map/ppermute | solution.py:27
  45.8 16.2 %collective-permute-start.11 = (f32[128,512]{1,0:T(8,128)S(1)}, f32[128,512]{1,0:T(8,128)S(1)}, u32[]{:S(2)}, u32[]{:S(2)}) collective-permute-start(f32[128,512]{1,0:T(8,128)S(1)} %get-tuple-element.41), channel_id=1, source_target_pairs={{0,2},{1,3},{2,0},{3,1},{4,6},{5,7},{6,4},{7,5},{8,10},{9,11},{10,... | collective-permute-start | bytes 786440 | tf_op jit(solution)/shard_map/ppermute | solution.py:27
  45.9 16.1 %collective-permute-start.12 = (f32[128,512]{1,0:T(8,128)S(1)}, f32[128,512]{1,0:T(8,128)S(1)}, u32[]{:S(2)}, u32[]{:S(2)}) collective-permute-start(f32[128,512]{1,0:T(8,128)S(1)} %get-tuple-element.42), channel_id=1, source_target_pairs={{2,4},{3,5},{4,2},{5,3},{10,12},{11,13},{12,10},{13,11},{18,20},{1... | collective-permute-start | bytes 786440 | tf_op jit(solution)/shard_map/ppermute | solution.py:27
  49.8 12.2 %collective-permute-start.13 = (f32[128,512]{1,0:T(8,128)S(1)}, f32[128,512]{1,0:T(8,128)S(1)}, u32[]{:S(2)}, u32[]{:S(2)}) collective-permute-start(f32[128,512]{1,0:T(8,128)S(1)} %get-tuple-element.43), channel_id=1, source_target_pairs={{1,2},{2,1},{3,4},{4,3},{5,6},{6,5},{9,10},{10,9},{11,12},{12,11},... | collective-permute-start | bytes 786440 | tf_op jit(solution)/shard_map/ppermute | solution.py:27
  59.9 14.2 %collective-permute-start.9 = (f32[512,512]{1,0:T(8,128)S(1)}, f32[512,512]{1,0:T(8,128)S(1)}, u32[]{:S(2)}, u32[]{:S(2)}) collective-permute-start(f32[512,512]{1,0:T(8,128)S(1)} %get-tuple-element.31.refs_11_), channel_id=1, source_target_pairs={{0,8},{8,16},{16,24},{24,0},{1,9},{9,17},{17,25},{25,1},{2,10},{10... | collective-permute-start | bytes 3145736 | tf_op jit(solution)/shard_map/ppermute | solution.py:32
  63.0 22.4 %collective-permute-start.14 = (f32[512,512]{1,0:T(8,128)S(1)}, f32[512,512]{1,0:T(8,128)S(1)}, u32[]{:S(2)}, u32[]{:S(2)}) collective-permute-start(f32[512,512]{1,0:T(8,128)S(1)} %shard_map.102), channel_id=1, source_target_pairs={{0,8},{8,16},{16,24},{24,0},{1,9},{9,17},{17,25},{25,1},{2,10},{10... | collective-permute-start | bytes 3145736 | tf_op jit(solution)/shard_map/ppermute | solution.py:32
  63.7 13.6 %collective-permute-start.15 = (f32[128,512]{1,0:T(8,128)S(1)}, f32[128,512]{1,0:T(8,128)S(1)}, u32[]{:S(2)}, u32[]{:S(2)}) collective-permute-start(f32[128,512]{1,0:T(8,128)S(1)} %get-tuple-element.44.refs_7_), channel_id=1, source_target_pairs={{0,1},{1,0},{2,3},{3,2},{4,5},{5,4},{6,7},{7,6},{8,9},{9,8},{10,11... | collective-permute-start | bytes 786440 | tf_op jit(solution)/shard_map/ppermute | solution.py:27
  64.7 12.5 %collective-permute-start.16 = (f32[128,512]{1,0:T(8,128)S(1)}, f32[128,512]{1,0:T(8,128)S(1)}, u32[]{:S(2)}, u32[]{:S(2)}) collective-permute-start(f32[128,512]{1,0:T(8,128)S(1)} %get-tuple-element.45), channel_id=1, source_target_pairs={{0,2},{1,3},{2,0},{3,1},{4,6},{5,7},{6,4},{7,5},{8,10},{9,11},{10,... | collective-permute-start | bytes 786440 | tf_op jit(solution)/shard_map/ppermute | solution.py:27
  64.7 12.5 %collective-permute-start.17 = (f32[128,512]{1,0:T(8,128)S(1)}, f32[128,512]{1,0:T(8,128)S(1)}, u32[]{:S(2)}, u32[]{:S(2)}) collective-permute-start(f32[128,512]{1,0:T(8,128)S(1)} %get-tuple-element.46), channel_id=1, source_target_pairs={{2,4},{3,5},{4,2},{5,3},{10,12},{11,13},{12,10},{13,11},{18,20},{1... | collective-permute-start | bytes 786440 | tf_op jit(solution)/shard_map/ppermute | solution.py:27
  74.1 9.2 %collective-permute-start.18 = (f32[128,512]{1,0:T(8,128)S(1)}, f32[128,512]{1,0:T(8,128)S(1)}, u32[]{:S(2)}, u32[]{:S(2)}) collective-permute-start(f32[128,512]{1,0:T(8,128)S(1)} %get-tuple-element.47), channel_id=1, source_target_pairs={{1,2},{2,1},{3,4},{4,3},{5,6},{6,5},{9,10},{10,9},{11,12},{12,11},... | collective-permute-start | bytes 786440 | tf_op jit(solution)/shard_map/ppermute | solution.py:27

commit v3 on v2

--- a/solution.py
+++ b/solution.py
@@ -63,8 +63,17 @@
     return jax.ShapeDtypeStruct(shape, dtype)
 
 
-def prepare_kernel(place_ref, slot_ref, count_ref, index_ref, got_ref, *refs, kind):
-    vals_ref, feats_ref, high_ref, low_ref, sent_ref, held, total, sem = refs
+def prepare_kernel(place_ref, slot_ref, count_ref, index_ref, got_ref, last_ref, *refs, kind):
+    (vals_ref, feats_ref, first_ref, fresh_ref), refs = refs[:4], refs[4:]
+    high_ref, low_ref, sent_ref, left_ref, right_ref, held, total, sem = refs
+    half = left_ref.shape[1]
+    for mine, origin in ((last_ref[0] == 0, first_ref), (last_ref[0] != 0, fresh_ref)):
+
+        @pl.when(mine)
+        def _():
+            pltpu.make_async_copy(origin.at[:, :half], left_ref, sem.at[2]).start()
+            pltpu.make_async_copy(origin.at[:, half:], right_ref, sem.at[3]).start()
+
     copies = [pltpu.make_async_copy(vals_ref, held, sem.at[0])]
     row = pl.multiple_of(got_ref[index_ref[kind]] * BLK, BLK)
     copies.append(pltpu.make_async_copy(feats_ref.at[pl.ds(row, BLK)], sent_ref, sem.at[1]))
@@ -85,22 +94,24 @@
     high_ref[...] = high
     low_ref[...] = low
     copies[1].wait()
+    pltpu.make_async_copy(first_ref.at[:, :half], left_ref, sem.at[2]).wait()
+    pltpu.make_async_copy(first_ref.at[:, half:], right_ref, sem.at[3]).wait()
 
 
 def in_hbm(value):
     return pltpu.with_memory_space_constraint(value, pltpu.HBM)
 
 
-def prepare(kind, place, slots, counts, index, got, vals, feats, after=()):
+def prepare(kind, place, slots, counts, index, got, last, vals, feats, first, fresh, after=()):
     rows, width = feats.shape
     span = rows + 2 * REACH * BLK
     return call(
         functools.partial(prepare_kernel, kind=kind),
-        (place, slots, counts, index, got[kind], in_hbm(vals), in_hbm(feats)),
-        [SMEM] * 5 + [HBM] * 2,
-        (vmem(rows, span, dtype=BF16),) * 2 + (vmem(BLK, width),),
+        (place, slots, counts, index, got[kind], last, *[in_hbm(v) for v in (vals, feats, first, fresh)]),
+        [SMEM] * 6 + [HBM] * 4,
+        (vmem(rows, span, dtype=BF16),) * 2 + (vmem(BLK, width),) + (vmem(rows, width // 2),) * 2,
         nbytes=4 * vals.size + 4 * rows * span,
-        scratch=[pltpu.VMEM(vals.shape, F32), pltpu.VMEM((rows, span), F32), ONE((2,))],
+        scratch=[pltpu.VMEM(vals.shape, F32), pltpu.VMEM((rows, span), F32), ONE((4,))],
         after=after,
     )
 
@@ -160,14 +171,14 @@
     return jnp.concatenate([ref[...] for ref in refs], axis=0)
 
 
-def early_kernel(beta_ref, last_ref, high_ref, low_ref, weight_ref, *refs):
-    came, sources, (out_ref, left_ref, right_ref), refs = refs[:-10], refs[-10:-7], refs[-7:-4], refs[-4:]
-    held, sem = refs[:3], refs[3]
-    feats_ref, first_ref, fresh_ref = held
+def early_kernel(beta_ref, high_ref, low_ref, weight_ref, *refs):
+    came, sources, out_ref, refs = refs[:-6], refs[-6:-4], refs[-4], refs[-3:]
+    held, sem = refs[:2], refs[2]
+    feats_ref, first_ref = held
     copies = [pltpu.make_async_copy(s, h, sem.at[i]) for i, (s, h) in enumerate(zip(sources, held))]
     for copy in copies:
         copy.start()
-    rows, half = left_ref.shape
+    rows = feats_ref.shape[0]
     mixed = times_adj(high_ref, low_ref, rows, stacked(came))
     copies[0].wait()
     mixed = mixed + times_adj(high_ref, low_ref, 0, feats_ref[...])
@@ -175,24 +186,20 @@
     mixed = mixed + 0.1 * first_ref[...]
     beta = beta_ref[0]
     out_ref[...] = (1.0 - beta) * mixed + beta * dot3(halves(mixed), halves(weight_ref[...]))
-    copies[2].wait()
-    last = last_ref[0] != 0
-    left_ref[...] = jnp.where(last, fresh_ref[:, :half], first_ref[:, :half])
-    right_ref[...] = jnp.where(last, fresh_ref[:, half:], first_ref[:, half:])
-
-
-def early(beta, last, adj, weight, came, feats, first, fresh):
+
+
+def early(beta, adj, weight, came, feats, first):
     rows, width = feats.shape
-    arrays = (feats, first, fresh)
+    arrays = (feats, first)
     return call(
         early_kernel,
-        (beta, last, *adj, weight, *came, *[in_hbm(v) for v in arrays]),
-        [SMEM] * 2 + [VMEM] * (3 + len(came)) + [HBM] * 3,
-        (vmem(rows, width),) + (vmem(rows, width // 2),) * 2,
+        (beta, *adj, weight, *came, *[in_hbm(v) for v in arrays]),
+        [SMEM] + [VMEM] * (3 + len(came)) + [HBM] * 2,
+        (vmem(rows, width),),
         flops=6 * rows * width * (width + rows + len(came) * BLK),
         nbytes=4 * (width * width + 5 * rows * width),
         scratch=[pltpu.VMEM(v.shape, F32) for v in arrays] + [ONE((len(arrays),))],
-    )
+    )[0]
 
 
 def late_kernel(beta_ref, last_ref, index_ref, *refs, kinds):
@@ -245,7 +252,7 @@
         copy.wait()
 
 
-def own_right(adj, feats, first, left, right):
+def own_right(adj, feats, first, left, right, after=()):
     rows, half = feats.shape
     return call(
         right_kernel,
@@ -255,6 +262,7 @@
         flops=6 * rows * rows * half,
         nbytes=28 * rows * half,
         scratch=[ONE((2,))],
+        after=after,
     )
 
 
@@ -356,17 +364,19 @@
 
     sent = pick(others, index, got, feats, after=got[final:])
     came = [swap(value, *SWAPS[k]) for k, value in enumerate(sent)]
-    *adj, sent = prepare(final, place, adj_slot, adj_count, index, got, adj_vals, feats, after=sent[:1])
+    *adj, sent, first_left, first_right = prepare(
+        final, place, adj_slot, adj_count, index, got, last, adj_vals, feats, first, fresh, after=sent[:1]
+    )
     crossing = swap(sent, *SWAPS[final])
-    known, first_left, first_right = early(beta, last, adj, weight, came, feats, first, fresh)
     handed_left = hand_on(first_left)
+    known = early(beta, adj, weight, came, feats, first)
     out_left, out_right, left, right, *sent = late(
         every, beta, last, index, got, adj, known, weight, (first_left, first_right), crossing
     )
 
     left = hand_on(left)
     came = [swap(value, *kind) for value, kind in zip(sent, SWAPS)]
-    mixed, first_out = own_right(adj, right, first_right, out_left, out_right)
+    mixed, first_out = own_right(adj, right, first_right, out_left, out_right, after=(handed_left,))
     sent = choose(every, index, got, left)
     right = hand_on(add_received(adj, mixed, came, after=sent[:1]))
     came = [swap(value, *kind) for value, kind in zip(sent, SWAPS)]

time: 91.4 us -> 86.2 us (0.943)
  the two profiles are of different devices: /device:TPU:10 before, /device:TPU:16 now
where the time goes in v3:
time: 86.2 us; the launch traced here: 85.8 us
  starting transfers between devices  30.4 us (35%)
  waiting for transfers between devices  27.8 us (32%)
  Pallas kernels  26.2 us (30%)
  between operations  1.19 us (1%)
    ppermute x16, starting transfers between devices, swap(): return lax.ppermute(value, 'graph', sorted(pairs))  30.1 us
    pallas_call x9, Pallas kernels, call(): pl.pallas_call(body, out_shape=outs, in_specs=list(in_specs) + [VMEM] * l...  26.2 us
    ppermute x16, waiting for transfers between devices, swap(): return lax.ppermute(value, 'graph', sorted(pairs))  22.4 us
    ppermute x3, waiting for transfers between devices, hand_on(): lax.ppermute(value, 'segment', [(i, (i + 1) % peers) for i in range(peers)])  5.46 us
  transfers between devices with their start and end apart: 19, of which 11 were waited for; matrix products, arithmetic and copies ran while one was open for 0% of the time, Pallas kernels for 21%

profile of v3, /device:TPU:16, one launch (start us, length us, event | category | flops | bytes accessed | tf_op | source)
XLA Modules:
  0.0 85.8 jit_solution(5112579263756313370)
XLA Ops:
  0.7 3.4 %collective-permute-start = (s32[4]{0:T(128)}, s32[4]{0:T(128)S(1)}, u32[]{:S(2)}, u32[]{:S(2)}) collective-permute-start(s32[4]{0:T(128)} %bitcast.25), channel_id=1, source_target_pairs={{1,2},{2,1},{3,4},{4,3},{5,6},{6,5},{9,10},{10,9},{11,12},{12,11},... | collective-permute-start | bytes 56 | tf_op jit(solution)/shard_map/ppermute | solution.py:27
  4.1 1.7 %collective-permute-start.1 = (s32[4]{0:T(128)}, s32[4]{0:T(128)S(1)}, u32[]{:S(2)}, u32[]{:S(2)}) collective-permute-start(s32[4]{0:T(128)} %bitcast.26), channel_id=1, source_target_pairs={{0,1},{1,0},{2,3},{3,2},{4,5},{5,4},{6,7},{7,6},{8,9},{9,8},{10,11... | collective-permute-start | bytes 56 | tf_op jit(solution)/shard_map/ppermute | solution.py:27
  5.8 2.8 %collective-permute-start.3 = (s32[4]{0:T(128)}, s32[4]{0:T(128)S(1)}, u32[]{:S(2)}, u32[]{:S(2)}) collective-permute-start(s32[4]{0:T(128)} %bitcast.28), channel_id=1, source_target_pairs={{2,4},{3,5},{4,2},{5,3},{10,12},{11,13},{12,10},{13,11},{18,20},{1... | collective-permute-start | bytes 56 | tf_op jit(solution)/shard_map/ppermute | solution.py:27
  8.8 0.7 collective-permute-done.2.refs_2_.refs_4_
  9.5 1.9 %collective-permute-done.3.refs_3_.refs_5_ = s32[4]{0:T(128)S(1)} collective-permute-done((s32[4]{0:T(128)}, s32[4]{0:T(128)S(1)}, u32[]{:S(2)}, u32[]{:S(2)}) %collective-permute-start.3) | collective-permute-done | bytes 48 | tf_op jit(solution)/shard_map/ppermute | solution.py:27
  11.4 2.0 %shard_map.95 = (f32[128,1024]{1,0:T(8,128)S(1)}, f32[128,1024]{1,0:T(8,128)S(1)}, f32[128,1024]{1,0:T(8,128)S(1)}) custom-call(s32[4]{0:T(128)S(1)} %get-tuple-element.47.refs_0_.refs_3_.refs_2_, s32[4]{0:T(128)S(1)} %collective-permute-done.1.refs_1_.refs_3_, s32[4]{0:T(128)S(1)} %collective-permute-done.2.refs_2_.refs_4_, ...), custom_call_target="tpu_custom_call" | custom-call | bytes 3145728 | tf_op jit(solution)/shard_map/pallas_call | solution.py:51
  13.3 2.0 %collective-permute-start.4 = (f32[128,1024]{1,0:T(8,128)S(1)}, f32[128,1024]{1,0:T(8,128)S(1)}, u32[]{:S(2)}, u32[]{:S(2)}) collective-permute-start(f32[128,1024]{1,0:T(8,128)S(1)} %get-tuple-element.24.refs_10_), channel_id=1, source_target_pairs={{0,1},{1,0},{2,3},{3,2},{4,5},{5,4},{6,7},{7,6},{8,9},{9,8},{10,11... | collective-permute-start | bytes 1572872 | tf_op jit(solution)/shard_map/ppermute | solution.py:27
  15.4 1.9 %collective-permute-start.6 = (f32[128,1024]{1,0:T(8,128)S(1)}, f32[128,1024]{1,0:T(8,128)S(1)}, u32[]{:S(2)}, u32[]{:S(2)}) collective-permute-start(f32[128,1024]{1,0:T(8,128)S(1)} %get-tuple-element.28), channel_id=1, source_target_pairs={{2,4},{3,5},{4,2},{5,3},{10,12},{11,13},{12,10},{13,11},{18,20},{1... | collective-permute-start | bytes 1572872 | tf_op jit(solution)/shard_map/ppermute | solution.py:27
  17.4 3.6 %shard_map.96 = (bf16[512,1024]{1,0:T(8,128)(2,1)S(1)}, bf16[512,1024]{1,0:T(8,128)(2,1)S(1)}, f32[128,1024]{1,0:T(8,128)S(1)}, f32[512,512]{1,0:T(8,128)S(1)}, f32[512,512]{1,0:T(8,128)S(1)}) custom-call(s32[4]{0:T(128)S(1)} %get-tuple-element.46.refs_0_, s32[4,4]{1,0:T(4,128)S(1)} %copy-done.1, s32[4]{0:T(128)S(1)} %copy-done.2, ...), custom_call_target="tpu_custom_call" | custom-call | bytes 3145728 | tf_op jit(solution)/shard_map/pallas_call | solution.py:51
  21.0 3.5 %collective-permute-start.7 = (f32[128,1024]{1,0:T(8,128)S(1)}, f32[128,1024]{1,0:T(8,128)S(1)}, u32[]{:S(2)}, u32[]{:S(2)}) collective-permute-start(f32[128,1024]{1,0:T(8,128)S(1)} %get-tuple-element.31), channel_id=1, source_target_pairs={{1,2},{2,1},{3,4},{4,3},{5,6},{6,5},{9,10},{10,9},{11,12},{12,11},... | collective-permute-start | bytes 1572872 | tf_op jit(solution)/shard_map/ppermute | solution.py:27
  24.5 2.2 %collective-permute-done.4.refs_4_ = f32[128,1024]{1,0:T(8,128)S(1)} collective-permute-done((f32[128,1024]{1,0:T(8,128)S(1)}, f32[128,1024]{1,0:T(8,128)S(1)}, u32[]{:S(2)}, u32[]{:S(2)}) %collective-permute-start.4) | collective-permute-done | bytes 524320 | tf_op jit(solution)/shard_map/ppermute | solution.py:27
  26.7 3.5 %collective-permute-done.5.refs_5_ = f32[128,1024]{1,0:T(8,128)S(1)} collective-permute-done((f32[128,1024]{1,0:T(8,128)S(1)}, f32[128,1024]{1,0:T(8,128)S(1)}, u32[]{:S(2)}, u32[]{:S(2)}) %collective-permute-start.5) | collective-permute-done | bytes 524320 | tf_op jit(solution)/shard_map/ppermute | solution.py:27
  30.2 8.0 %shard_map.97.refs_9_ = f32[512,1024]{1,0:T(8,128)S(1)} custom-call(f32[1]{0:T(128)} %bitcast.12.refs_0_, bf16[512,1024]{1,0:T(8,128)(2,1)S(1)} %get-tuple-element.25.refs_1_.refs_7_.refs_0_, bf16[512,1024]{1,0:T(8,128)(2,1)S(1)} %get-tuple-element.26.refs_2_.refs_8_.refs_1_, f32[1024,1024]{1,0:T(8,128)S(1)} %bitcast.16, ...), custom_call_target="tpu_custom_call" | custom-call | flops 6039797760 | bytes 14680064 | tf_op jit(solution)/shard_map/pallas_call | solution.py:51
  38.2 1.5 %collective-permute-done.7.refs_13_ = f32[128,1024]{1,0:T(8,128)S(1)} collective-permute-done((f32[128,1024]{1,0:T(8,128)S(1)}, f32[128,1024]{1,0:T(8,128)S(1)}, u32[]{:S(2)}, u32[]{:S(2)}) %collective-permute-start.7) | collective-permute-done | bytes 524320 | tf_op jit(solution)/shard_map/ppermute | solution.py:27
  39.7 3.3 %shard_map.98 = (f32[512,512]{1,0:T(8,128)S(1)}, f32[512,512]{1,0:T(8,128)S(1)}, f32[512,512]{1,0:T(8,128)S(1)}, f32[512,512]{1,0:T(8,128)S(1)}, f32[128,512]{1,...) custom-call(f32[1]{0:T(128)} %bitcast.12.refs_0_, ...), custom_call_target="tpu_custom_call" | custom-call | flops 1207959552 | bytes 16777216 | tf_op jit(solution)/shard_map/pallas_call | solution.py:51
  43.0 0.6 collective-permute-start.10
  43.6 3.3 %collective-permute-start.12 = (f32[128,512]{1,0:T(8,128)S(1)}, f32[128,512]{1,0:T(8,128)S(1)}, u32[]{:S(2)}, u32[]{:S(2)}) collective-permute-start(f32[128,512]{1,0:T(8,128)S(1)} %get-tuple-element.40), channel_id=1, source_target_pairs={{2,4},{3,5},{4,2},{5,3},{10,12},{11,13},{12,10},{13,11},{18,20},{1... | collective-permute-start | bytes 786440 | tf_op jit(solution)/shard_map/ppermute | solution.py:27
  46.9 3.5 %collective-permute-start.13 = (f32[128,512]{1,0:T(8,128)S(1)}, f32[128,512]{1,0:T(8,128)S(1)}, u32[]{:S(2)}, u32[]{:S(2)}) collective-permute-start(f32[128,512]{1,0:T(8,128)S(1)} %get-tuple-element.41), channel_id=1, source_target_pairs={{1,2},{2,1},{3,4},{4,3},{5,6},{6,5},{9,10},{10,9},{11,12},{12,11},... | collective-permute-start | bytes 786440 | tf_op jit(solution)/shard_map/ppermute | solution.py:27
  50.4 1.4 %shard_map.99 = (f32[512,512]{1,0:T(8,128)S(1)}, f32[512,1024]{1,0:T(8,128)}) custom-call(bf16[512,1024]{1,0:T(8,128)(2,1)S(1)} %get-tuple-element.25.refs_1_.refs_7_.refs_0_, bf16[512,1024]{1,0:T(8,128)(2,1)S(1)} %get-tuple-element.26.refs_2_.refs_8_.refs_1_, f32[512,512]{1,0:T(8,128)S(1)} %get-tuple-element.32.refs_2_, ...), custom_call_target="tpu_custom_call" | custom-call | flops 805306368 | bytes 7340032 | tf_op jit(solution)/shard_map/pallas_call | solution.py:51
  51.8 5.5 %collective-permute-done.9.refs_2_.refs_5_ = f32[512,512]{1,0:T(8,128)S(1)} collective-permute-done((f32[512,512]{1,0:T(8,128)S(1)}, f32[512,512]{1,0:T(8,128)S(1)}, u32[]{:S(2)}, u32[]{:S(2)}) %collective-permute-start.9) | collective-permute-done | bytes 1048608 | tf_op jit(solution)/shard_map/ppermute | solution.py:32
  57.2 0.6 shard_map.101
  57.9 3.0 %collective-permute-done.13.refs_6_ = f32[128,512]{1,0:T(8,128)S(1)} collective-permute-done((f32[128,512]{1,0:T(8,128)S(1)}, f32[128,512]{1,0:T(8,128)S(1)}, u32[]{:S(2)}, u32[]{:S(2)}) %collective-permute-start.13) | collective-permute-done | bytes 262176 | tf_op jit(solution)/shard_map/ppermute | solution.py:27
  61.0 1.0 %shard_map.102 = f32[512,512]{1,0:T(8,128)S(1)} custom-call(bf16[512,1024]{1,0:T(8,128)(2,1)S(1)} %get-tuple-element.25.refs_1_.refs_7_.refs_0_, bf16[512,1024]{1,0:T(8,128)(2,1)S(1)} %get-tuple-element.26.refs_2_.refs_8_.refs_1_, f32[512,512]{1,0:T(8,128)S(1)} %get-tuple-element.37.refs_2_, f32[128,512]{1,0:T(8,128)S(1)} %collective-permute-done.10.refs_3_, ...), custom_call_target="tpu_custom_call" | custom-call | flops 805306368 | bytes 2097152 | tf_op jit(solution)/shard_map/pallas_call | solution.py:51
  62.0 0.2 collective-permute-start.14
  62.2 3.8 %collective-permute-start.17 = (f32[128,512]{1,0:T(8,128)S(1)}, f32[128,512]{1,0:T(8,128)S(1)}, u32[]{:S(2)}, u32[]{:S(2)}) collective-permute-start(f32[128,512]{1,0:T(8,128)S(1)} %get-tuple-element.44), channel_id=1, source_target_pairs={{2,4},{3,5},{4,2},{5,3},{10,12},{11,13},{12,10},{13,11},{18,20},{1... | collective-permute-start | bytes 786440 | tf_op jit(solution)/shard_map/ppermute | solution.py:27
  66.0 3.6 %collective-permute-start.18 = (f32[128,512]{1,0:T(8,128)S(1)}, f32[128,512]{1,0:T(8,128)S(1)}, u32[]{:S(2)}, u32[]{:S(2)}) collective-permute-start(f32[128,512]{1,0:T(8,128)S(1)} %get-tuple-element.45), channel_id=1, source_target_pairs={{1,2},{2,1},{3,4},{4,3},{5,6},{6,5},{9,10},{10,9},{11,12},{12,11},... | collective-permute-start | bytes 786440 | tf_op jit(solution)/shard_map/ppermute | solution.py:27
  69.6 1.0 %shard_map.100.refs_3_ = f32[512,512]{1,0:T(8,128)S(1)} custom-call(bf16[512,1024]{1,0:T(8,128)(2,1)S(1)} %get-tuple-element.25.refs_1_.refs_7_.refs_0_, bf16[512,1024]{1,0:T(8,128)(2,1)S(1)} %get-tuple-element.26.refs_2_.refs_8_.refs_1_, f32[512,512]{1,0:T(8,128)S(1)} %collective-permute-done.9.refs_2_.refs_5_, ...), custom_call_target="tpu_custom_call" | custom-call | flops 805306368 | bytes 3145728 | tf_op jit(solution)/shard_map/pallas_call | solution.py:51
  70.6 0.6 collective-permute-done.15.refs_6_
  71.2 0.1 collective-permute-done.16.refs_7_
  71.3 1.9 %collective-permute-done.17.refs_8_ = f32[128,512]{1,0:T(8,128)S(1)} collective-permute-done((f32[128,512]{1,0:T(8,128)S(1)}, f32[128,512]{1,0:T(8,128)S(1)}, u32[]{:S(2)}, u32[]{:S(2)}) %collective-permute-start.17) | collective-permute-done | bytes 262176 | tf_op jit(solution)/shard_map/ppermute | solution.py:27
  73.2 6.9 %collective-permute-done.18.refs_9_ = f32[128,512]{1,0:T(8,128)S(1)} collective-permute-done((f32[128,512]{1,0:T(8,128)S(1)}, f32[128,512]{1,0:T(8,128)S(1)}, u32[]{:S(2)}, u32[]{:S(2)}) %collective-permute-start.18) | collective-permute-done | bytes 262176 | tf_op jit(solution)/shard_map/ppermute | solution.py:27
  80.1 5.5 %shard_map.103 = f32[512,1024]{1,0:T(8,128)} custom-call(f32[1]{0:T(128)} %bitcast.12.refs_0_, bf16[512,1024]{1,0:T(8,128)(2,1)S(1)} %get-tuple-element.25.refs_1_.refs_7_.refs_0_, bf16[512,1024]{1,0:T(8,128)(2,1)S(1)} %get-tuple-element.26.refs_2_.refs_8_.refs_1_, f32[512,512]{1,0:T(8,128)S(1)} %shard_map.100.refs_3_, ...), custom_call_target="tpu_custom_call" | custom-call | flops 4026531840 | bytes 10485760 | tf_op jit(solution)/shard_map/pallas_call | solution.py:51
  (22 shorter events, 0.3 us)
Async XLA Ops:
  0.6 16.7 %copy-start.1 = (s32[4,4]{1,0:T(4,128)S(1)}, s32[4,4]{1,0:T(4,128)}, u32[]{:S(2)}) copy-start(s32[4,4]{1,0:T(4,128)} %refs_1_.1) | copy-start | bytes 196
  0.6 16.7 %copy-start.2 = (s32[4]{0:T(128)S(1)}, s32[4]{0:T(128)}, u32[]{:S(2)}) copy-start(s32[4]{0:T(128)} %refs_2_.1) | copy-start | bytes 52
  0.7 8.1 %collective-permute-start = (s32[4]{0:T(128)}, s32[4]{0:T(128)S(1)}, u32[]{:S(2)}, u32[]{:S(2)}) collective-permute-start(s32[4]{0:T(128)} %bitcast.25), channel_id=1, source_target_pairs={{1,2},{2,1},{3,4},{4,3},{5,6},{6,5},{9,10},{10,9},{11,12},{12,11},... | collective-permute-start | bytes 56 | tf_op jit(solution)/shard_map/ppermute | solution.py:27
  4.1 4.7 %collective-permute-start.1 = (s32[4]{0:T(128)}, s32[4]{0:T(128)S(1)}, u32[]{:S(2)}, u32[]{:S(2)}) collective-permute-start(s32[4]{0:T(128)} %bitcast.26), channel_id=1, source_target_pairs={{0,1},{1,0},{2,3},{3,2},{4,5},{5,4},{6,7},{7,6},{8,9},{9,8},{10,11... | collective-permute-start | bytes 56 | tf_op jit(solution)/shard_map/ppermute | solution.py:27
  5.8 3.7 %collective-permute-start.2 = (s32[4]{0:T(128)}, s32[4]{0:T(128)S(1)}, u32[]{:S(2)}, u32[]{:S(2)}) collective-permute-start(s32[4]{0:T(128)} %bitcast.27), channel_id=1, source_target_pairs={{0,2},{1,3},{2,0},{3,1},{4,6},{5,7},{6,4},{7,5},{8,10},{9,11},{10,... | collective-permute-start | bytes 56 | tf_op jit(solution)/shard_map/ppermute | solution.py:27
  5.8 5.6 %collective-permute-start.3 = (s32[4]{0:T(128)}, s32[4]{0:T(128)S(1)}, u32[]{:S(2)}, u32[]{:S(2)}) collective-permute-start(s32[4]{0:T(128)} %bitcast.28), channel_id=1, source_target_pairs={{2,4},{3,5},{4,2},{5,3},{10,12},{11,13},{12,10},{13,11},{18,20},{1... | collective-permute-start | bytes 56 | tf_op jit(solution)/shard_map/ppermute | solution.py:27
  13.3 13.3 %collective-permute-start.4 = (f32[128,1024]{1,0:T(8,128)S(1)}, f32[128,1024]{1,0:T(8,128)S(1)}, u32[]{:S(2)}, u32[]{:S(2)}) collective-permute-start(f32[128,1024]{1,0:T(8,128)S(1)} %get-tuple-element.24.refs_10_), channel_id=1, source_target_pairs={{0,1},{1,0},{2,3},{3,2},{4,5},{5,4},{6,7},{7,6},{8,9},{9,8},{10,11... | collective-permute-start | bytes 1572872 | tf_op jit(solution)/shard_map/ppermute | solution.py:27
  15.4 14.9 %collective-permute-start.5 = (f32[128,1024]{1,0:T(8,128)S(1)}, f32[128,1024]{1,0:T(8,128)S(1)}, u32[]{:S(2)}, u32[]{:S(2)}) collective-permute-start(f32[128,1024]{1,0:T(8,128)S(1)} %get-tuple-element.27), channel_id=1, source_target_pairs={{0,2},{1,3},{2,0},{3,1},{4,6},{5,7},{6,4},{7,5},{8,10},{9,11},{10,... | collective-permute-start | bytes 1572872 | tf_op jit(solution)/shard_map/ppermute | solution.py:27
  15.4 14.9 %collective-permute-start.6 = (f32[128,1024]{1,0:T(8,128)S(1)}, f32[128,1024]{1,0:T(8,128)S(1)}, u32[]{:S(2)}, u32[]{:S(2)}) collective-permute-start(f32[128,1024]{1,0:T(8,128)S(1)} %get-tuple-element.28), channel_id=1, source_target_pairs={{2,4},{3,5},{4,2},{5,3},{10,12},{11,13},{12,10},{13,11},{18,20},{1... | collective-permute-start | bytes 1572872 | tf_op jit(solution)/shard_map/ppermute | solution.py:27
  17.4 12.8 %copy-start = (f32[1,1024,1024]{2,1,0:T(8,128)S(1)}, f32[1,1024,1024]{2,1,0:T(8,128)}, u32[]{:S(2)}) copy-start(f32[1,1024,1024]{2,1,0:T(8,128)} %param.11) | copy-start | bytes 12582916
  21.0 18.7 %collective-permute-start.7 = (f32[128,1024]{1,0:T(8,128)S(1)}, f32[128,1024]{1,0:T(8,128)S(1)}, u32[]{:S(2)}, u32[]{:S(2)}) collective-permute-start(f32[128,1024]{1,0:T(8,128)S(1)} %get-tuple-element.31), channel_id=1, source_target_pairs={{1,2},{2,1},{3,4},{4,3},{5,6},{6,5},{9,10},{10,9},{11,12},{12,11},... | collective-permute-start | bytes 1572872 | tf_op jit(solution)/shard_map/ppermute | solution.py:27
  24.5 22.5 %collective-permute-start.8 = (f32[512,512]{1,0:T(8,128)S(1)}, f32[512,512]{1,0:T(8,128)S(1)}, u32[]{:S(2)}, u32[]{:S(2)}) collective-permute-start(f32[512,512]{1,0:T(8,128)S(1)} %get-tuple-element.29.refs_11_), channel_id=1, source_target_pairs={{0,8},{8,16},{16,24},{24,0},{1,9},{9,17},{17,25},{25,1},{2,10},{10... | collective-permute-start | bytes 3145736 | tf_op jit(solution)/shard_map/ppermute | solution.py:32
  43.0 14.3 %collective-permute-start.9 = (f32[512,512]{1,0:T(8,128)S(1)}, f32[512,512]{1,0:T(8,128)S(1)}, u32[]{:S(2)}, u32[]{:S(2)}) collective-permute-start(f32[512,512]{1,0:T(8,128)S(1)} %get-tuple-element.36), channel_id=1, source_target_pairs={{0,8},{8,16},{16,24},{24,0},{1,9},{9,17},{17,25},{25,1},{2,10},{10... | collective-permute-start | bytes 3145736 | tf_op jit(solution)/shard_map/ppermute | solution.py:32
  43.0 14.9 %collective-permute-start.10 = (f32[128,512]{1,0:T(8,128)S(1)}, f32[128,512]{1,0:T(8,128)S(1)}, u32[]{:S(2)}, u32[]{:S(2)}) collective-permute-start(f32[128,512]{1,0:T(8,128)S(1)} %get-tuple-element.38), channel_id=1, source_target_pairs={{0,1},{1,0},{2,3},{3,2},{4,5},{5,4},{6,7},{7,6},{8,9},{9,8},{10,11... | collective-permute-start | bytes 786440 | tf_op jit(solution)/shard_map/ppermute | solution.py:27
  43.6 14.3 %collective-permute-start.11 = (f32[128,512]{1,0:T(8,128)S(1)}, f32[128,512]{1,0:T(8,128)S(1)}, u32[]{:S(2)}, u32[]{:S(2)}) collective-permute-start(f32[128,512]{1,0:T(8,128)S(1)} %get-tuple-element.39), channel_id=1, source_target_pairs={{0,2},{1,3},{2,0},{3,1},{4,6},{5,7},{6,4},{7,5},{8,10},{9,11},{10,... | collective-permute-start | bytes 786440 | tf_op jit(solution)/shard_map/ppermute | solution.py:27
  43.6 14.3 %collective-permute-start.12 = (f32[128,512]{1,0:T(8,128)S(1)}, f32[128,512]{1,0:T(8,128)S(1)}, u32[]{:S(2)}, u32[]{:S(2)}) collective-permute-start(f32[128,512]{1,0:T(8,128)S(1)} %get-tuple-element.40), channel_id=1, source_target_pairs={{2,4},{3,5},{4,2},{5,3},{10,12},{11,13},{12,10},{13,11},{18,20},{1... | collective-permute-start | bytes 786440 | tf_op jit(solution)/shard_map/ppermute | solution.py:27
  46.9 14.0 %collective-permute-start.13 = (f32[128,512]{1,0:T(8,128)S(1)}, f32[128,512]{1,0:T(8,128)S(1)}, u32[]{:S(2)}, u32[]{:S(2)}) collective-permute-start(f32[128,512]{1,0:T(8,128)S(1)} %get-tuple-element.41), channel_id=1, source_target_pairs={{1,2},{2,1},{3,4},{4,3},{5,6},{6,5},{9,10},{10,9},{11,12},{12,11},... | collective-permute-start | bytes 786440 | tf_op jit(solution)/shard_map/ppermute | solution.py:27
  62.0 18.2 %collective-permute-start.14 = (f32[512,512]{1,0:T(8,128)S(1)}, f32[512,512]{1,0:T(8,128)S(1)}, u32[]{:S(2)}, u32[]{:S(2)}) collective-permute-start(f32[512,512]{1,0:T(8,128)S(1)} %shard_map.102), channel_id=1, source_target_pairs={{0,8},{8,16},{16,24},{24,0},{1,9},{9,17},{17,25},{25,1},{2,10},{10... | collective-permute-start | bytes 3145736 | tf_op jit(solution)/shard_map/ppermute | solution.py:32
  62.1 9.0 %collective-permute-start.15 = (f32[128,512]{1,0:T(8,128)S(1)}, f32[128,512]{1,0:T(8,128)S(1)}, u32[]{:S(2)}, u32[]{:S(2)}) collective-permute-start(f32[128,512]{1,0:T(8,128)S(1)} %get-tuple-element.42.refs_7_), channel_id=1, source_target_pairs={{0,1},{1,0},{2,3},{3,2},{4,5},{5,4},{6,7},{7,6},{8,9},{9,8},{10,11... | collective-permute-start | bytes 786440 | tf_op jit(solution)/shard_map/ppermute | solution.py:27
  62.1 9.1 %collective-permute-start.16 = (f32[128,512]{1,0:T(8,128)S(1)}, f32[128,512]{1,0:T(8,128)S(1)}, u32[]{:S(2)}, u32[]{:S(2)}) collective-permute-start(f32[128,512]{1,0:T(8,128)S(1)} %get-tuple-element.43), channel_id=1, source_target_pairs={{0,2},{1,3},{2,0},{3,1},{4,6},{5,7},{6,4},{7,5},{8,10},{9,11},{10,... | collective-permute-start | bytes 786440 | tf_op jit(solution)/shard_map/ppermute | solution.py:27
  62.2 11.0 %collective-permute-start.17 = (f32[128,512]{1,0:T(8,128)S(1)}, f32[128,512]{1,0:T(8,128)S(1)}, u32[]{:S(2)}, u32[]{:S(2)}) collective-permute-start(f32[128,512]{1,0:T(8,128)S(1)} %get-tuple-element.44), channel_id=1, source_target_pairs={{2,4},{3,5},{4,2},{5,3},{10,12},{11,13},{12,10},{13,11},{18,20},{1... | collective-permute-start | bytes 786440 | tf_op jit(solution)/shard_map/ppermute | solution.py:27
  66.0 14.1 %collective-permute-start.18 = (f32[128,512]{1,0:T(8,128)S(1)}, f32[128,512]{1,0:T(8,128)S(1)}, u32[]{:S(2)}, u32[]{:S(2)}) collective-permute-start(f32[128,512]{1,0:T(8,128)S(1)} %get-tuple-element.45), channel_id=1, source_target_pairs={{1,2},{2,1},{3,4},{4,3},{5,6},{6,5},{9,10},{10,9},{11,12},{12,11},... | collective-permute-start | bytes 786440 | tf_op jit(solution)/shard_map/ppermute | solution.py:27

commit v4 on v3

--- a/solution.py
+++ b/solution.py
@@ -171,34 +171,46 @@
     return jnp.concatenate([ref[...] for ref in refs], axis=0)
 
 
-def early_kernel(beta_ref, high_ref, low_ref, weight_ref, *refs):
-    came, sources, out_ref, refs = refs[:-6], refs[-6:-4], refs[-4], refs[-3:]
-    held, sem = refs[:2], refs[2]
-    feats_ref, first_ref = held
+def mix_kernel(high_ref, low_ref, *refs):
+    sources, out_ref, held, sem = refs[:2], refs[2], refs[3:5], refs[5]
     copies = [pltpu.make_async_copy(s, h, sem.at[i]) for i, (s, h) in enumerate(zip(sources, held))]
     for copy in copies:
         copy.start()
-    rows = feats_ref.shape[0]
-    mixed = times_adj(high_ref, low_ref, rows, stacked(came))
-    copies[0].wait()
-    mixed = mixed + times_adj(high_ref, low_ref, 0, feats_ref[...])
-    copies[1].wait()
-    mixed = mixed + 0.1 * first_ref[...]
+    for copy in copies:
+        copy.wait()
+    out_ref[...] = times_adj(high_ref, low_ref, 0, held[0][...]) + 0.1 * held[1][...]
+
+
+def own_first(adj, feats, first):
+    rows, width = feats.shape
+    return call(
+        mix_kernel,
+        (*adj, in_hbm(feats), in_hbm(first)),
+        [VMEM] * 2 + [HBM] * 2,
+        (vmem(rows, width),),
+        flops=6 * rows * rows * width,
+        nbytes=12 * rows * width,
+        scratch=[pltpu.VMEM(feats.shape, F32)] * 2 + [ONE((2,))],
+    )[0]
+
+
+def early_kernel(beta_ref, high_ref, low_ref, weight_ref, base_ref, *refs):
+    came, out_ref = refs[:-1], refs[-1]
+    rows = base_ref.shape[0]
+    mixed = base_ref[...] + times_adj(high_ref, low_ref, rows, stacked(came))
     beta = beta_ref[0]
     out_ref[...] = (1.0 - beta) * mixed + beta * dot3(halves(mixed), halves(weight_ref[...]))
 
 
-def early(beta, adj, weight, came, feats, first):
-    rows, width = feats.shape
-    arrays = (feats, first)
+def early(beta, adj, weight, base, came):
+    rows, width = base.shape
     return call(
         early_kernel,
-        (beta, *adj, weight, *came, *[in_hbm(v) for v in arrays]),
-        [SMEM] + [VMEM] * (3 + len(came)) + [HBM] * 2,
+        (beta, *adj, weight, base, *came),
+        [SMEM] + [VMEM] * (4 + len(came)),
         (vmem(rows, width),),
-        flops=6 * rows * width * (width + rows + len(came) * BLK),
-        nbytes=4 * (width * width + 5 * rows * width),
-        scratch=[pltpu.VMEM(v.shape, F32) for v in arrays] + [ONE((len(arrays),))],
+        flops=6 * rows * width * (width + len(came) * BLK),
+        nbytes=4 * (width * width + 2 * rows * width),
     )[0]
 
 
@@ -300,19 +312,41 @@
     )[0]
 
 
-def second_kernel(beta_ref, high_ref, low_ref, left_ref, right_ref, weight_ref, *refs, tile):
+def term_kernel(beta_ref, right_ref, weight_ref, out_ref):
+    half = right_ref.shape[1]
+    right = right_ref[...]
+    beta = beta_ref[0]
+    term = beta * dot3(halves(right), halves(weight_ref[half:, :]))
+    out_ref[:, :half] = term[:, :half]
+    out_ref[:, half:] = term[:, half:] + (1.0 - beta) * right
+
+
+def right_term(beta, right, weight):
+    rows, half = right.shape
+    width = weight.shape[1]
+    return call(
+        term_kernel,
+        (beta, right, weight),
+        [SMEM] + [VMEM] * 2,
+        (vmem(rows, width),),
+        flops=6 * rows * half * width,
+        nbytes=4 * (half * width + 2 * rows * width),
+    )[0]
+
+
+def second_kernel(beta_ref, high_ref, low_ref, left_ref, term_ref, weight_ref, *refs, tile):
     came, (out_ref, held, sem) = refs[:-3], refs[-3:]
     rows, half = left_ref.shape
     width = weight_ref.shape[1]
     left = left_ref[...] + times_adj(high_ref, low_ref, rows, stacked(came))
-    mixed = (left, right_ref[...])
-    pair = halves(jnp.concatenate(mixed, axis=1))
+    pair = halves(left)
     beta = beta_ref[0]
     copies = []
     for i, at in enumerate(range(0, width, tile)):
         cut = slice(at, at + tile)
-        own = mixed[at // half][:, at % half : at % half + tile]
-        value = (1.0 - beta) * own + beta * dot3(pair, halves(weight_ref[:, cut]))
+        value = term_ref[:, cut] + beta * dot3(pair, halves(weight_ref[:half, cut]))
+        if at < half:
+            value = value + (1.0 - beta) * left[:, cut]
         held[:, cut] = jnp.maximum(value, 0.0)
         copies.append(pltpu.make_async_copy(held.at[:, cut], out_ref.at[:, cut], sem.at[i]))
         copies[-1].start()
@@ -320,18 +354,17 @@
         copy.wait()
 
 
-def second_layer(beta, adj, left, right, weight, came, tile=256):
+def second_layer(beta, adj, left, term, weight, came, tile=256):
     rows, half = left.shape
     width = weight.shape[1]
     return call(
         functools.partial(second_kernel, tile=tile),
-        (beta, *adj, left, right, weight, *came),
+        (beta, *adj, left, term, weight, *came),
         [SMEM] + [VMEM] * (5 + len(came)),
         (pltpu.HBM((rows, width), F32),),
-        flops=6 * rows * width * (width + len(came) * BLK // 2),
-        nbytes=4 * (width * width + 3 * rows * width),
+        flops=6 * rows * half * (width + len(came) * BLK),
+        nbytes=4 * (half * width + 3 * rows * width),
         scratch=[pltpu.VMEM((rows, width), F32), ONE((width // tile,))],
-        vmem=16,
     )[0]
 
 
@@ -369,7 +402,7 @@
     )
     crossing = swap(sent, *SWAPS[final])
     handed_left = hand_on(first_left)
-    known = early(beta, adj, weight, came, feats, first)
+    known = early(beta, adj, weight, own_first(adj, feats, first), came)
     out_left, out_right, left, right, *sent = late(
         every, beta, last, index, got, adj, known, weight, (first_left, first_right), crossing
     )
@@ -381,7 +414,7 @@
     right = hand_on(add_received(adj, mixed, came, after=sent[:1]))
     came = [swap(value, *kind) for value, kind in zip(sent, SWAPS)]
     mixed = own_left(adj, left, handed_left)
-    second_out = second_layer(beta, adj, mixed, right, weight, came)
+    second_out = second_layer(beta, adj, mixed, right_term(beta, right, weight), weight, came)
     return first_out[None], second_out[None]
 
 

time: 86.2 us -> 84.6 us (0.981)
  waiting for transfers between devices: 27.8 us -> 24.7 us
  Pallas kernels: 26.2 us -> 27.6 us
    ppermute x16, waiting for transfers between devices: 22.4 us -> 13.7 us  [swap(): return lax.ppermute(value, 'graph', sorted(pairs))]
    ppermute x3, waiting for transfers between devices: 5.46 us -> 11.1 us  [hand_on(): lax.ppermute(value, 'segment', [(i, (i + 1) % peers) for i in range(peers)])]
    pallas_call x9 -> x11, Pallas kernels: 26.2 us -> 27.6 us  [call(): pl.pallas_call(body, out_shape=outs, in_specs=list(in_specs) + [VMEM] * l...]
  transfers between devices with their start and end apart: 19 -> 19, of which waited for: 11 -> 8; matrix products, arithmetic and copies ran while one was open for 0% -> 0% of each run, Pallas kernels for 21% -> 25%
where the time goes in v4:
time: 84.6 us; the launch traced here: 84.1 us
  starting transfers between devices  30.4 us (36%)
  Pallas kernels  27.6 us (33%)
  waiting for transfers between devices  24.7 us (29%)
  between operations  1.25 us (1%)
    ppermute x16, starting transfers between devices, swap(): return lax.ppermute(value, 'graph', sorted(pairs))  30.1 us
    pallas_call x11, Pallas kernels, call(): pl.pallas_call(body, out_shape=outs, in_specs=list(in_specs) + [VMEM] * l...  27.6 us
    ppermute x16, waiting for transfers between devices, swap(): return lax.ppermute(value, 'graph', sorted(pairs))  13.7 us
    ppermute x3, waiting for transfers between devices, hand_on(): lax.ppermute(value, 'segment', [(i, (i + 1) % peers) for i in range(peers)])  11.1 us
  transfers between devices with their start and end apart: 19, of which 8 were waited for; matrix products, arithmetic and copies ran while one was open for 0% of the time, Pallas kernels for 25%

profile of v4, /device:TPU:16, one launch (start us, length us, event | category | flops | bytes accessed | tf_op | source)
XLA Modules:
  0.0 84.1 jit_solution(9347288286924191001)
XLA Ops:
  0.7 3.4 %collective-permute-start = (s32[4]{0:T(128)}, s32[4]{0:T(128)S(1)}, u32[]{:S(2)}, u32[]{:S(2)}) collective-permute-start(s32[4]{0:T(128)} %bitcast.27), channel_id=1, source_target_pairs={{1,2},{2,1},{3,4},{4,3},{5,6},{6,5},{9,10},{10,9},{11,12},{12,11},... | collective-permute-start | bytes 56 | tf_op jit(solution)/shard_map/ppermute | solution.py:27
  4.1 1.7 %collective-permute-start.1 = (s32[4]{0:T(128)}, s32[4]{0:T(128)S(1)}, u32[]{:S(2)}, u32[]{:S(2)}) collective-permute-start(s32[4]{0:T(128)} %bitcast.28), channel_id=1, source_target_pairs={{0,1},{1,0},{2,3},{3,2},{4,5},{5,4},{6,7},{7,6},{8,9},{9,8},{10,11... | collective-permute-start | bytes 56 | tf_op jit(solution)/shard_map/ppermute | solution.py:27
  5.8 2.8 %collective-permute-start.3 = (s32[4]{0:T(128)}, s32[4]{0:T(128)S(1)}, u32[]{:S(2)}, u32[]{:S(2)}) collective-permute-start(s32[4]{0:T(128)} %bitcast.30), channel_id=1, source_target_pairs={{2,4},{3,5},{4,2},{5,3},{10,12},{11,13},{12,10},{13,11},{18,20},{1... | collective-permute-start | bytes 56 | tf_op jit(solution)/shard_map/ppermute | solution.py:27
  8.7 0.1 pad_add_fusion
  8.8 0.7 collective-permute-done.2.refs_2_.refs_4_
  9.5 1.9 %collective-permute-done.3.refs_3_.refs_5_ = s32[4]{0:T(128)S(1)} collective-permute-done((s32[4]{0:T(128)}, s32[4]{0:T(128)S(1)}, u32[]{:S(2)}, u32[]{:S(2)}) %collective-permute-start.3) | collective-permute-done | bytes 48 | tf_op jit(solution)/shard_map/ppermute | solution.py:27
  11.4 2.0 %shard_map.95 = (f32[128,1024]{1,0:T(8,128)S(1)}, f32[128,1024]{1,0:T(8,128)S(1)}, f32[128,1024]{1,0:T(8,128)S(1)}) custom-call(s32[4]{0:T(128)S(1)} %get-tuple-element.47.refs_0_.refs_3_.refs_2_, s32[4]{0:T(128)S(1)} %collective-permute-done.1.refs_1_.refs_3_, s32[4]{0:T(128)S(1)} %collective-permute-done.2.refs_2_.refs_4_, ...), custom_call_target="tpu_custom_call" | custom-call | bytes 3145728 | tf_op jit(solution)/shard_map/pallas_call | solution.py:51
  13.3 2.0 %collective-permute-start.4 = (f32[128,1024]{1,0:T(8,128)S(1)}, f32[128,1024]{1,0:T(8,128)S(1)}, u32[]{:S(2)}, u32[]{:S(2)}) collective-permute-start(f32[128,1024]{1,0:T(8,128)S(1)} %get-tuple-element.24.refs_10_), channel_id=1, source_target_pairs={{0,1},{1,0},{2,3},{3,2},{4,5},{5,4},{6,7},{7,6},{8,9},{9,8},{10,11... | collective-permute-start | bytes 1572872 | tf_op jit(solution)/shard_map/ppermute | solution.py:27
  15.4 1.9 %collective-permute-start.6 = (f32[128,1024]{1,0:T(8,128)S(1)}, f32[128,1024]{1,0:T(8,128)S(1)}, u32[]{:S(2)}, u32[]{:S(2)}) collective-permute-start(f32[128,1024]{1,0:T(8,128)S(1)} %get-tuple-element.28), channel_id=1, source_target_pairs={{2,4},{3,5},{4,2},{5,3},{10,12},{11,13},{12,10},{13,11},{18,20},{1... | collective-permute-start | bytes 1572872 | tf_op jit(solution)/shard_map/ppermute | solution.py:27
  17.4 3.3 %shard_map.96 = (bf16[512,1024]{1,0:T(8,128)(2,1)S(1)}, bf16[512,1024]{1,0:T(8,128)(2,1)S(1)}, f32[128,1024]{1,0:T(8,128)S(1)}, f32[512,512]{1,0:T(8,128)S(1)}, f32[512,512]{1,0:T(8,128)S(1)}) custom-call(s32[4]{0:T(128)S(1)} %get-tuple-element.46.refs_0_, s32[4,4]{1,0:T(4,128)S(1)} %copy-done.1, s32[4]{0:T(128)S(1)} %copy-done.2, ...), custom_call_target="tpu_custom_call" | custom-call | bytes 3145728 | tf_op jit(solution)/shard_map/pallas_call | solution.py:51
  20.7 3.5 %collective-permute-start.7 = (f32[128,1024]{1,0:T(8,128)S(1)}, f32[128,1024]{1,0:T(8,128)S(1)}, u32[]{:S(2)}, u32[]{:S(2)}) collective-permute-start(f32[128,1024]{1,0:T(8,128)S(1)} %get-tuple-element.31), channel_id=1, source_target_pairs={{1,2},{2,1},{3,4},{4,3},{5,6},{6,5},{9,10},{10,9},{11,12},{12,11},... | collective-permute-start | bytes 1572872 | tf_op jit(solution)/shard_map/ppermute | solution.py:27
  24.2 4.2 %shard_map.97.refs_4_ = f32[512,1024]{1,0:T(8,128)S(1)} custom-call(bf16[512,1024]{1,0:T(8,128)(2,1)S(1)} %get-tuple-element.25.refs_0_.refs_1_.refs_7_, bf16[512,1024]{1,0:T(8,128)(2,1)S(1)} %get-tuple-element.26.refs_1_.refs_2_.refs_8_, f32[512,1024]{1,0:T(8,128)} %bitcast.22, f32[512,1024]{1,0:T(8,128)} %bitcast.24), custom_call_target="tpu_custom_call" | custom-call | flops 1610612736 | bytes 6291456 | tf_op jit(solution)/shard_map/pallas_call | solution.py:51
  28.5 1.7 %collective-permute-done.5.refs_6_ = f32[128,1024]{1,0:T(8,128)S(1)} collective-permute-done((f32[128,1024]{1,0:T(8,128)S(1)}, f32[128,1024]{1,0:T(8,128)S(1)}, u32[]{:S(2)}, u32[]{:S(2)}) %collective-permute-start.5) | collective-permute-done | bytes 524320 | tf_op jit(solution)/shard_map/ppermute | solution.py:27
  30.2 5.2 %shard_map.98.refs_9_ = f32[512,1024]{1,0:T(8,128)S(1)} custom-call(f32[1]{0:T(128)} %bitcast.12.refs_0_, bf16[512,1024]{1,0:T(8,128)(2,1)S(1)} %get-tuple-element.25.refs_0_.refs_1_.refs_7_, bf16[512,1024]{1,0:T(8,128)(2,1)S(1)} %get-tuple-element.26.refs_1_.refs_2_.refs_8_, f32[1024,1024]{1,0:T(8,128)S(1)} %bitcast.16, f32[512,1024]{1,0:T(8,128)S(1)} %shard_map.97.refs_4_, ...), custom_call_target="tpu_custom_call" | custom-call | flops 4429185024 | bytes 8388608 | tf_op jit(solution)/shard_map/pallas_call | solution.py:51
  35.5 4.2 %collective-permute-done.7.refs_13_ = f32[128,1024]{1,0:T(8,128)S(1)} collective-permute-done((f32[128,1024]{1,0:T(8,128)S(1)}, f32[128,1024]{1,0:T(8,128)S(1)}, u32[]{:S(2)}, u32[]{:S(2)}) %collective-permute-start.7) | collective-permute-done | bytes 524320 | tf_op jit(solution)/shard_map/ppermute | solution.py:27
  39.7 3.2 %shard_map.99 = (f32[512,512]{1,0:T(8,128)S(1)}, f32[512,512]{1,0:T(8,128)S(1)}, f32[512,512]{1,0:T(8,128)S(1)}, f32[512,512]{1,0:T(8,128)S(1)}, f32[128,512]{1,...) custom-call(f32[1]{0:T(128)} %bitcast.12.refs_0_, ...), custom_call_target="tpu_custom_call" | custom-call | flops 1207959552 | bytes 16777216 | tf_op jit(solution)/shard_map/pallas_call | solution.py:51
  43.0 0.1 collective-permute-start.10
  43.1 3.7 %collective-permute-start.12 = (f32[128,512]{1,0:T(8,128)S(1)}, f32[128,512]{1,0:T(8,128)S(1)}, u32[]{:S(2)}, u32[]{:S(2)}) collective-permute-start(f32[128,512]{1,0:T(8,128)S(1)} %get-tuple-element.40), channel_id=1, source_target_pairs={{2,4},{3,5},{4,2},{5,3},{10,12},{11,13},{12,10},{13,11},{18,20},{1... | collective-permute-start | bytes 786440 | tf_op jit(solution)/shard_map/ppermute | solution.py:27
  46.9 3.5 %collective-permute-start.13 = (f32[128,512]{1,0:T(8,128)S(1)}, f32[128,512]{1,0:T(8,128)S(1)}, u32[]{:S(2)}, u32[]{:S(2)}) collective-permute-start(f32[128,512]{1,0:T(8,128)S(1)} %get-tuple-element.41), channel_id=1, source_target_pairs={{1,2},{2,1},{3,4},{4,3},{5,6},{6,5},{9,10},{10,9},{11,12},{12,11},... | collective-permute-start | bytes 786440 | tf_op jit(solution)/shard_map/ppermute | solution.py:27
  50.4 1.4 %shard_map.100 = (f32[512,512]{1,0:T(8,128)S(1)}, f32[512,1024]{1,0:T(8,128)}) custom-call(bf16[512,1024]{1,0:T(8,128)(2,1)S(1)} %get-tuple-element.25.refs_0_.refs_1_.refs_7_, bf16[512,1024]{1,0:T(8,128)(2,1)S(1)} %get-tuple-element.26.refs_1_.refs_2_.refs_8_, f32[512,512]{1,0:T(8,128)S(1)} %get-tuple-element.32.refs_2_, ...), custom_call_target="tpu_custom_call" | custom-call | flops 805306368 | bytes 7340032 | tf_op jit(solution)/shard_map/pallas_call | solution.py:51
  51.7 5.5 %collective-permute-done.9.refs_2_.refs_5_ = f32[512,512]{1,0:T(8,128)S(1)} collective-permute-done((f32[512,512]{1,0:T(8,128)S(1)}, f32[512,512]{1,0:T(8,128)S(1)}, u32[]{:S(2)}, u32[]{:S(2)}) %collective-permute-start.9) | collective-permute-done | bytes 1048608 | tf_op jit(solution)/shard_map/ppermute | solution.py:32
  57.2 0.6 shard_map.102
  57.9 3.0 %collective-permute-done.13.refs_6_ = f32[128,512]{1,0:T(8,128)S(1)} collective-permute-done((f32[128,512]{1,0:T(8,128)S(1)}, f32[128,512]{1,0:T(8,128)S(1)}, u32[]{:S(2)}, u32[]{:S(2)}) %collective-permute-start.13) | collective-permute-done | bytes 262176 | tf_op jit(solution)/shard_map/ppermute | solution.py:27
  60.9 1.0 %shard_map.103 = f32[512,512]{1,0:T(8,128)S(1)} custom-call(bf16[512,1024]{1,0:T(8,128)(2,1)S(1)} %get-tuple-element.25.refs_0_.refs_1_.refs_7_, bf16[512,1024]{1,0:T(8,128)(2,1)S(1)} %get-tuple-element.26.refs_1_.refs_2_.refs_8_, f32[512,512]{1,0:T(8,128)S(1)} %get-tuple-element.37.refs_2_, f32[128,512]{1,0:T(8,128)S(1)} %collective-permute-done.10.refs_3_, ...), custom_call_target="tpu_custom_call" | custom-call | flops 805306368 | bytes 2097152 | tf_op jit(solution)/shard_map/pallas_call | solution.py:51
  61.9 0.2 collective-permute-start.14
  62.1 3.8 %collective-permute-start.17 = (f32[128,512]{1,0:T(8,128)S(1)}, f32[128,512]{1,0:T(8,128)S(1)}, u32[]{:S(2)}, u32[]{:S(2)}) collective-permute-start(f32[128,512]{1,0:T(8,128)S(1)} %get-tuple-element.44), channel_id=1, source_target_pairs={{2,4},{3,5},{4,2},{5,3},{10,12},{11,13},{12,10},{13,11},{18,20},{1... | collective-permute-start | bytes 786440 | tf_op jit(solution)/shard_map/ppermute | solution.py:27
  65.9 3.6 %collective-permute-start.18 = (f32[128,512]{1,0:T(8,128)S(1)}, f32[128,512]{1,0:T(8,128)S(1)}, u32[]{:S(2)}, u32[]{:S(2)}) collective-permute-start(f32[128,512]{1,0:T(8,128)S(1)} %get-tuple-element.45), channel_id=1, source_target_pairs={{1,2},{2,1},{3,4},{4,3},{5,6},{6,5},{9,10},{10,9},{11,12},{12,11},... | collective-permute-start | bytes 786440 | tf_op jit(solution)/shard_map/ppermute | solution.py:27
  69.6 1.0 %shard_map.101.refs_3_ = f32[512,512]{1,0:T(8,128)S(1)} custom-call(bf16[512,1024]{1,0:T(8,128)(2,1)S(1)} %get-tuple-element.25.refs_0_.refs_1_.refs_7_, bf16[512,1024]{1,0:T(8,128)(2,1)S(1)} %get-tuple-element.26.refs_1_.refs_2_.refs_8_, f32[512,512]{1,0:T(8,128)S(1)} %collective-permute-done.9.refs_2_.refs_5_, ...), custom_call_target="tpu_custom_call" | custom-call | flops 805306368 | bytes 3145728 | tf_op jit(solution)/shard_map/pallas_call | solution.py:51
  70.6 5.6 %collective-permute-done.14.refs_1_ = f32[512,512]{1,0:T(8,128)S(1)} collective-permute-done((f32[512,512]{1,0:T(8,128)S(1)}, f32[512,512]{1,0:T(8,128)S(1)}, u32[]{:S(2)}, u32[]{:S(2)}) %collective-permute-start.14) | collective-permute-done | bytes 1048608 | tf_op jit(solution)/shard_map/ppermute | solution.py:32
  76.2 1.8 %shard_map.104.refs_4_ = f32[512,1024]{1,0:T(8,128)S(1)} custom-call(f32[1]{0:T(128)} %bitcast.12.refs_0_, f32[512,512]{1,0:T(8,128)S(1)} %collective-permute-done.14.refs_1_, f32[1024,1024]{1,0:T(8,128)S(1)} %bitcast.18), custom_call_target="tpu_custom_call" | custom-call | flops 1610612736 | bytes 6291456 | tf_op jit(solution)/shard_map/pallas_call | solution.py:51
  78.1 2.0 %collective-permute-done.18.refs_9_ = f32[128,512]{1,0:T(8,128)S(1)} collective-permute-done((f32[128,512]{1,0:T(8,128)S(1)}, f32[128,512]{1,0:T(8,128)S(1)}, u32[]{:S(2)}, u32[]{:S(2)}) %collective-permute-start.18) | collective-permute-done | bytes 262176 | tf_op jit(solution)/shard_map/ppermute | solution.py:27
  80.1 3.8 %shard_map.105 = f32[512,1024]{1,0:T(8,128)} custom-call(f32[1]{0:T(128)} %bitcast.12.refs_0_, bf16[512,1024]{1,0:T(8,128)(2,1)S(1)} %get-tuple-element.25.refs_0_.refs_1_.refs_7_, bf16[512,1024]{1,0:T(8,128)(2,1)S(1)} %get-tuple-element.26.refs_1_.refs_2_.refs_8_, f32[512,512]{1,0:T(8,128)S(1)} %shard_map.101.refs_3_, f32[512,1024]{1,0:T(8,128)S(1)} %shard_map.104.refs_4_, ...), custom_call_target="tpu_custom_call" | custom-call | flops 2415919104 | bytes 8388608 | tf_op jit(solution)/shard_map/pallas_call | solution.py:51
  (24 shorter events, 0.3 us)
Async XLA Ops:
  0.6 16.7 %copy-start.1 = (s32[4,4]{1,0:T(4,128)S(1)}, s32[4,4]{1,0:T(4,128)}, u32[]{:S(2)}) copy-start(s32[4,4]{1,0:T(4,128)} %refs_1_.1) | copy-start | bytes 196
  0.6 16.7 %copy-start.2 = (s32[4]{0:T(128)S(1)}, s32[4]{0:T(128)}, u32[]{:S(2)}) copy-start(s32[4]{0:T(128)} %refs_2_.1) | copy-start | bytes 52
  0.7 8.1 %collective-permute-start = (s32[4]{0:T(128)}, s32[4]{0:T(128)S(1)}, u32[]{:S(2)}, u32[]{:S(2)}) collective-permute-start(s32[4]{0:T(128)} %bitcast.27), channel_id=1, source_target_pairs={{1,2},{2,1},{3,4},{4,3},{5,6},{6,5},{9,10},{10,9},{11,12},{12,11},... | collective-permute-start | bytes 56 | tf_op jit(solution)/shard_map/ppermute | solution.py:27
  4.1 4.7 %collective-permute-start.1 = (s32[4]{0:T(128)}, s32[4]{0:T(128)S(1)}, u32[]{:S(2)}, u32[]{:S(2)}) collective-permute-start(s32[4]{0:T(128)} %bitcast.28), channel_id=1, source_target_pairs={{0,1},{1,0},{2,3},{3,2},{4,5},{5,4},{6,7},{7,6},{8,9},{9,8},{10,11... | collective-permute-start | bytes 56 | tf_op jit(solution)/shard_map/ppermute | solution.py:27
  5.8 3.7 %collective-permute-start.2 = (s32[4]{0:T(128)}, s32[4]{0:T(128)S(1)}, u32[]{:S(2)}, u32[]{:S(2)}) collective-permute-start(s32[4]{0:T(128)} %bitcast.29), channel_id=1, source_target_pairs={{0,2},{1,3},{2,0},{3,1},{4,6},{5,7},{6,4},{7,5},{8,10},{9,11},{10,... | collective-permute-start | bytes 56 | tf_op jit(solution)/shard_map/ppermute | solution.py:27
  5.8 5.6 %collective-permute-start.3 = (s32[4]{0:T(128)}, s32[4]{0:T(128)S(1)}, u32[]{:S(2)}, u32[]{:S(2)}) collective-permute-start(s32[4]{0:T(128)} %bitcast.30), channel_id=1, source_target_pairs={{2,4},{3,5},{4,2},{5,3},{10,12},{11,13},{12,10},{13,11},{18,20},{1... | collective-permute-start | bytes 56 | tf_op jit(solution)/shard_map/ppermute | solution.py:27
  13.3 15.1 %collective-permute-start.4 = (f32[128,1024]{1,0:T(8,128)S(1)}, f32[128,1024]{1,0:T(8,128)S(1)}, u32[]{:S(2)}, u32[]{:S(2)}) collective-permute-start(f32[128,1024]{1,0:T(8,128)S(1)} %get-tuple-element.24.refs_10_), channel_id=1, source_target_pairs={{0,1},{1,0},{2,3},{3,2},{4,5},{5,4},{6,7},{7,6},{8,9},{9,8},{10,11... | collective-permute-start | bytes 1572872 | tf_op jit(solution)/shard_map/ppermute | solution.py:27
  15.4 14.9 %collective-permute-start.5 = (f32[128,1024]{1,0:T(8,128)S(1)}, f32[128,1024]{1,0:T(8,128)S(1)}, u32[]{:S(2)}, u32[]{:S(2)}) collective-permute-start(f32[128,1024]{1,0:T(8,128)S(1)} %get-tuple-element.27), channel_id=1, source_target_pairs={{0,2},{1,3},{2,0},{3,1},{4,6},{5,7},{6,4},{7,5},{8,10},{9,11},{10,... | collective-permute-start | bytes 1572872 | tf_op jit(solution)/shard_map/ppermute | solution.py:27
  15.4 14.9 %collective-permute-start.6 = (f32[128,1024]{1,0:T(8,128)S(1)}, f32[128,1024]{1,0:T(8,128)S(1)}, u32[]{:S(2)}, u32[]{:S(2)}) collective-permute-start(f32[128,1024]{1,0:T(8,128)S(1)} %get-tuple-element.28), channel_id=1, source_target_pairs={{2,4},{3,5},{4,2},{5,3},{10,12},{11,13},{12,10},{13,11},{18,20},{1... | collective-permute-start | bytes 1572872 | tf_op jit(solution)/shard_map/ppermute | solution.py:27
  20.7 19.0 %collective-permute-start.7 = (f32[128,1024]{1,0:T(8,128)S(1)}, f32[128,1024]{1,0:T(8,128)S(1)}, u32[]{:S(2)}, u32[]{:S(2)}) collective-permute-start(f32[128,1024]{1,0:T(8,128)S(1)} %get-tuple-element.31), channel_id=1, source_target_pairs={{1,2},{2,1},{3,4},{4,3},{5,6},{6,5},{9,10},{10,9},{11,12},{12,11},... | collective-permute-start | bytes 1572872 | tf_op jit(solution)/shard_map/ppermute | solution.py:27
  24.2 22.7 %collective-permute-start.8 = (f32[512,512]{1,0:T(8,128)S(1)}, f32[512,512]{1,0:T(8,128)S(1)}, u32[]{:S(2)}, u32[]{:S(2)}) collective-permute-start(f32[512,512]{1,0:T(8,128)S(1)} %get-tuple-element.29.refs_11_), channel_id=1, source_target_pairs={{0,8},{8,16},{16,24},{24,0},{1,9},{9,17},{17,25},{25,1},{2,10},{10... | collective-permute-start | bytes 3145736 | tf_op jit(solution)/shard_map/ppermute | solution.py:32
  24.2 6.0 %copy-start = (f32[1,1024,1024]{2,1,0:T(8,128)S(1)}, f32[1,1024,1024]{2,1,0:T(8,128)}, u32[]{:S(2)}) copy-start(f32[1,1024,1024]{2,1,0:T(8,128)} %param.11) | copy-start | bytes 12582916
  42.9 14.3 %collective-permute-start.9 = (f32[512,512]{1,0:T(8,128)S(1)}, f32[512,512]{1,0:T(8,128)S(1)}, u32[]{:S(2)}, u32[]{:S(2)}) collective-permute-start(f32[512,512]{1,0:T(8,128)S(1)} %get-tuple-element.36), channel_id=1, source_target_pairs={{0,8},{8,16},{16,24},{24,0},{1,9},{9,17},{17,25},{25,1},{2,10},{10... | collective-permute-start | bytes 3145736 | tf_op jit(solution)/shard_map/ppermute | solution.py:32
  43.0 14.9 %collective-permute-start.10 = (f32[128,512]{1,0:T(8,128)S(1)}, f32[128,512]{1,0:T(8,128)S(1)}, u32[]{:S(2)}, u32[]{:S(2)}) collective-permute-start(f32[128,512]{1,0:T(8,128)S(1)} %get-tuple-element.38), channel_id=1, source_target_pairs={{0,1},{1,0},{2,3},{3,2},{4,5},{5,4},{6,7},{7,6},{8,9},{9,8},{10,11... | collective-permute-start | bytes 786440 | tf_op jit(solution)/shard_map/ppermute | solution.py:27
  43.1 14.8 %collective-permute-start.11 = (f32[128,512]{1,0:T(8,128)S(1)}, f32[128,512]{1,0:T(8,128)S(1)}, u32[]{:S(2)}, u32[]{:S(2)}) collective-permute-start(f32[128,512]{1,0:T(8,128)S(1)} %get-tuple-element.39), channel_id=1, source_target_pairs={{0,2},{1,3},{2,0},{3,1},{4,6},{5,7},{6,4},{7,5},{8,10},{9,11},{10,... | collective-permute-start | bytes 786440 | tf_op jit(solution)/shard_map/ppermute | solution.py:27
  43.1 14.7 %collective-permute-start.12 = (f32[128,512]{1,0:T(8,128)S(1)}, f32[128,512]{1,0:T(8,128)S(1)}, u32[]{:S(2)}, u32[]{:S(2)}) collective-permute-start(f32[128,512]{1,0:T(8,128)S(1)} %get-tuple-element.40), channel_id=1, source_target_pairs={{2,4},{3,5},{4,2},{5,3},{10,12},{11,13},{12,10},{13,11},{18,20},{1... | collective-permute-start | bytes 786440 | tf_op jit(solution)/shard_map/ppermute | solution.py:27
  46.9 14.0 %collective-permute-start.13 = (f32[128,512]{1,0:T(8,128)S(1)}, f32[128,512]{1,0:T(8,128)S(1)}, u32[]{:S(2)}, u32[]{:S(2)}) collective-permute-start(f32[128,512]{1,0:T(8,128)S(1)} %get-tuple-element.41), channel_id=1, source_target_pairs={{1,2},{2,1},{3,4},{4,3},{5,6},{6,5},{9,10},{10,9},{11,12},{12,11},... | collective-permute-start | bytes 786440 | tf_op jit(solution)/shard_map/ppermute | solution.py:27
  61.9 14.3 %collective-permute-start.14 = (f32[512,512]{1,0:T(8,128)S(1)}, f32[512,512]{1,0:T(8,128)S(1)}, u32[]{:S(2)}, u32[]{:S(2)}) collective-permute-start(f32[512,512]{1,0:T(8,128)S(1)} %shard_map.103), channel_id=1, source_target_pairs={{0,8},{8,16},{16,24},{24,0},{1,9},{9,17},{17,25},{25,1},{2,10},{10... | collective-permute-start | bytes 3145736 | tf_op jit(solution)/shard_map/ppermute | solution.py:32
  62.1 16.0 %collective-permute-start.15 = (f32[128,512]{1,0:T(8,128)S(1)}, f32[128,512]{1,0:T(8,128)S(1)}, u32[]{:S(2)}, u32[]{:S(2)}) collective-permute-start(f32[128,512]{1,0:T(8,128)S(1)} %get-tuple-element.42.refs_7_), channel_id=1, source_target_pairs={{0,1},{1,0},{2,3},{3,2},{4,5},{5,4},{6,7},{7,6},{8,9},{9,8},{10,11... | collective-permute-start | bytes 786440 | tf_op jit(solution)/shard_map/ppermute | solution.py:27
  62.1 16.0 %collective-permute-start.16 = (f32[128,512]{1,0:T(8,128)S(1)}, f32[128,512]{1,0:T(8,128)S(1)}, u32[]{:S(2)}, u32[]{:S(2)}) collective-permute-start(f32[128,512]{1,0:T(8,128)S(1)} %get-tuple-element.43), channel_id=1, source_target_pairs={{0,2},{1,3},{2,0},{3,1},{4,6},{5,7},{6,4},{7,5},{8,10},{9,11},{10,... | collective-permute-start | bytes 786440 | tf_op jit(solution)/shard_map/ppermute | solution.py:27
  62.1 15.9 %collective-permute-start.17 = (f32[128,512]{1,0:T(8,128)S(1)}, f32[128,512]{1,0:T(8,128)S(1)}, u32[]{:S(2)}, u32[]{:S(2)}) collective-permute-start(f32[128,512]{1,0:T(8,128)S(1)} %get-tuple-element.44), channel_id=1, source_target_pairs={{2,4},{3,5},{4,2},{5,3},{10,12},{11,13},{12,10},{13,11},{18,20},{1... | collective-permute-start | bytes 786440 | tf_op jit(solution)/shard_map/ppermute | solution.py:27
  65.9 14.1 %collective-permute-start.18 = (f32[128,512]{1,0:T(8,128)S(1)}, f32[128,512]{1,0:T(8,128)S(1)}, u32[]{:S(2)}, u32[]{:S(2)}) collective-permute-start(f32[128,512]{1,0:T(8,128)S(1)} %get-tuple-element.45), channel_id=1, source_target_pairs={{1,2},{2,1},{3,4},{4,3},{5,6},{6,5},{9,10},{10,9},{11,12},{12,11},... | collective-permute-start | bytes 786440 | tf_op jit(solution)/shard_map/ppermute | solution.py:27

commit v5 on v4

--- a/solution.py
+++ b/solution.py
@@ -164,7 +164,9 @@
 
 def times_adj(high_ref, low_ref, at, value):
     cut = slice(at, at + value.shape[0])
-    return dot3((high_ref[:, cut], low_ref[:, cut]), halves(value))
+    a, b = (high_ref[:, cut], low_ref[:, cut]), halves(value)
+    rows, columns = jnp.concatenate([a[0], a[1], a[0]], axis=1), jnp.concatenate([b[0], b[0], b[1]], axis=0)
+    return jnp.dot(rows, columns, preferred_element_type=F32)
 
 
 def stacked(refs):
@@ -278,16 +280,17 @@
     )
 
 
-def left_kernel(high_ref, low_ref, feats_ref, first_ref, out_ref):
-    out_ref[...] = times_adj(high_ref, low_ref, 0, feats_ref[...]) + 0.1 * first_ref[...]
-
-
-def own_left(adj, feats, first):
+def left_kernel(high_ref, low_ref, feats_ref, first_ref, *refs):
+    came, out_ref = refs[:-1], refs[-1]
+    out_ref[...] = times_adj(high_ref, low_ref, 0, stacked((feats_ref, *came))) + 0.1 * first_ref[...]
+
+
+def own_left(adj, feats, first, came):
     rows, half = feats.shape
     return call(
         left_kernel,
-        (*adj, feats, first),
-        [VMEM] * 4,
+        (*adj, feats, first, *came),
+        [VMEM] * (4 + len(came)),
         (vmem(rows, half),),
         flops=6 * rows * rows * half,
         nbytes=12 * rows * half,
@@ -334,35 +337,59 @@
     )[0]
 
 
-def second_kernel(beta_ref, high_ref, low_ref, left_ref, term_ref, weight_ref, *refs, tile):
-    came, (out_ref, held, sem) = refs[:-3], refs[-3:]
+def known_kernel(beta_ref, high_ref, low_ref, left_ref, term_ref, weight_ref, *refs):
+    came, out_ref = refs[:-1], refs[-1]
     rows, half = left_ref.shape
+    column = high_ref.shape[1] - BLK - len(came) * BLK
+    left = left_ref[...] + times_adj(high_ref, low_ref, column, stacked(came))
+    beta = beta_ref[0]
+    value = term_ref[...] + beta * dot3(halves(left), halves(weight_ref[:half, :]))
+    out_ref[:, :half] = value[:, :half] + (1.0 - beta) * left
+    out_ref[:, half:] = value[:, half:]
+
+
+def second_known(beta, adj, left, term, weight, came):
+    rows, half = left.shape
+    width = weight.shape[1]
+    return call(
+        known_kernel,
+        (beta, *adj, left, term, weight, *came),
+        [SMEM] + [VMEM] * (5 + len(came)),
+        (vmem(rows, width),),
+        flops=6 * rows * half * (width + len(came) * BLK),
+        nbytes=4 * (half * width + 3 * rows * width),
+    )[0]
+
+
+def second_kernel(beta_ref, high_ref, low_ref, base_ref, weight_ref, came_ref, out_ref, held, sem, *, tile):
+    half = came_ref.shape[1]
     width = weight_ref.shape[1]
-    left = left_ref[...] + times_adj(high_ref, low_ref, rows, stacked(came))
-    pair = halves(left)
+    came = came_ref[...]
+    pair = halves(came)
     beta = beta_ref[0]
+    column = high_ref.shape[1] - BLK
     copies = []
     for i, at in enumerate(range(0, width, tile)):
         cut = slice(at, at + tile)
-        value = term_ref[:, cut] + beta * dot3(pair, halves(weight_ref[:half, cut]))
+        through = beta * dot3(pair, halves(weight_ref[:half, cut]))
         if at < half:
-            value = value + (1.0 - beta) * left[:, cut]
-        held[:, cut] = jnp.maximum(value, 0.0)
+            through = through + (1.0 - beta) * came[:, cut]
+        held[:, cut] = jnp.maximum(base_ref[:, cut] + times_adj(high_ref, low_ref, column, through), 0.0)
         copies.append(pltpu.make_async_copy(held.at[:, cut], out_ref.at[:, cut], sem.at[i]))
         copies[-1].start()
     for copy in copies:
         copy.wait()
 
 
-def second_layer(beta, adj, left, term, weight, came, tile=256):
-    rows, half = left.shape
-    width = weight.shape[1]
+def second_layer(beta, adj, base, weight, came, tile=256):
+    rows, width = base.shape
+    half = came.shape[1]
     return call(
         functools.partial(second_kernel, tile=tile),
-        (beta, *adj, left, term, weight, *came),
-        [SMEM] + [VMEM] * (5 + len(came)),
+        (beta, *adj, base, weight, came),
+        [SMEM] + [VMEM] * 5,
         (pltpu.HBM((rows, width), F32),),
-        flops=6 * rows * half * (width + len(came) * BLK),
+        flops=6 * BLK * width * (half + rows),
         nbytes=4 * (half * width + 3 * rows * width),
         scratch=[pltpu.VMEM((rows, width), F32), ONE((width // tile,))],
     )[0]
@@ -413,8 +440,9 @@
     sent = choose(every, index, got, left)
     right = hand_on(add_received(adj, mixed, came, after=sent[:1]))
     came = [swap(value, *kind) for value, kind in zip(sent, SWAPS)]
-    mixed = own_left(adj, left, handed_left)
-    second_out = second_layer(beta, adj, mixed, right_term(beta, right, weight), weight, came)
+    mixed = own_left(adj, left, handed_left, came[:1])
+    known = second_known(beta, adj, mixed, right_term(beta, right, weight), weight, came[1:final])
+    second_out = second_layer(beta, adj, known, weight, came[final])
     return first_out[None], second_out[None]
 
 

time: 84.6 us -> 83.1 us (0.982)
  waiting for transfers between devices: 24.7 us -> 22.7 us
    ppermute x3, waiting for transfers between devices: 11.1 us -> 9.24 us  [hand_on(): lax.ppermute(value, 'segment', [(i, (i + 1) % peers) for i in range(peers)])]
    pallas_call x11 -> x12, Pallas kernels: 27.6 us -> 28.3 us  [call(): pl.pallas_call(body, out_shape=outs, in_specs=list(in_specs) + [VMEM] * l...]
  transfers between devices with their start and end apart: 19 -> 19, of which waited for: 8 -> 8; matrix products, arithmetic and copies ran while one was open for 0% -> 0% of each run, Pallas kernels for 25% -> 28%
where the time goes in v5:
time: 83.1 us; the launch traced here: 82.8 us
  starting transfers between devices  30.4 us (37%)
  Pallas kernels  28.3 us (34%)
  waiting for transfers between devices  22.7 us (27%)
  between operations  1.25 us (2%)
    ppermute x16, starting transfers between devices, swap(): return lax.ppermute(value, 'graph', sorted(pairs))  30.1 us
    pallas_call x12, Pallas kernels, call(): pl.pallas_call(body, out_shape=outs, in_specs=list(in_specs) + [VMEM] * l...  28.3 us
    ppermute x16, waiting for transfers between devices, swap(): return lax.ppermute(value, 'graph', sorted(pairs))  13.5 us
    ppermute x3, waiting for transfers between devices, hand_on(): lax.ppermute(value, 'segment', [(i, (i + 1) % peers) for i in range(peers)])  9.24 us
  transfers between devices with their start and end apart: 19, of which 8 were waited for; matrix products, arithmetic and copies ran while one was open for 0% of the time, Pallas kernels for 28%

profile of v5, /device:TPU:16, one launch (start us, length us, event | category | flops | bytes accessed | tf_op | source)
XLA Modules:
  0.0 82.8 jit_solution(2462284981407785318)
XLA Ops:
  0.7 3.4 %collective-permute-start = (s32[4]{0:T(128)}, s32[4]{0:T(128)S(1)}, u32[]{:S(2)}, u32[]{:S(2)}) collective-permute-start(s32[4]{0:T(128)} %bitcast.28), channel_id=1, source_target_pairs={{1,2},{2,1},{3,4},{4,3},{5,6},{6,5},{9,10},{10,9},{11,12},{12,11},... | collective-permute-start | bytes 56 | tf_op jit(solution)/shard_map/ppermute | solution.py:27
  4.1 1.7 %collective-permute-start.1 = (s32[4]{0:T(128)}, s32[4]{0:T(128)S(1)}, u32[]{:S(2)}, u32[]{:S(2)}) collective-permute-start(s32[4]{0:T(128)} %bitcast.29), channel_id=1, source_target_pairs={{0,1},{1,0},{2,3},{3,2},{4,5},{5,4},{6,7},{7,6},{8,9},{9,8},{10,11... | collective-permute-start | bytes 56 | tf_op jit(solution)/shard_map/ppermute | solution.py:27
  5.8 2.8 %collective-permute-start.3 = (s32[4]{0:T(128)}, s32[4]{0:T(128)S(1)}, u32[]{:S(2)}, u32[]{:S(2)}) collective-permute-start(s32[4]{0:T(128)} %bitcast.31), channel_id=1, source_target_pairs={{2,4},{3,5},{4,2},{5,3},{10,12},{11,13},{12,10},{13,11},{18,20},{1... | collective-permute-start | bytes 56 | tf_op jit(solution)/shard_map/ppermute | solution.py:27
  8.7 0.1 pad_add_fusion
  8.8 0.7 collective-permute-done.2.refs_2_.refs_4_
  9.5 1.9 %collective-permute-done.3.refs_3_.refs_5_ = s32[4]{0:T(128)S(1)} collective-permute-done((s32[4]{0:T(128)}, s32[4]{0:T(128)S(1)}, u32[]{:S(2)}, u32[]{:S(2)}) %collective-permute-start.3) | collective-permute-done | bytes 48 | tf_op jit(solution)/shard_map/ppermute | solution.py:27
  11.4 2.0 %shard_map.95 = (f32[128,1024]{1,0:T(8,128)S(1)}, f32[128,1024]{1,0:T(8,128)S(1)}, f32[128,1024]{1,0:T(8,128)S(1)}) custom-call(s32[4]{0:T(128)S(1)} %get-tuple-element.47.refs_0_.refs_3_.refs_2_, s32[4]{0:T(128)S(1)} %collective-permute-done.1.refs_1_.refs_3_, s32[4]{0:T(128)S(1)} %collective-permute-done.2.refs_2_.refs_4_, ...), custom_call_target="tpu_custom_call" | custom-call | bytes 3145728 | tf_op jit(solution)/shard_map/pallas_call | solution.py:51
  13.3 2.0 %collective-permute-start.4 = (f32[128,1024]{1,0:T(8,128)S(1)}, f32[128,1024]{1,0:T(8,128)S(1)}, u32[]{:S(2)}, u32[]{:S(2)}) collective-permute-start(f32[128,1024]{1,0:T(8,128)S(1)} %get-tuple-element.24.refs_10_), channel_id=1, source_target_pairs={{0,1},{1,0},{2,3},{3,2},{4,5},{5,4},{6,7},{7,6},{8,9},{9,8},{10,11... | collective-permute-start | bytes 1572872 | tf_op jit(solution)/shard_map/ppermute | solution.py:27
  15.4 1.9 %collective-permute-start.6 = (f32[128,1024]{1,0:T(8,128)S(1)}, f32[128,1024]{1,0:T(8,128)S(1)}, u32[]{:S(2)}, u32[]{:S(2)}) collective-permute-start(f32[128,1024]{1,0:T(8,128)S(1)} %get-tuple-element.28), channel_id=1, source_target_pairs={{2,4},{3,5},{4,2},{5,3},{10,12},{11,13},{12,10},{13,11},{18,20},{1... | collective-permute-start | bytes 1572872 | tf_op jit(solution)/shard_map/ppermute | solution.py:27
  17.4 3.3 %shard_map.96 = (bf16[512,1024]{1,0:T(8,128)(2,1)S(1)}, bf16[512,1024]{1,0:T(8,128)(2,1)S(1)}, f32[128,1024]{1,0:T(8,128)S(1)}, f32[512,512]{1,0:T(8,128)S(1)}, f32[512,512]{1,0:T(8,128)S(1)}) custom-call(s32[4]{0:T(128)S(1)} %get-tuple-element.46.refs_0_, s32[4,4]{1,0:T(4,128)S(1)} %copy-done.1, s32[4]{0:T(128)S(1)} %copy-done.2, ...), custom_call_target="tpu_custom_call" | custom-call | bytes 3145728 | tf_op jit(solution)/shard_map/pallas_call | solution.py:51
  20.7 3.5 %collective-permute-start.7 = (f32[128,1024]{1,0:T(8,128)S(1)}, f32[128,1024]{1,0:T(8,128)S(1)}, u32[]{:S(2)}, u32[]{:S(2)}) collective-permute-start(f32[128,1024]{1,0:T(8,128)S(1)} %get-tuple-element.31), channel_id=1, source_target_pairs={{1,2},{2,1},{3,4},{4,3},{5,6},{6,5},{9,10},{10,9},{11,12},{12,11},... | collective-permute-start | bytes 1572872 | tf_op jit(solution)/shard_map/ppermute | solution.py:27
  24.2 4.2 %shard_map.97.refs_4_ = f32[512,1024]{1,0:T(8,128)S(1)} custom-call(bf16[512,1024]{1,0:T(8,128)(2,1)S(1)} %get-tuple-element.25.refs_0_.refs_1_.refs_7_, bf16[512,1024]{1,0:T(8,128)(2,1)S(1)} %get-tuple-element.26.refs_1_.refs_2_.refs_8_, f32[512,1024]{1,0:T(8,128)} %bitcast.23, f32[512,1024]{1,0:T(8,128)} %bitcast.25), custom_call_target="tpu_custom_call" | custom-call | flops 1610612736 | bytes 6291456 | tf_op jit(solution)/shard_map/pallas_call | solution.py:51
  28.5 1.8 %collective-permute-done.5.refs_6_ = f32[128,1024]{1,0:T(8,128)S(1)} collective-permute-done((f32[128,1024]{1,0:T(8,128)S(1)}, f32[128,1024]{1,0:T(8,128)S(1)}, u32[]{:S(2)}, u32[]{:S(2)}) %collective-permute-start.5) | collective-permute-done | bytes 524320 | tf_op jit(solution)/shard_map/ppermute | solution.py:27
  30.2 5.0 %shard_map.98.refs_9_ = f32[512,1024]{1,0:T(8,128)S(1)} custom-call(f32[1]{0:T(128)} %bitcast.12.refs_0_, bf16[512,1024]{1,0:T(8,128)(2,1)S(1)} %get-tuple-element.25.refs_0_.refs_1_.refs_7_, bf16[512,1024]{1,0:T(8,128)(2,1)S(1)} %get-tuple-element.26.refs_1_.refs_2_.refs_8_, f32[1024,1024]{1,0:T(8,128)S(1)} %bitcast.16, f32[512,1024]{1,0:T(8,128)S(1)} %shard_map.97.refs_4_, ...), custom_call_target="tpu_custom_call" | custom-call | flops 4429185024 | bytes 8388608 | tf_op jit(solution)/shard_map/pallas_call | solution.py:51
  35.2 4.5 %collective-permute-done.7.refs_13_ = f32[128,1024]{1,0:T(8,128)S(1)} collective-permute-done((f32[128,1024]{1,0:T(8,128)S(1)}, f32[128,1024]{1,0:T(8,128)S(1)}, u32[]{:S(2)}, u32[]{:S(2)}) %collective-permute-start.7) | collective-permute-done | bytes 524320 | tf_op jit(solution)/shard_map/ppermute | solution.py:27
  39.7 3.0 %shard_map.99 = (f32[512,512]{1,0:T(8,128)S(1)}, f32[512,512]{1,0:T(8,128)S(1)}, f32[512,512]{1,0:T(8,128)S(1)}, f32[512,512]{1,0:T(8,128)S(1)}, f32[128,512]{1,...) custom-call(f32[1]{0:T(128)} %bitcast.12.refs_0_, ...), custom_call_target="tpu_custom_call" | custom-call | flops 1207959552 | bytes 16777216 | tf_op jit(solution)/shard_map/pallas_call | solution.py:51
  42.9 3.7 %collective-permute-start.13 = (f32[128,512]{1,0:T(8,128)S(1)}, f32[128,512]{1,0:T(8,128)S(1)}, u32[]{:S(2)}, u32[]{:S(2)}) collective-permute-start(f32[128,512]{1,0:T(8,128)S(1)} %get-tuple-element.41), channel_id=1, source_target_pairs={{2,4},{3,5},{4,2},{5,3},{10,12},{11,13},{12,10},{13,11},{18,20},{1... | collective-permute-start | bytes 786440 | tf_op jit(solution)/shard_map/ppermute | solution.py:27
  46.7 3.5 %collective-permute-start.14 = (f32[128,512]{1,0:T(8,128)S(1)}, f32[128,512]{1,0:T(8,128)S(1)}, u32[]{:S(2)}, u32[]{:S(2)}) collective-permute-start(f32[128,512]{1,0:T(8,128)S(1)} %get-tuple-element.42), channel_id=1, source_target_pairs={{1,2},{2,1},{3,4},{4,3},{5,6},{6,5},{9,10},{10,9},{11,12},{12,11},... | collective-permute-start | bytes 786440 | tf_op jit(solution)/shard_map/ppermute | solution.py:27
  50.1 1.4 %shard_map.100 = (f32[512,512]{1,0:T(8,128)S(1)}, f32[512,1024]{1,0:T(8,128)}) custom-call(bf16[512,1024]{1,0:T(8,128)(2,1)S(1)} %get-tuple-element.25.refs_0_.refs_1_.refs_7_, bf16[512,1024]{1,0:T(8,128)(2,1)S(1)} %get-tuple-element.26.refs_1_.refs_2_.refs_8_, f32[512,512]{1,0:T(8,128)S(1)} %get-tuple-element.32.refs_2_, ...), custom_call_target="tpu_custom_call" | custom-call | flops 805306368 | bytes 7340032 | tf_op jit(solution)/shard_map/pallas_call | solution.py:51
  51.5 5.5 %collective-permute-done.9.refs_5_.refs_2_ = f32[512,512]{1,0:T(8,128)S(1)} collective-permute-done((f32[512,512]{1,0:T(8,128)S(1)}, f32[512,512]{1,0:T(8,128)S(1)}, u32[]{:S(2)}, u32[]{:S(2)}) %collective-permute-start.9) | collective-permute-done | bytes 1048608 | tf_op jit(solution)/shard_map/ppermute | solution.py:32
  57.0 0.6 shard_map.101
  57.7 3.0 %collective-permute-done.14.refs_6_ = f32[128,512]{1,0:T(8,128)S(1)} collective-permute-done((f32[128,512]{1,0:T(8,128)S(1)}, f32[128,512]{1,0:T(8,128)S(1)}, u32[]{:S(2)}, u32[]{:S(2)}) %collective-permute-start.14) | collective-permute-done | bytes 262176 | tf_op jit(solution)/shard_map/ppermute | solution.py:27
  60.7 1.0 %shard_map.103 = f32[512,512]{1,0:T(8,128)S(1)} custom-call(bf16[512,1024]{1,0:T(8,128)(2,1)S(1)} %get-tuple-element.25.refs_0_.refs_1_.refs_7_, bf16[512,1024]{1,0:T(8,128)(2,1)S(1)} %get-tuple-element.26.refs_1_.refs_2_.refs_8_, f32[512,512]{1,0:T(8,128)S(1)} %get-tuple-element.38.refs_2_, f32[128,512]{1,0:T(8,128)S(1)} %collective-permute-done.11.refs_3_, ...), custom_call_target="tpu_custom_call" | custom-call | flops 805306368 | bytes 2097152 | tf_op jit(solution)/shard_map/pallas_call | solution.py:51
  61.7 0.2 collective-permute-start.15
  61.9 3.8 %collective-permute-start.17 = (f32[128,512]{1,0:T(8,128)S(1)}, f32[128,512]{1,0:T(8,128)S(1)}, u32[]{:S(2)}, u32[]{:S(2)}) collective-permute-start(f32[128,512]{1,0:T(8,128)S(1)} %get-tuple-element.44), channel_id=1, source_target_pairs={{2,4},{3,5},{4,2},{5,3},{10,12},{11,13},{12,10},{13,11},{18,20},{1... | collective-permute-start | bytes 786440 | tf_op jit(solution)/shard_map/ppermute | solution.py:27
  65.7 3.7 %collective-permute-start.18 = (f32[128,512]{1,0:T(8,128)S(1)}, f32[128,512]{1,0:T(8,128)S(1)}, u32[]{:S(2)}, u32[]{:S(2)}) collective-permute-start(f32[128,512]{1,0:T(8,128)S(1)} %get-tuple-element.45), channel_id=1, source_target_pairs={{1,2},{2,1},{3,4},{4,3},{5,6},{6,5},{9,10},{10,9},{11,12},{12,11},... | collective-permute-start | bytes 786440 | tf_op jit(solution)/shard_map/ppermute | solution.py:27
  69.4 1.6 %collective-permute-done.10.refs_4_ = f32[128,512]{1,0:T(8,128)S(1)} collective-permute-done((f32[128,512]{1,0:T(8,128)S(1)}, f32[128,512]{1,0:T(8,128)S(1)}, u32[]{:S(2)}, u32[]{:S(2)}) %collective-permute-start.10) | collective-permute-done | bytes 262176 | tf_op jit(solution)/shard_map/ppermute | solution.py:27
  70.9 1.3 %shard_map.102.refs_3_ = f32[512,512]{1,0:T(8,128)S(1)} custom-call(bf16[512,1024]{1,0:T(8,128)(2,1)S(1)} %get-tuple-element.25.refs_0_.refs_1_.refs_7_, bf16[512,1024]{1,0:T(8,128)(2,1)S(1)} %get-tuple-element.26.refs_1_.refs_2_.refs_8_, f32[512,512]{1,0:T(8,128)S(1)} %collective-permute-done.9.refs_5_.refs_2_, ...), custom_call_target="tpu_custom_call" | custom-call | flops 805306368 | bytes 3145728 | tf_op jit(solution)/shard_map/pallas_call | solution.py:51
  72.2 3.8 %collective-permute-done.15.refs_1_ = f32[512,512]{1,0:T(8,128)S(1)} collective-permute-done((f32[512,512]{1,0:T(8,128)S(1)}, f32[512,512]{1,0:T(8,128)S(1)}, u32[]{:S(2)}, u32[]{:S(2)}) %collective-permute-start.15) | collective-permute-done | bytes 1048608 | tf_op jit(solution)/shard_map/ppermute | solution.py:32
  76.0 1.8 %shard_map.104.refs_4_ = f32[512,1024]{1,0:T(8,128)S(1)} custom-call(f32[1]{0:T(128)} %bitcast.12.refs_0_, f32[512,512]{1,0:T(8,128)S(1)} %collective-permute-done.15.refs_1_, f32[1024,1024]{1,0:T(8,128)S(1)} %bitcast.18), custom_call_target="tpu_custom_call" | custom-call | flops 1610612736 | bytes 6291456 | tf_op jit(solution)/shard_map/pallas_call | solution.py:51
  77.9 2.3 %shard_map.105.refs_3_ = f32[512,1024]{1,0:T(8,128)S(1)} custom-call(f32[1]{0:T(128)} %bitcast.12.refs_0_, bf16[512,1024]{1,0:T(8,128)(2,1)S(1)} %get-tuple-element.25.refs_0_.refs_1_.refs_7_, bf16[512,1024]{1,0:T(8,128)(2,1)S(1)} %get-tuple-element.26.refs_1_.refs_2_.refs_8_, f32[512,512]{1,0:T(8,128)S(1)} %shard_map.102.refs_3_, ...), custom_call_target="tpu_custom_call" | custom-call | flops 2013265920 | bytes 8388608 | tf_op jit(solution)/shard_map/pallas_call | solution.py:51
  80.2 2.4 %shard_map.106 = f32[512,1024]{1,0:T(8,128)} custom-call(f32[1]{0:T(128)} %bitcast.12.refs_0_, bf16[512,1024]{1,0:T(8,128)(2,1)S(1)} %get-tuple-element.25.refs_0_.refs_1_.refs_7_, bf16[512,1024]{1,0:T(8,128)(2,1)S(1)} %get-tuple-element.26.refs_1_.refs_2_.refs_8_, f32[512,1024]{1,0:T(8,128)S(1)} %shard_map.105.refs_3_, f32[1024,1024]{1,0:T(8,128)S(1)} %bitcast.20, ...), custom_call_target="tpu_custom_call" | custom-call | flops 805306368 | bytes 8388608 | tf_op jit(solution)/shard_map/pallas_call | solution.py:51
  (25 shorter events, 0.4 us)
Async XLA Ops:
  0.6 16.7 %copy-start.1 = (s32[4,4]{1,0:T(4,128)S(1)}, s32[4,4]{1,0:T(4,128)}, u32[]{:S(2)}) copy-start(s32[4,4]{1,0:T(4,128)} %refs_1_.1) | copy-start | bytes 196
  0.6 16.7 %copy-start.2 = (s32[4]{0:T(128)S(1)}, s32[4]{0:T(128)}, u32[]{:S(2)}) copy-start(s32[4]{0:T(128)} %refs_2_.1) | copy-start | bytes 52
  0.7 8.1 %collective-permute-start = (s32[4]{0:T(128)}, s32[4]{0:T(128)S(1)}, u32[]{:S(2)}, u32[]{:S(2)}) collective-permute-start(s32[4]{0:T(128)} %bitcast.28), channel_id=1, source_target_pairs={{1,2},{2,1},{3,4},{4,3},{5,6},{6,5},{9,10},{10,9},{11,12},{12,11},... | collective-permute-start | bytes 56 | tf_op jit(solution)/shard_map/ppermute | solution.py:27
  4.1 4.7 %collective-permute-start.1 = (s32[4]{0:T(128)}, s32[4]{0:T(128)S(1)}, u32[]{:S(2)}, u32[]{:S(2)}) collective-permute-start(s32[4]{0:T(128)} %bitcast.29), channel_id=1, source_target_pairs={{0,1},{1,0},{2,3},{3,2},{4,5},{5,4},{6,7},{7,6},{8,9},{9,8},{10,11... | collective-permute-start | bytes 56 | tf_op jit(solution)/shard_map/ppermute | solution.py:27
  5.8 3.7 %collective-permute-start.2 = (s32[4]{0:T(128)}, s32[4]{0:T(128)S(1)}, u32[]{:S(2)}, u32[]{:S(2)}) collective-permute-start(s32[4]{0:T(128)} %bitcast.30), channel_id=1, source_target_pairs={{0,2},{1,3},{2,0},{3,1},{4,6},{5,7},{6,4},{7,5},{8,10},{9,11},{10,... | collective-permute-start | bytes 56 | tf_op jit(solution)/shard_map/ppermute | solution.py:27
  5.8 5.6 %collective-permute-start.3 = (s32[4]{0:T(128)}, s32[4]{0:T(128)S(1)}, u32[]{:S(2)}, u32[]{:S(2)}) collective-permute-start(s32[4]{0:T(128)} %bitcast.31), channel_id=1, source_target_pairs={{2,4},{3,5},{4,2},{5,3},{10,12},{11,13},{12,10},{13,11},{18,20},{1... | collective-permute-start | bytes 56 | tf_op jit(solution)/shard_map/ppermute | solution.py:27
  13.3 15.1 %collective-permute-start.4 = (f32[128,1024]{1,0:T(8,128)S(1)}, f32[128,1024]{1,0:T(8,128)S(1)}, u32[]{:S(2)}, u32[]{:S(2)}) collective-permute-start(f32[128,1024]{1,0:T(8,128)S(1)} %get-tuple-element.24.refs_10_), channel_id=1, source_target_pairs={{0,1},{1,0},{2,3},{3,2},{4,5},{5,4},{6,7},{7,6},{8,9},{9,8},{10,11... | collective-permute-start | bytes 1572872 | tf_op jit(solution)/shard_map/ppermute | solution.py:27
  15.4 14.9 %collective-permute-start.5 = (f32[128,1024]{1,0:T(8,128)S(1)}, f32[128,1024]{1,0:T(8,128)S(1)}, u32[]{:S(2)}, u32[]{:S(2)}) collective-permute-start(f32[128,1024]{1,0:T(8,128)S(1)} %get-tuple-element.27), channel_id=1, source_target_pairs={{0,2},{1,3},{2,0},{3,1},{4,6},{5,7},{6,4},{7,5},{8,10},{9,11},{10,... | collective-permute-start | bytes 1572872 | tf_op jit(solution)/shard_map/ppermute | solution.py:27
  15.4 14.9 %collective-permute-start.6 = (f32[128,1024]{1,0:T(8,128)S(1)}, f32[128,1024]{1,0:T(8,128)S(1)}, u32[]{:S(2)}, u32[]{:S(2)}) collective-permute-start(f32[128,1024]{1,0:T(8,128)S(1)} %get-tuple-element.28), channel_id=1, source_target_pairs={{2,4},{3,5},{4,2},{5,3},{10,12},{11,13},{12,10},{13,11},{18,20},{1... | collective-permute-start | bytes 1572872 | tf_op jit(solution)/shard_map/ppermute | solution.py:27
  20.7 19.0 %collective-permute-start.7 = (f32[128,1024]{1,0:T(8,128)S(1)}, f32[128,1024]{1,0:T(8,128)S(1)}, u32[]{:S(2)}, u32[]{:S(2)}) collective-permute-start(f32[128,1024]{1,0:T(8,128)S(1)} %get-tuple-element.31), channel_id=1, source_target_pairs={{1,2},{2,1},{3,4},{4,3},{5,6},{6,5},{9,10},{10,9},{11,12},{12,11},... | collective-permute-start | bytes 1572872 | tf_op jit(solution)/shard_map/ppermute | solution.py:27
  24.1 22.5 %collective-permute-start.8 = (f32[512,512]{1,0:T(8,128)S(1)}, f32[512,512]{1,0:T(8,128)S(1)}, u32[]{:S(2)}, u32[]{:S(2)}) collective-permute-start(f32[512,512]{1,0:T(8,128)S(1)} %get-tuple-element.29.refs_11_), channel_id=1, source_target_pairs={{0,8},{8,16},{16,24},{24,0},{1,9},{9,17},{17,25},{25,1},{2,10},{10... | collective-permute-start | bytes 3145736 | tf_op jit(solution)/shard_map/ppermute | solution.py:32
  24.2 6.0 %copy-start = (f32[1,1024,1024]{2,1,0:T(8,128)S(1)}, f32[1,1024,1024]{2,1,0:T(8,128)}, u32[]{:S(2)}) copy-start(f32[1,1024,1024]{2,1,0:T(8,128)} %param.11) | copy-start | bytes 12582916
  42.7 14.3 %collective-permute-start.9 = (f32[512,512]{1,0:T(8,128)S(1)}, f32[512,512]{1,0:T(8,128)S(1)}, u32[]{:S(2)}, u32[]{:S(2)}) collective-permute-start(f32[512,512]{1,0:T(8,128)S(1)} %get-tuple-element.36), channel_id=1, source_target_pairs={{0,8},{8,16},{16,24},{24,0},{1,9},{9,17},{17,25},{25,1},{2,10},{10... | collective-permute-start | bytes 3145736 | tf_op jit(solution)/shard_map/ppermute | solution.py:32
  42.8 14.9 %collective-permute-start.11 = (f32[128,512]{1,0:T(8,128)S(1)}, f32[128,512]{1,0:T(8,128)S(1)}, u32[]{:S(2)}, u32[]{:S(2)}) collective-permute-start(f32[128,512]{1,0:T(8,128)S(1)} %get-tuple-element.39), channel_id=1, source_target_pairs={{0,1},{1,0},{2,3},{3,2},{4,5},{5,4},{6,7},{7,6},{8,9},{9,8},{10,11... | collective-permute-start | bytes 786440 | tf_op jit(solution)/shard_map/ppermute | solution.py:27
  42.8 14.8 %collective-permute-start.12 = (f32[128,512]{1,0:T(8,128)S(1)}, f32[128,512]{1,0:T(8,128)S(1)}, u32[]{:S(2)}, u32[]{:S(2)}) collective-permute-start(f32[128,512]{1,0:T(8,128)S(1)} %get-tuple-element.40), channel_id=1, source_target_pairs={{0,2},{1,3},{2,0},{3,1},{4,6},{5,7},{6,4},{7,5},{8,10},{9,11},{10,... | collective-permute-start | bytes 786440 | tf_op jit(solution)/shard_map/ppermute | solution.py:27
  42.9 14.7 %collective-permute-start.13 = (f32[128,512]{1,0:T(8,128)S(1)}, f32[128,512]{1,0:T(8,128)S(1)}, u32[]{:S(2)}, u32[]{:S(2)}) collective-permute-start(f32[128,512]{1,0:T(8,128)S(1)} %get-tuple-element.41), channel_id=1, source_target_pairs={{2,4},{3,5},{4,2},{5,3},{10,12},{11,13},{12,10},{13,11},{18,20},{1... | collective-permute-start | bytes 786440 | tf_op jit(solution)/shard_map/ppermute | solution.py:27
  46.7 14.0 %collective-permute-start.14 = (f32[128,512]{1,0:T(8,128)S(1)}, f32[128,512]{1,0:T(8,128)S(1)}, u32[]{:S(2)}, u32[]{:S(2)}) collective-permute-start(f32[128,512]{1,0:T(8,128)S(1)} %get-tuple-element.42), channel_id=1, source_target_pairs={{1,2},{2,1},{3,4},{4,3},{5,6},{6,5},{9,10},{10,9},{11,12},{12,11},... | collective-permute-start | bytes 786440 | tf_op jit(solution)/shard_map/ppermute | solution.py:27
  61.7 14.3 %collective-permute-start.15 = (f32[512,512]{1,0:T(8,128)S(1)}, f32[512,512]{1,0:T(8,128)S(1)}, u32[]{:S(2)}, u32[]{:S(2)}) collective-permute-start(f32[512,512]{1,0:T(8,128)S(1)} %shard_map.103), channel_id=1, source_target_pairs={{0,8},{8,16},{16,24},{24,0},{1,9},{9,17},{17,25},{25,1},{2,10},{10... | collective-permute-start | bytes 3145736 | tf_op jit(solution)/shard_map/ppermute | solution.py:32
  61.9 9.1 %collective-permute-start.10 = (f32[128,512]{1,0:T(8,128)S(1)}, f32[128,512]{1,0:T(8,128)S(1)}, u32[]{:S(2)}, u32[]{:S(2)}) collective-permute-start(f32[128,512]{1,0:T(8,128)S(1)} %get-tuple-element.37.refs_7_), channel_id=1, source_target_pairs={{0,1},{1,0},{2,3},{3,2},{4,5},{5,4},{6,7},{7,6},{8,9},{9,8},{10,11... | collective-permute-start | bytes 786440 | tf_op jit(solution)/shard_map/ppermute | solution.py:27
  61.9 16.0 %collective-permute-start.16 = (f32[128,512]{1,0:T(8,128)S(1)}, f32[128,512]{1,0:T(8,128)S(1)}, u32[]{:S(2)}, u32[]{:S(2)}) collective-permute-start(f32[128,512]{1,0:T(8,128)S(1)} %get-tuple-element.43), channel_id=1, source_target_pairs={{0,2},{1,3},{2,0},{3,1},{4,6},{5,7},{6,4},{7,5},{8,10},{9,11},{10,... | collective-permute-start | bytes 786440 | tf_op jit(solution)/shard_map/ppermute | solution.py:27
  61.9 15.9 %collective-permute-start.17 = (f32[128,512]{1,0:T(8,128)S(1)}, f32[128,512]{1,0:T(8,128)S(1)}, u32[]{:S(2)}, u32[]{:S(2)}) collective-permute-start(f32[128,512]{1,0:T(8,128)S(1)} %get-tuple-element.44), channel_id=1, source_target_pairs={{2,4},{3,5},{4,2},{5,3},{10,12},{11,13},{12,10},{13,11},{18,20},{1... | collective-permute-start | bytes 786440 | tf_op jit(solution)/shard_map/ppermute | solution.py:27
  65.7 14.5 %collective-permute-start.18 = (f32[128,512]{1,0:T(8,128)S(1)}, f32[128,512]{1,0:T(8,128)S(1)}, u32[]{:S(2)}, u32[]{:S(2)}) collective-permute-start(f32[128,512]{1,0:T(8,128)S(1)} %get-tuple-element.45), channel_id=1, source_target_pairs={{1,2},{2,1},{3,4},{4,3},{5,6},{6,5},{9,10},{10,9},{11,12},{12,11},... | collective-permute-start | bytes 786440 | tf_op jit(solution)/shard_map/ppermute | solution.py:27

commit v6 on v5

--- a/solution.py
+++ b/solution.py
@@ -297,15 +297,15 @@
     )[0]
 
 
-def add_kernel(high_ref, low_ref, base_ref, *refs):
-    rows = base_ref.shape[0]
-    refs[-1][...] = base_ref[...] + times_adj(high_ref, low_ref, rows, stacked(refs[:-1]))
-
-
-def add_received(adj, base, came, after=()):
+def add_kernel(high_ref, low_ref, base_ref, *refs, skip):
+    column = base_ref.shape[0] + skip * BLK
+    refs[-1][...] = base_ref[...] + times_adj(high_ref, low_ref, column, stacked(refs[:-1]))
+
+
+def add_received(adj, base, came, skip, after=()):
     rows, width = base.shape
     return call(
-        add_kernel,
+        functools.partial(add_kernel, skip=skip),
         (*adj, base, *came),
         [VMEM] * (3 + len(came)),
         (vmem(rows, width),),
@@ -438,7 +438,8 @@
     came = [swap(value, *kind) for value, kind in zip(sent, SWAPS)]
     mixed, first_out = own_right(adj, right, first_right, out_left, out_right, after=(handed_left,))
     sent = choose(every, index, got, left)
-    right = hand_on(add_received(adj, mixed, came, after=sent[:1]))
+    mixed = add_received(adj, mixed, came[:final], 0)
+    right = hand_on(add_received(adj, mixed, came[final:], final, after=sent[:1]))
     came = [swap(value, *kind) for value, kind in zip(sent, SWAPS)]
     mixed = own_left(adj, left, handed_left, came[:1])
     known = second_known(beta, adj, mixed, right_term(beta, right, weight), weight, came[1:final])

time: 83.1 us -> 82.6 us (level)
    ppermute x3, waiting for transfers between devices: 9.24 us -> 6.28 us  [hand_on(): lax.ppermute(value, 'segment', [(i, (i + 1) % peers) for i in range(peers)])]
    ppermute x16, waiting for transfers between devices: 13.5 us -> 15.6 us  [swap(): return lax.ppermute(value, 'graph', sorted(pairs))]
    pallas_call x12 -> x13, Pallas kernels: 28.3 us -> 28.6 us  [call(): pl.pallas_call(body, out_shape=outs, in_specs=list(in_specs) + [VMEM] * l...]
  transfers between devices with their start and end apart: 19 -> 19, of which waited for: 8 -> 10; matrix products, arithmetic and copies ran while one was open for 0% -> 0% of each run, Pallas kernels for 28% -> 29%
where the time goes in v6:
time: 82.6 us; the launch traced here: 82.2 us
  starting transfers between devices  30.4 us (37%)
  Pallas kernels  28.6 us (35%)
  waiting for transfers between devices  21.9 us (27%)
  between operations  1.25 us (2%)
    ppermute x16, starting transfers between devices, swap(): return lax.ppermute(value, 'graph', sorted(pairs))  30.1 us
    pallas_call x13, Pallas kernels, call(): pl.pallas_call(body, out_shape=outs, in_specs=list(in_specs) + [VMEM] * l...  28.6 us
    ppermute x16, waiting for transfers between devices, swap(): return lax.ppermute(value, 'graph', sorted(pairs))  15.6 us
    ppermute x3, waiting for transfers between devices, hand_on(): lax.ppermute(value, 'segment', [(i, (i + 1) % peers) for i in range(peers)])  6.28 us
  transfers between devices with their start and end apart: 19, of which 10 were waited for; matrix products, arithmetic and copies ran while one was open for 0% of the time, Pallas kernels for 29%

profile of v6, /device:TPU:16, one launch (start us, length us, event | category | flops | bytes accessed | tf_op | source)
XLA Modules:
  0.0 82.2 jit_solution(3142327741837627697)
XLA Ops:
  0.7 3.4 %collective-permute-start = (s32[4]{0:T(128)}, s32[4]{0:T(128)S(1)}, u32[]{:S(2)}, u32[]{:S(2)}) collective-permute-start(s32[4]{0:T(128)} %bitcast.28), channel_id=1, source_target_pairs={{1,2},{2,1},{3,4},{4,3},{5,6},{6,5},{9,10},{10,9},{11,12},{12,11},... | collective-permute-start | bytes 56 | tf_op jit(solution)/shard_map/ppermute | solution.py:27
  4.1 1.7 %collective-permute-start.1 = (s32[4]{0:T(128)}, s32[4]{0:T(128)S(1)}, u32[]{:S(2)}, u32[]{:S(2)}) collective-permute-start(s32[4]{0:T(128)} %bitcast.29), channel_id=1, source_target_pairs={{0,1},{1,0},{2,3},{3,2},{4,5},{5,4},{6,7},{7,6},{8,9},{9,8},{10,11... | collective-permute-start | bytes 56 | tf_op jit(solution)/shard_map/ppermute | solution.py:27
  5.8 2.8 %collective-permute-start.3 = (s32[4]{0:T(128)}, s32[4]{0:T(128)S(1)}, u32[]{:S(2)}, u32[]{:S(2)}) collective-permute-start(s32[4]{0:T(128)} %bitcast.31), channel_id=1, source_target_pairs={{2,4},{3,5},{4,2},{5,3},{10,12},{11,13},{12,10},{13,11},{18,20},{1... | collective-permute-start | bytes 56 | tf_op jit(solution)/shard_map/ppermute | solution.py:27
  8.8 0.7 collective-permute-done.2.refs_2_.refs_4_
  9.5 1.9 %collective-permute-done.3.refs_3_.refs_5_ = s32[4]{0:T(128)S(1)} collective-permute-done((s32[4]{0:T(128)}, s32[4]{0:T(128)S(1)}, u32[]{:S(2)}, u32[]{:S(2)}) %collective-permute-start.3) | collective-permute-done | bytes 48 | tf_op jit(solution)/shard_map/ppermute | solution.py:27
  11.4 2.0 %shard_map.95 = (f32[128,1024]{1,0:T(8,128)S(1)}, f32[128,1024]{1,0:T(8,128)S(1)}, f32[128,1024]{1,0:T(8,128)S(1)}) custom-call(s32[4]{0:T(128)S(1)} %get-tuple-element.47.refs_0_.refs_3_.refs_2_, s32[4]{0:T(128)S(1)} %collective-permute-done.1.refs_1_.refs_3_, s32[4]{0:T(128)S(1)} %collective-permute-done.2.refs_2_.refs_4_, ...), custom_call_target="tpu_custom_call" | custom-call | bytes 3145728 | tf_op jit(solution)/shard_map/pallas_call | solution.py:51
  13.3 2.0 %collective-permute-start.4 = (f32[128,1024]{1,0:T(8,128)S(1)}, f32[128,1024]{1,0:T(8,128)S(1)}, u32[]{:S(2)}, u32[]{:S(2)}) collective-permute-start(f32[128,1024]{1,0:T(8,128)S(1)} %get-tuple-element.24.refs_10_), channel_id=1, source_target_pairs={{0,1},{1,0},{2,3},{3,2},{4,5},{5,4},{6,7},{7,6},{8,9},{9,8},{10,11... | collective-permute-start | bytes 1572872 | tf_op jit(solution)/shard_map/ppermute | solution.py:27
  15.4 1.9 %collective-permute-start.6 = (f32[128,1024]{1,0:T(8,128)S(1)}, f32[128,1024]{1,0:T(8,128)S(1)}, u32[]{:S(2)}, u32[]{:S(2)}) collective-permute-start(f32[128,1024]{1,0:T(8,128)S(1)} %get-tuple-element.28), channel_id=1, source_target_pairs={{2,4},{3,5},{4,2},{5,3},{10,12},{11,13},{12,10},{13,11},{18,20},{1... | collective-permute-start | bytes 1572872 | tf_op jit(solution)/shard_map/ppermute | solution.py:27
  17.4 3.3 %shard_map.96 = (bf16[512,1024]{1,0:T(8,128)(2,1)S(1)}, bf16[512,1024]{1,0:T(8,128)(2,1)S(1)}, f32[128,1024]{1,0:T(8,128)S(1)}, f32[512,512]{1,0:T(8,128)S(1)}, f32[512,512]{1,0:T(8,128)S(1)}) custom-call(s32[4]{0:T(128)S(1)} %get-tuple-element.46.refs_0_, s32[4,4]{1,0:T(4,128)S(1)} %copy-done.1, s32[4]{0:T(128)S(1)} %copy-done.2, ...), custom_call_target="tpu_custom_call" | custom-call | bytes 3145728 | tf_op jit(solution)/shard_map/pallas_call | solution.py:51
  20.7 3.5 %collective-permute-start.7 = (f32[128,1024]{1,0:T(8,128)S(1)}, f32[128,1024]{1,0:T(8,128)S(1)}, u32[]{:S(2)}, u32[]{:S(2)}) collective-permute-start(f32[128,1024]{1,0:T(8,128)S(1)} %get-tuple-element.31), channel_id=1, source_target_pairs={{1,2},{2,1},{3,4},{4,3},{5,6},{6,5},{9,10},{10,9},{11,12},{12,11},... | collective-permute-start | bytes 1572872 | tf_op jit(solution)/shard_map/ppermute | solution.py:27
  24.2 4.2 %shard_map.97.refs_4_ = f32[512,1024]{1,0:T(8,128)S(1)} custom-call(bf16[512,1024]{1,0:T(8,128)(2,1)S(1)} %get-tuple-element.25.refs_0_.refs_1_.refs_7_, bf16[512,1024]{1,0:T(8,128)(2,1)S(1)} %get-tuple-element.26.refs_1_.refs_2_.refs_8_, f32[512,1024]{1,0:T(8,128)} %bitcast.23, f32[512,1024]{1,0:T(8,128)} %bitcast.25), custom_call_target="tpu_custom_call" | custom-call | flops 1610612736 | bytes 6291456 | tf_op jit(solution)/shard_map/pallas_call | solution.py:51
  28.5 1.8 %collective-permute-done.5.refs_6_ = f32[128,1024]{1,0:T(8,128)S(1)} collective-permute-done((f32[128,1024]{1,0:T(8,128)S(1)}, f32[128,1024]{1,0:T(8,128)S(1)}, u32[]{:S(2)}, u32[]{:S(2)}) %collective-permute-start.5) | collective-permute-done | bytes 524320 | tf_op jit(solution)/shard_map/ppermute | solution.py:27
  30.2 5.0 %shard_map.98.refs_9_ = f32[512,1024]{1,0:T(8,128)S(1)} custom-call(f32[1]{0:T(128)} %bitcast.12.refs_0_, bf16[512,1024]{1,0:T(8,128)(2,1)S(1)} %get-tuple-element.25.refs_0_.refs_1_.refs_7_, bf16[512,1024]{1,0:T(8,128)(2,1)S(1)} %get-tuple-element.26.refs_1_.refs_2_.refs_8_, f32[1024,1024]{1,0:T(8,128)S(1)} %bitcast.16, f32[512,1024]{1,0:T(8,128)S(1)} %shard_map.97.refs_4_, ...), custom_call_target="tpu_custom_call" | custom-call | flops 4429185024 | bytes 8388608 | tf_op jit(solution)/shard_map/pallas_call | solution.py:51
  35.2 4.5 %collective-permute-done.7.refs_13_ = f32[128,1024]{1,0:T(8,128)S(1)} collective-permute-done((f32[128,1024]{1,0:T(8,128)S(1)}, f32[128,1024]{1,0:T(8,128)S(1)}, u32[]{:S(2)}, u32[]{:S(2)}) %collective-permute-start.7) | collective-permute-done | bytes 524320 | tf_op jit(solution)/shard_map/ppermute | solution.py:27
  39.7 3.0 %shard_map.99 = (f32[512,512]{1,0:T(8,128)S(1)}, f32[512,512]{1,0:T(8,128)S(1)}, f32[512,512]{1,0:T(8,128)S(1)}, f32[512,512]{1,0:T(8,128)S(1)}, f32[128,512]{1,...) custom-call(f32[1]{0:T(128)} %bitcast.12.refs_0_, ...), custom_call_target="tpu_custom_call" | custom-call | flops 1207959552 | bytes 16777216 | tf_op jit(solution)/shard_map/pallas_call | solution.py:51
  42.9 3.7 %collective-permute-start.13 = (f32[128,512]{1,0:T(8,128)S(1)}, f32[128,512]{1,0:T(8,128)S(1)}, u32[]{:S(2)}, u32[]{:S(2)}) collective-permute-start(f32[128,512]{1,0:T(8,128)S(1)} %get-tuple-element.41), channel_id=1, source_target_pairs={{2,4},{3,5},{4,2},{5,3},{10,12},{11,13},{12,10},{13,11},{18,20},{1... | collective-permute-start | bytes 786440 | tf_op jit(solution)/shard_map/ppermute | solution.py:27
  46.7 3.5 %collective-permute-start.14 = (f32[128,512]{1,0:T(8,128)S(1)}, f32[128,512]{1,0:T(8,128)S(1)}, u32[]{:S(2)}, u32[]{:S(2)}) collective-permute-start(f32[128,512]{1,0:T(8,128)S(1)} %get-tuple-element.42), channel_id=1, source_target_pairs={{1,2},{2,1},{3,4},{4,3},{5,6},{6,5},{9,10},{10,9},{11,12},{12,11},... | collective-permute-start | bytes 786440 | tf_op jit(solution)/shard_map/ppermute | solution.py:27
  50.1 1.4 %shard_map.100 = (f32[512,512]{1,0:T(8,128)S(1)}, f32[512,1024]{1,0:T(8,128)}) custom-call(bf16[512,1024]{1,0:T(8,128)(2,1)S(1)} %get-tuple-element.25.refs_0_.refs_1_.refs_7_, bf16[512,1024]{1,0:T(8,128)(2,1)S(1)} %get-tuple-element.26.refs_1_.refs_2_.refs_8_, f32[512,512]{1,0:T(8,128)S(1)} %get-tuple-element.32.refs_2_, ...), custom_call_target="tpu_custom_call" | custom-call | flops 805306368 | bytes 7340032 | tf_op jit(solution)/shard_map/pallas_call | solution.py:51
  51.7 1.9 %collective-permute-done.13.refs_5_ = f32[128,512]{1,0:T(8,128)S(1)} collective-permute-done((f32[128,512]{1,0:T(8,128)S(1)}, f32[128,512]{1,0:T(8,128)S(1)}, u32[]{:S(2)}, u32[]{:S(2)}) %collective-permute-start.13) | collective-permute-done | bytes 262176 | tf_op jit(solution)/shard_map/ppermute | solution.py:27
  53.6 0.9 %shard_map.103.refs_2_ = f32[512,512]{1,0:T(8,128)S(1)} custom-call(bf16[512,1024]{1,0:T(8,128)(2,1)S(1)} %get-tuple-element.25.refs_0_.refs_1_.refs_7_, bf16[512,1024]{1,0:T(8,128)(2,1)S(1)} %get-tuple-element.26.refs_1_.refs_2_.refs_8_, f32[512,512]{1,0:T(8,128)S(1)} %get-tuple-element.38.refs_2_, f32[128,512]{1,0:T(8,128)S(1)} %collective-permute-done.11.refs_3_, ...), custom_call_target="tpu_custom_call" | custom-call | flops 603979776 | bytes 2097152 | tf_op jit(solution)/shard_map/pallas_call | solution.py:51
  54.5 2.5 %collective-permute-done.9.refs_5_.refs_2_ = f32[512,512]{1,0:T(8,128)S(1)} collective-permute-done((f32[512,512]{1,0:T(8,128)S(1)}, f32[512,512]{1,0:T(8,128)S(1)}, u32[]{:S(2)}, u32[]{:S(2)}) %collective-permute-start.9) | collective-permute-done | bytes 1048608 | tf_op jit(solution)/shard_map/ppermute | solution.py:32
  57.0 0.6 shard_map.101
  57.6 3.1 %collective-permute-done.14.refs_3_ = f32[128,512]{1,0:T(8,128)S(1)} collective-permute-done((f32[128,512]{1,0:T(8,128)S(1)}, f32[128,512]{1,0:T(8,128)S(1)}, u32[]{:S(2)}, u32[]{:S(2)}) %collective-permute-start.14) | collective-permute-done | bytes 262176 | tf_op jit(solution)/shard_map/ppermute | solution.py:27
  60.7 0.4 shard_map.104
  61.4 3.8 %collective-permute-start.17 = (f32[128,512]{1,0:T(8,128)S(1)}, f32[128,512]{1,0:T(8,128)S(1)}, u32[]{:S(2)}, u32[]{:S(2)}) collective-permute-start(f32[128,512]{1,0:T(8,128)S(1)} %get-tuple-element.44), channel_id=1, source_target_pairs={{2,4},{3,5},{4,2},{5,3},{10,12},{11,13},{12,10},{13,11},{18,20},{1... | collective-permute-start | bytes 786440 | tf_op jit(solution)/shard_map/ppermute | solution.py:27
  65.2 3.6 %collective-permute-start.18 = (f32[128,512]{1,0:T(8,128)S(1)}, f32[128,512]{1,0:T(8,128)S(1)}, u32[]{:S(2)}, u32[]{:S(2)}) collective-permute-start(f32[128,512]{1,0:T(8,128)S(1)} %get-tuple-element.45), channel_id=1, source_target_pairs={{1,2},{2,1},{3,4},{4,3},{5,6},{6,5},{9,10},{10,9},{11,12},{12,11},... | collective-permute-start | bytes 786440 | tf_op jit(solution)/shard_map/ppermute | solution.py:27
  68.8 1.6 %collective-permute-done.10.refs_4_ = f32[128,512]{1,0:T(8,128)S(1)} collective-permute-done((f32[128,512]{1,0:T(8,128)S(1)}, f32[128,512]{1,0:T(8,128)S(1)}, u32[]{:S(2)}, u32[]{:S(2)}) %collective-permute-start.10) | collective-permute-done | bytes 262176 | tf_op jit(solution)/shard_map/ppermute | solution.py:27
  70.4 1.3 %shard_map.102.refs_3_ = f32[512,512]{1,0:T(8,128)S(1)} custom-call(bf16[512,1024]{1,0:T(8,128)(2,1)S(1)} %get-tuple-element.25.refs_0_.refs_1_.refs_7_, bf16[512,1024]{1,0:T(8,128)(2,1)S(1)} %get-tuple-element.26.refs_1_.refs_2_.refs_8_, f32[512,512]{1,0:T(8,128)S(1)} %collective-permute-done.9.refs_5_.refs_2_, ...), custom_call_target="tpu_custom_call" | custom-call | flops 805306368 | bytes 3145728 | tf_op jit(solution)/shard_map/pallas_call | solution.py:51
  71.6 3.8 %collective-permute-done.15.refs_1_ = f32[512,512]{1,0:T(8,128)S(1)} collective-permute-done((f32[512,512]{1,0:T(8,128)S(1)}, f32[512,512]{1,0:T(8,128)S(1)}, u32[]{:S(2)}, u32[]{:S(2)}) %collective-permute-start.15) | collective-permute-done | bytes 1048608 | tf_op jit(solution)/shard_map/ppermute | solution.py:32
  75.4 1.8 %shard_map.105.refs_4_ = f32[512,1024]{1,0:T(8,128)S(1)} custom-call(f32[1]{0:T(128)} %bitcast.12.refs_0_, f32[512,512]{1,0:T(8,128)S(1)} %collective-permute-done.15.refs_1_, f32[1024,1024]{1,0:T(8,128)S(1)} %bitcast.18), custom_call_target="tpu_custom_call" | custom-call | flops 1610612736 | bytes 6291456 | tf_op jit(solution)/shard_map/pallas_call | solution.py:51
  77.3 2.3 %shard_map.106.refs_3_ = f32[512,1024]{1,0:T(8,128)S(1)} custom-call(f32[1]{0:T(128)} %bitcast.12.refs_0_, bf16[512,1024]{1,0:T(8,128)(2,1)S(1)} %get-tuple-element.25.refs_0_.refs_1_.refs_7_, bf16[512,1024]{1,0:T(8,128)(2,1)S(1)} %get-tuple-element.26.refs_1_.refs_2_.refs_8_, f32[512,512]{1,0:T(8,128)S(1)} %shard_map.102.refs_3_, ...), custom_call_target="tpu_custom_call" | custom-call | flops 2013265920 | bytes 8388608 | tf_op jit(solution)/shard_map/pallas_call | solution.py:51
  79.6 2.4 %shard_map.107 = f32[512,1024]{1,0:T(8,128)} custom-call(f32[1]{0:T(128)} %bitcast.12.refs_0_, bf16[512,1024]{1,0:T(8,128)(2,1)S(1)} %get-tuple-element.25.refs_0_.refs_1_.refs_7_, bf16[512,1024]{1,0:T(8,128)(2,1)S(1)} %get-tuple-element.26.refs_1_.refs_2_.refs_8_, f32[512,1024]{1,0:T(8,128)S(1)} %shard_map.106.refs_3_, f32[1024,1024]{1,0:T(8,128)S(1)} %bitcast.20, ...), custom_call_target="tpu_custom_call" | custom-call | flops 805306368 | bytes 8388608 | tf_op jit(solution)/shard_map/pallas_call | solution.py:51
  (26 shorter events, 0.8 us)
Async XLA Ops:
  0.6 16.7 %copy-start.1 = (s32[4,4]{1,0:T(4,128)S(1)}, s32[4,4]{1,0:T(4,128)}, u32[]{:S(2)}) copy-start(s32[4,4]{1,0:T(4,128)} %refs_1_.1) | copy-start | bytes 196
  0.6 16.7 %copy-start.2 = (s32[4]{0:T(128)S(1)}, s32[4]{0:T(128)}, u32[]{:S(2)}) copy-start(s32[4]{0:T(128)} %refs_2_.1) | copy-start | bytes 52
  0.7 8.1 %collective-permute-start = (s32[4]{0:T(128)}, s32[4]{0:T(128)S(1)}, u32[]{:S(2)}, u32[]{:S(2)}) collective-permute-start(s32[4]{0:T(128)} %bitcast.28), channel_id=1, source_target_pairs={{1,2},{2,1},{3,4},{4,3},{5,6},{6,5},{9,10},{10,9},{11,12},{12,11},... | collective-permute-start | bytes 56 | tf_op jit(solution)/shard_map/ppermute | solution.py:27
  4.1 4.7 %collective-permute-start.1 = (s32[4]{0:T(128)}, s32[4]{0:T(128)S(1)}, u32[]{:S(2)}, u32[]{:S(2)}) collective-permute-start(s32[4]{0:T(128)} %bitcast.29), channel_id=1, source_target_pairs={{0,1},{1,0},{2,3},{3,2},{4,5},{5,4},{6,7},{7,6},{8,9},{9,8},{10,11... | collective-permute-start | bytes 56 | tf_op jit(solution)/shard_map/ppermute | solution.py:27
  5.8 3.7 %collective-permute-start.2 = (s32[4]{0:T(128)}, s32[4]{0:T(128)S(1)}, u32[]{:S(2)}, u32[]{:S(2)}) collective-permute-start(s32[4]{0:T(128)} %bitcast.30), channel_id=1, source_target_pairs={{0,2},{1,3},{2,0},{3,1},{4,6},{5,7},{6,4},{7,5},{8,10},{9,11},{10,... | collective-permute-start | bytes 56 | tf_op jit(solution)/shard_map/ppermute | solution.py:27
  5.8 5.6 %collective-permute-start.3 = (s32[4]{0:T(128)}, s32[4]{0:T(128)S(1)}, u32[]{:S(2)}, u32[]{:S(2)}) collective-permute-start(s32[4]{0:T(128)} %bitcast.31), channel_id=1, source_target_pairs={{2,4},{3,5},{4,2},{5,3},{10,12},{11,13},{12,10},{13,11},{18,20},{1... | collective-permute-start | bytes 56 | tf_op jit(solution)/shard_map/ppermute | solution.py:27
  13.3 15.1 %collective-permute-start.4 = (f32[128,1024]{1,0:T(8,128)S(1)}, f32[128,1024]{1,0:T(8,128)S(1)}, u32[]{:S(2)}, u32[]{:S(2)}) collective-permute-start(f32[128,1024]{1,0:T(8,128)S(1)} %get-tuple-element.24.refs_10_), channel_id=1, source_target_pairs={{0,1},{1,0},{2,3},{3,2},{4,5},{5,4},{6,7},{7,6},{8,9},{9,8},{10,11... | collective-permute-start | bytes 1572872 | tf_op jit(solution)/shard_map/ppermute | solution.py:27
  15.4 14.9 %collective-permute-start.5 = (f32[128,1024]{1,0:T(8,128)S(1)}, f32[128,1024]{1,0:T(8,128)S(1)}, u32[]{:S(2)}, u32[]{:S(2)}) collective-permute-start(f32[128,1024]{1,0:T(8,128)S(1)} %get-tuple-element.27), channel_id=1, source_target_pairs={{0,2},{1,3},{2,0},{3,1},{4,6},{5,7},{6,4},{7,5},{8,10},{9,11},{10,... | collective-permute-start | bytes 1572872 | tf_op jit(solution)/shard_map/ppermute | solution.py:27
  15.4 14.9 %collective-permute-start.6 = (f32[128,1024]{1,0:T(8,128)S(1)}, f32[128,1024]{1,0:T(8,128)S(1)}, u32[]{:S(2)}, u32[]{:S(2)}) collective-permute-start(f32[128,1024]{1,0:T(8,128)S(1)} %get-tuple-element.28), channel_id=1, source_target_pairs={{2,4},{3,5},{4,2},{5,3},{10,12},{11,13},{12,10},{13,11},{18,20},{1... | collective-permute-start | bytes 1572872 | tf_op jit(solution)/shard_map/ppermute | solution.py:27
  20.7 19.0 %collective-permute-start.7 = (f32[128,1024]{1,0:T(8,128)S(1)}, f32[128,1024]{1,0:T(8,128)S(1)}, u32[]{:S(2)}, u32[]{:S(2)}) collective-permute-start(f32[128,1024]{1,0:T(8,128)S(1)} %get-tuple-element.31), channel_id=1, source_target_pairs={{1,2},{2,1},{3,4},{4,3},{5,6},{6,5},{9,10},{10,9},{11,12},{12,11},... | collective-permute-start | bytes 1572872 | tf_op jit(solution)/shard_map/ppermute | solution.py:27
  24.2 22.5 %collective-permute-start.8 = (f32[512,512]{1,0:T(8,128)S(1)}, f32[512,512]{1,0:T(8,128)S(1)}, u32[]{:S(2)}, u32[]{:S(2)}) collective-permute-start(f32[512,512]{1,0:T(8,128)S(1)} %get-tuple-element.29.refs_11_), channel_id=1, source_target_pairs={{0,8},{8,16},{16,24},{24,0},{1,9},{9,17},{17,25},{25,1},{2,10},{10... | collective-permute-start | bytes 3145736 | tf_op jit(solution)/shard_map/ppermute | solution.py:32
  24.2 6.0 %copy-start = (f32[1,1024,1024]{2,1,0:T(8,128)S(1)}, f32[1,1024,1024]{2,1,0:T(8,128)}, u32[]{:S(2)}) copy-start(f32[1,1024,1024]{2,1,0:T(8,128)} %param.11) | copy-start | bytes 12582916
  42.7 14.3 %collective-permute-start.9 = (f32[512,512]{1,0:T(8,128)S(1)}, f32[512,512]{1,0:T(8,128)S(1)}, u32[]{:S(2)}, u32[]{:S(2)}) collective-permute-start(f32[512,512]{1,0:T(8,128)S(1)} %get-tuple-element.36), channel_id=1, source_target_pairs={{0,8},{8,16},{16,24},{24,0},{1,9},{9,17},{17,25},{25,1},{2,10},{10... | collective-permute-start | bytes 3145736 | tf_op jit(solution)/shard_map/ppermute | solution.py:32
  42.8 8.8 %collective-permute-start.11 = (f32[128,512]{1,0:T(8,128)S(1)}, f32[128,512]{1,0:T(8,128)S(1)}, u32[]{:S(2)}, u32[]{:S(2)}) collective-permute-start(f32[128,512]{1,0:T(8,128)S(1)} %get-tuple-element.39), channel_id=1, source_target_pairs={{0,1},{1,0},{2,3},{3,2},{4,5},{5,4},{6,7},{7,6},{8,9},{9,8},{10,11... | collective-permute-start | bytes 786440 | tf_op jit(solution)/shard_map/ppermute | solution.py:27
  42.8 8.8 %collective-permute-start.12 = (f32[128,512]{1,0:T(8,128)S(1)}, f32[128,512]{1,0:T(8,128)S(1)}, u32[]{:S(2)}, u32[]{:S(2)}) collective-permute-start(f32[128,512]{1,0:T(8,128)S(1)} %get-tuple-element.40), channel_id=1, source_target_pairs={{0,2},{1,3},{2,0},{3,1},{4,6},{5,7},{6,4},{7,5},{8,10},{9,11},{10,... | collective-permute-start | bytes 786440 | tf_op jit(solution)/shard_map/ppermute | solution.py:27
  42.9 10.7 %collective-permute-start.13 = (f32[128,512]{1,0:T(8,128)S(1)}, f32[128,512]{1,0:T(8,128)S(1)}, u32[]{:S(2)}, u32[]{:S(2)}) collective-permute-start(f32[128,512]{1,0:T(8,128)S(1)} %get-tuple-element.41), channel_id=1, source_target_pairs={{2,4},{3,5},{4,2},{5,3},{10,12},{11,13},{12,10},{13,11},{18,20},{1... | collective-permute-start | bytes 786440 | tf_op jit(solution)/shard_map/ppermute | solution.py:27
  46.7 14.0 %collective-permute-start.14 = (f32[128,512]{1,0:T(8,128)S(1)}, f32[128,512]{1,0:T(8,128)S(1)}, u32[]{:S(2)}, u32[]{:S(2)}) collective-permute-start(f32[128,512]{1,0:T(8,128)S(1)} %get-tuple-element.42), channel_id=1, source_target_pairs={{1,2},{2,1},{3,4},{4,3},{5,6},{6,5},{9,10},{10,9},{11,12},{12,11},... | collective-permute-start | bytes 786440 | tf_op jit(solution)/shard_map/ppermute | solution.py:27
  61.1 14.3 %collective-permute-start.15 = (f32[512,512]{1,0:T(8,128)S(1)}, f32[512,512]{1,0:T(8,128)S(1)}, u32[]{:S(2)}, u32[]{:S(2)}) collective-permute-start(f32[512,512]{1,0:T(8,128)S(1)} %shard_map.104), channel_id=1, source_target_pairs={{0,8},{8,16},{16,24},{24,0},{1,9},{9,17},{17,25},{25,1},{2,10},{10... | collective-permute-start | bytes 3145736 | tf_op jit(solution)/shard_map/ppermute | solution.py:32
  61.3 9.1 %collective-permute-start.10 = (f32[128,512]{1,0:T(8,128)S(1)}, f32[128,512]{1,0:T(8,128)S(1)}, u32[]{:S(2)}, u32[]{:S(2)}) collective-permute-start(f32[128,512]{1,0:T(8,128)S(1)} %get-tuple-element.37.refs_4_), channel_id=1, source_target_pairs={{0,1},{1,0},{2,3},{3,2},{4,5},{5,4},{6,7},{7,6},{8,9},{9,8},{10,11... | collective-permute-start | bytes 786440 | tf_op jit(solution)/shard_map/ppermute | solution.py:27
  61.3 16.0 %collective-permute-start.16 = (f32[128,512]{1,0:T(8,128)S(1)}, f32[128,512]{1,0:T(8,128)S(1)}, u32[]{:S(2)}, u32[]{:S(2)}) collective-permute-start(f32[128,512]{1,0:T(8,128)S(1)} %get-tuple-element.43), channel_id=1, source_target_pairs={{0,2},{1,3},{2,0},{3,1},{4,6},{5,7},{6,4},{7,5},{8,10},{9,11},{10,... | collective-permute-start | bytes 786440 | tf_op jit(solution)/shard_map/ppermute | solution.py:27
  61.4 15.9 %collective-permute-start.17 = (f32[128,512]{1,0:T(8,128)S(1)}, f32[128,512]{1,0:T(8,128)S(1)}, u32[]{:S(2)}, u32[]{:S(2)}) collective-permute-start(f32[128,512]{1,0:T(8,128)S(1)} %get-tuple-element.44), channel_id=1, source_target_pairs={{2,4},{3,5},{4,2},{5,3},{10,12},{11,13},{12,10},{13,11},{18,20},{1... | collective-permute-start | bytes 786440 | tf_op jit(solution)/shard_map/ppermute | solution.py:27
  65.2 14.5 %collective-permute-start.18 = (f32[128,512]{1,0:T(8,128)S(1)}, f32[128,512]{1,0:T(8,128)S(1)}, u32[]{:S(2)}, u32[]{:S(2)}) collective-permute-start(f32[128,512]{1,0:T(8,128)S(1)} %get-tuple-element.45), channel_id=1, source_target_pairs={{1,2},{2,1},{3,4},{4,3},{5,6},{6,5},{9,10},{10,9},{11,12},{12,11},... | collective-permute-start | bytes 786440 | tf_op jit(solution)/shard_map/ppermute | solution.py:27

commit v7 on v6

--- a/solution.py
+++ b/solution.py
@@ -381,7 +381,7 @@
         copy.wait()
 
 
-def second_layer(beta, adj, base, weight, came, tile=256):
+def second_layer(beta, adj, base, weight, came, tile=512):
     rows, width = base.shape
     half = came.shape[1]
     return call(

time: 82.6 us -> 82.9 us (level)
  no operation moved by 1% of the time
where the time goes in v7:
time: 82.9 us; the launch traced here: 82.5 us
  starting transfers between devices  30.4 us (37%)
  Pallas kernels  28.9 us (35%)
  waiting for transfers between devices  21.9 us (26%)
  between operations  1.25 us (2%)
    ppermute x16, starting transfers between devices, swap(): return lax.ppermute(value, 'graph', sorted(pairs))  30.1 us
    pallas_call x13, Pallas kernels, call(): pl.pallas_call(body, out_shape=outs, in_specs=list(in_specs) + [VMEM] * l...  28.9 us
    ppermute x16, waiting for transfers between devices, swap(): return lax.ppermute(value, 'graph', sorted(pairs))  15.6 us
    ppermute x3, waiting for transfers between devices, hand_on(): lax.ppermute(value, 'segment', [(i, (i + 1) % peers) for i in range(peers)])  6.28 us
  transfers between devices with their start and end apart: 19, of which 10 were waited for; matrix products, arithmetic and copies ran while one was open for 0% of the time, Pallas kernels for 29%

profile of v7, /device:TPU:16, one launch (start us, length us, event | category | flops | bytes accessed | tf_op | source)
XLA Modules:
  0.0 82.5 jit_solution(12147592078957878946)
XLA Ops:
  0.7 3.4 %collective-permute-start = (s32[4]{0:T(128)}, s32[4]{0:T(128)S(1)}, u32[]{:S(2)}, u32[]{:S(2)}) collective-permute-start(s32[4]{0:T(128)} %bitcast.28), channel_id=1, source_target_pairs={{1,2},{2,1},{3,4},{4,3},{5,6},{6,5},{9,10},{10,9},{11,12},{12,11},... | collective-permute-start | bytes 56 | tf_op jit(solution)/shard_map/ppermute | solution.py:27
  4.1 1.7 %collective-permute-start.1 = (s32[4]{0:T(128)}, s32[4]{0:T(128)S(1)}, u32[]{:S(2)}, u32[]{:S(2)}) collective-permute-start(s32[4]{0:T(128)} %bitcast.29), channel_id=1, source_target_pairs={{0,1},{1,0},{2,3},{3,2},{4,5},{5,4},{6,7},{7,6},{8,9},{9,8},{10,11... | collective-permute-start | bytes 56 | tf_op jit(solution)/shard_map/ppermute | solution.py:27
  5.8 2.8 %collective-permute-start.3 = (s32[4]{0:T(128)}, s32[4]{0:T(128)S(1)}, u32[]{:S(2)}, u32[]{:S(2)}) collective-permute-start(s32[4]{0:T(128)} %bitcast.31), channel_id=1, source_target_pairs={{2,4},{3,5},{4,2},{5,3},{10,12},{11,13},{12,10},{13,11},{18,20},{1... | collective-permute-start | bytes 56 | tf_op jit(solution)/shard_map/ppermute | solution.py:27
  8.8 0.7 collective-permute-done.2.refs_2_.refs_4_
  9.5 1.9 %collective-permute-done.3.refs_3_.refs_5_ = s32[4]{0:T(128)S(1)} collective-permute-done((s32[4]{0:T(128)}, s32[4]{0:T(128)S(1)}, u32[]{:S(2)}, u32[]{:S(2)}) %collective-permute-start.3) | collective-permute-done | bytes 48 | tf_op jit(solution)/shard_map/ppermute | solution.py:27
  11.4 2.0 %shard_map.95 = (f32[128,1024]{1,0:T(8,128)S(1)}, f32[128,1024]{1,0:T(8,128)S(1)}, f32[128,1024]{1,0:T(8,128)S(1)}) custom-call(s32[4]{0:T(128)S(1)} %get-tuple-element.47.refs_0_.refs_3_.refs_2_, s32[4]{0:T(128)S(1)} %collective-permute-done.1.refs_1_.refs_3_, s32[4]{0:T(128)S(1)} %collective-permute-done.2.refs_2_.refs_4_, ...), custom_call_target="tpu_custom_call" | custom-call | bytes 3145728 | tf_op jit(solution)/shard_map/pallas_call | solution.py:51
  13.4 2.0 %collective-permute-start.4 = (f32[128,1024]{1,0:T(8,128)S(1)}, f32[128,1024]{1,0:T(8,128)S(1)}, u32[]{:S(2)}, u32[]{:S(2)}) collective-permute-start(f32[128,1024]{1,0:T(8,128)S(1)} %get-tuple-element.24.refs_10_), channel_id=1, source_target_pairs={{0,1},{1,0},{2,3},{3,2},{4,5},{5,4},{6,7},{7,6},{8,9},{9,8},{10,11... | collective-permute-start | bytes 1572872 | tf_op jit(solution)/shard_map/ppermute | solution.py:27
  15.4 1.9 %collective-permute-start.6 = (f32[128,1024]{1,0:T(8,128)S(1)}, f32[128,1024]{1,0:T(8,128)S(1)}, u32[]{:S(2)}, u32[]{:S(2)}) collective-permute-start(f32[128,1024]{1,0:T(8,128)S(1)} %get-tuple-element.28), channel_id=1, source_target_pairs={{2,4},{3,5},{4,2},{5,3},{10,12},{11,13},{12,10},{13,11},{18,20},{1... | collective-permute-start | bytes 1572872 | tf_op jit(solution)/shard_map/ppermute | solution.py:27
  17.4 3.3 %shard_map.96 = (bf16[512,1024]{1,0:T(8,128)(2,1)S(1)}, bf16[512,1024]{1,0:T(8,128)(2,1)S(1)}, f32[128,1024]{1,0:T(8,128)S(1)}, f32[512,512]{1,0:T(8,128)S(1)}, f32[512,512]{1,0:T(8,128)S(1)}) custom-call(s32[4]{0:T(128)S(1)} %get-tuple-element.46.refs_0_, s32[4,4]{1,0:T(4,128)S(1)} %copy-done.1, s32[4]{0:T(128)S(1)} %copy-done.2, ...), custom_call_target="tpu_custom_call" | custom-call | bytes 3145728 | tf_op jit(solution)/shard_map/pallas_call | solution.py:51
  20.7 3.5 %collective-permute-start.7 = (f32[128,1024]{1,0:T(8,128)S(1)}, f32[128,1024]{1,0:T(8,128)S(1)}, u32[]{:S(2)}, u32[]{:S(2)}) collective-permute-start(f32[128,1024]{1,0:T(8,128)S(1)} %get-tuple-element.31), channel_id=1, source_target_pairs={{1,2},{2,1},{3,4},{4,3},{5,6},{6,5},{9,10},{10,9},{11,12},{12,11},... | collective-permute-start | bytes 1572872 | tf_op jit(solution)/shard_map/ppermute | solution.py:27
  24.2 4.2 %shard_map.97.refs_4_ = f32[512,1024]{1,0:T(8,128)S(1)} custom-call(bf16[512,1024]{1,0:T(8,128)(2,1)S(1)} %get-tuple-element.25.refs_0_.refs_1_.refs_7_, bf16[512,1024]{1,0:T(8,128)(2,1)S(1)} %get-tuple-element.26.refs_1_.refs_2_.refs_8_, f32[512,1024]{1,0:T(8,128)} %bitcast.23, f32[512,1024]{1,0:T(8,128)} %bitcast.25), custom_call_target="tpu_custom_call" | custom-call | flops 1610612736 | bytes 6291456 | tf_op jit(solution)/shard_map/pallas_call | solution.py:51
  28.5 1.7 %collective-permute-done.5.refs_6_ = f32[128,1024]{1,0:T(8,128)S(1)} collective-permute-done((f32[128,1024]{1,0:T(8,128)S(1)}, f32[128,1024]{1,0:T(8,128)S(1)}, u32[]{:S(2)}, u32[]{:S(2)}) %collective-permute-start.5) | collective-permute-done | bytes 524320 | tf_op jit(solution)/shard_map/ppermute | solution.py:27
  30.2 5.0 %shard_map.98.refs_9_ = f32[512,1024]{1,0:T(8,128)S(1)} custom-call(f32[1]{0:T(128)} %bitcast.12.refs_0_, bf16[512,1024]{1,0:T(8,128)(2,1)S(1)} %get-tuple-element.25.refs_0_.refs_1_.refs_7_, bf16[512,1024]{1,0:T(8,128)(2,1)S(1)} %get-tuple-element.26.refs_1_.refs_2_.refs_8_, f32[1024,1024]{1,0:T(8,128)S(1)} %bitcast.16, f32[512,1024]{1,0:T(8,128)S(1)} %shard_map.97.refs_4_, ...), custom_call_target="tpu_custom_call" | custom-call | flops 4429185024 | bytes 8388608 | tf_op jit(solution)/shard_map/pallas_call | solution.py:51
  35.2 4.5 %collective-permute-done.7.refs_13_ = f32[128,1024]{1,0:T(8,128)S(1)} collective-permute-done((f32[128,1024]{1,0:T(8,128)S(1)}, f32[128,1024]{1,0:T(8,128)S(1)}, u32[]{:S(2)}, u32[]{:S(2)}) %collective-permute-start.7) | collective-permute-done | bytes 524320 | tf_op jit(solution)/shard_map/ppermute | solution.py:27
  39.7 3.0 %shard_map.99 = (f32[512,512]{1,0:T(8,128)S(1)}, f32[512,512]{1,0:T(8,128)S(1)}, f32[512,512]{1,0:T(8,128)S(1)}, f32[512,512]{1,0:T(8,128)S(1)}, f32[128,512]{1,...) custom-call(f32[1]{0:T(128)} %bitcast.12.refs_0_, ...), custom_call_target="tpu_custom_call" | custom-call | flops 1207959552 | bytes 16777216 | tf_op jit(solution)/shard_map/pallas_call | solution.py:51
  42.9 3.7 %collective-permute-start.13 = (f32[128,512]{1,0:T(8,128)S(1)}, f32[128,512]{1,0:T(8,128)S(1)}, u32[]{:S(2)}, u32[]{:S(2)}) collective-permute-start(f32[128,512]{1,0:T(8,128)S(1)} %get-tuple-element.41), channel_id=1, source_target_pairs={{2,4},{3,5},{4,2},{5,3},{10,12},{11,13},{12,10},{13,11},{18,20},{1... | collective-permute-start | bytes 786440 | tf_op jit(solution)/shard_map/ppermute | solution.py:27
  46.7 3.5 %collective-permute-start.14 = (f32[128,512]{1,0:T(8,128)S(1)}, f32[128,512]{1,0:T(8,128)S(1)}, u32[]{:S(2)}, u32[]{:S(2)}) collective-permute-start(f32[128,512]{1,0:T(8,128)S(1)} %get-tuple-element.42), channel_id=1, source_target_pairs={{1,2},{2,1},{3,4},{4,3},{5,6},{6,5},{9,10},{10,9},{11,12},{12,11},... | collective-permute-start | bytes 786440 | tf_op jit(solution)/shard_map/ppermute | solution.py:27
  50.2 1.4 %shard_map.100 = (f32[512,512]{1,0:T(8,128)S(1)}, f32[512,1024]{1,0:T(8,128)}) custom-call(bf16[512,1024]{1,0:T(8,128)(2,1)S(1)} %get-tuple-element.25.refs_0_.refs_1_.refs_7_, bf16[512,1024]{1,0:T(8,128)(2,1)S(1)} %get-tuple-element.26.refs_1_.refs_2_.refs_8_, f32[512,512]{1,0:T(8,128)S(1)} %get-tuple-element.32.refs_2_, ...), custom_call_target="tpu_custom_call" | custom-call | flops 805306368 | bytes 7340032 | tf_op jit(solution)/shard_map/pallas_call | solution.py:51
  51.7 1.9 %collective-permute-done.13.refs_5_ = f32[128,512]{1,0:T(8,128)S(1)} collective-permute-done((f32[128,512]{1,0:T(8,128)S(1)}, f32[128,512]{1,0:T(8,128)S(1)}, u32[]{:S(2)}, u32[]{:S(2)}) %collective-permute-start.13) | collective-permute-done | bytes 262176 | tf_op jit(solution)/shard_map/ppermute | solution.py:27
  53.6 0.9 %shard_map.103.refs_2_ = f32[512,512]{1,0:T(8,128)S(1)} custom-call(bf16[512,1024]{1,0:T(8,128)(2,1)S(1)} %get-tuple-element.25.refs_0_.refs_1_.refs_7_, bf16[512,1024]{1,0:T(8,128)(2,1)S(1)} %get-tuple-element.26.refs_1_.refs_2_.refs_8_, f32[512,512]{1,0:T(8,128)S(1)} %get-tuple-element.38.refs_2_, f32[128,512]{1,0:T(8,128)S(1)} %collective-permute-done.11.refs_3_, ...), custom_call_target="tpu_custom_call" | custom-call | flops 603979776 | bytes 2097152 | tf_op jit(solution)/shard_map/pallas_call | solution.py:51
  54.5 2.5 %collective-permute-done.9.refs_5_.refs_2_ = f32[512,512]{1,0:T(8,128)S(1)} collective-permute-done((f32[512,512]{1,0:T(8,128)S(1)}, f32[512,512]{1,0:T(8,128)S(1)}, u32[]{:S(2)}, u32[]{:S(2)}) %collective-permute-start.9) | collective-permute-done | bytes 1048608 | tf_op jit(solution)/shard_map/ppermute | solution.py:32
  57.0 0.6 shard_map.101
  57.6 3.1 %collective-permute-done.14.refs_3_ = f32[128,512]{1,0:T(8,128)S(1)} collective-permute-done((f32[128,512]{1,0:T(8,128)S(1)}, f32[128,512]{1,0:T(8,128)S(1)}, u32[]{:S(2)}, u32[]{:S(2)}) %collective-permute-start.14) | collective-permute-done | bytes 262176 | tf_op jit(solution)/shard_map/ppermute | solution.py:27
  60.7 0.4 shard_map.104
  61.4 3.8 %collective-permute-start.17 = (f32[128,512]{1,0:T(8,128)S(1)}, f32[128,512]{1,0:T(8,128)S(1)}, u32[]{:S(2)}, u32[]{:S(2)}) collective-permute-start(f32[128,512]{1,0:T(8,128)S(1)} %get-tuple-element.44), channel_id=1, source_target_pairs={{2,4},{3,5},{4,2},{5,3},{10,12},{11,13},{12,10},{13,11},{18,20},{1... | collective-permute-start | bytes 786440 | tf_op jit(solution)/shard_map/ppermute | solution.py:27
  65.2 3.7 %collective-permute-start.18 = (f32[128,512]{1,0:T(8,128)S(1)}, f32[128,512]{1,0:T(8,128)S(1)}, u32[]{:S(2)}, u32[]{:S(2)}) collective-permute-start(f32[128,512]{1,0:T(8,128)S(1)} %get-tuple-element.45), channel_id=1, source_target_pairs={{1,2},{2,1},{3,4},{4,3},{5,6},{6,5},{9,10},{10,9},{11,12},{12,11},... | collective-permute-start | bytes 786440 | tf_op jit(solution)/shard_map/ppermute | solution.py:27
  68.8 1.6 %collective-permute-done.10.refs_4_ = f32[128,512]{1,0:T(8,128)S(1)} collective-permute-done((f32[128,512]{1,0:T(8,128)S(1)}, f32[128,512]{1,0:T(8,128)S(1)}, u32[]{:S(2)}, u32[]{:S(2)}) %collective-permute-start.10) | collective-permute-done | bytes 262176 | tf_op jit(solution)/shard_map/ppermute | solution.py:27
  70.4 1.3 %shard_map.102.refs_3_ = f32[512,512]{1,0:T(8,128)S(1)} custom-call(bf16[512,1024]{1,0:T(8,128)(2,1)S(1)} %get-tuple-element.25.refs_0_.refs_1_.refs_7_, bf16[512,1024]{1,0:T(8,128)(2,1)S(1)} %get-tuple-element.26.refs_1_.refs_2_.refs_8_, f32[512,512]{1,0:T(8,128)S(1)} %collective-permute-done.9.refs_5_.refs_2_, ...), custom_call_target="tpu_custom_call" | custom-call | flops 805306368 | bytes 3145728 | tf_op jit(solution)/shard_map/pallas_call | solution.py:51
  71.7 3.8 %collective-permute-done.15.refs_1_ = f32[512,512]{1,0:T(8,128)S(1)} collective-permute-done((f32[512,512]{1,0:T(8,128)S(1)}, f32[512,512]{1,0:T(8,128)S(1)}, u32[]{:S(2)}, u32[]{:S(2)}) %collective-permute-start.15) | collective-permute-done | bytes 1048608 | tf_op jit(solution)/shard_map/ppermute | solution.py:32
  75.4 1.8 %shard_map.105.refs_4_ = f32[512,1024]{1,0:T(8,128)S(1)} custom-call(f32[1]{0:T(128)} %bitcast.12.refs_0_, f32[512,512]{1,0:T(8,128)S(1)} %collective-permute-done.15.refs_1_, f32[1024,1024]{1,0:T(8,128)S(1)} %bitcast.18), custom_call_target="tpu_custom_call" | custom-call | flops 1610612736 | bytes 6291456 | tf_op jit(solution)/shard_map/pallas_call | solution.py:51
  77.3 2.3 %shard_map.106.refs_3_ = f32[512,1024]{1,0:T(8,128)S(1)} custom-call(f32[1]{0:T(128)} %bitcast.12.refs_0_, bf16[512,1024]{1,0:T(8,128)(2,1)S(1)} %get-tuple-element.25.refs_0_.refs_1_.refs_7_, bf16[512,1024]{1,0:T(8,128)(2,1)S(1)} %get-tuple-element.26.refs_1_.refs_2_.refs_8_, f32[512,512]{1,0:T(8,128)S(1)} %shard_map.102.refs_3_, ...), custom_call_target="tpu_custom_call" | custom-call | flops 2013265920 | bytes 8388608 | tf_op jit(solution)/shard_map/pallas_call | solution.py:51
  79.7 2.7 %shard_map.107 = f32[512,1024]{1,0:T(8,128)} custom-call(f32[1]{0:T(128)} %bitcast.12.refs_0_, bf16[512,1024]{1,0:T(8,128)(2,1)S(1)} %get-tuple-element.25.refs_0_.refs_1_.refs_7_, bf16[512,1024]{1,0:T(8,128)(2,1)S(1)} %get-tuple-element.26.refs_1_.refs_2_.refs_8_, f32[512,1024]{1,0:T(8,128)S(1)} %shard_map.106.refs_3_, f32[1024,1024]{1,0:T(8,128)S(1)} %bitcast.20, ...), custom_call_target="tpu_custom_call" | custom-call | flops 805306368 | bytes 8388608 | tf_op jit(solution)/shard_map/pallas_call | solution.py:51
  (26 shorter events, 0.8 us)
Async XLA Ops:
  0.6 16.7 %copy-start.1 = (s32[4,4]{1,0:T(4,128)S(1)}, s32[4,4]{1,0:T(4,128)}, u32[]{:S(2)}) copy-start(s32[4,4]{1,0:T(4,128)} %refs_1_.1) | copy-start | bytes 196
  0.6 16.7 %copy-start.2 = (s32[4]{0:T(128)S(1)}, s32[4]{0:T(128)}, u32[]{:S(2)}) copy-start(s32[4]{0:T(128)} %refs_2_.1) | copy-start | bytes 52
  0.7 8.1 %collective-permute-start = (s32[4]{0:T(128)}, s32[4]{0:T(128)S(1)}, u32[]{:S(2)}, u32[]{:S(2)}) collective-permute-start(s32[4]{0:T(128)} %bitcast.28), channel_id=1, source_target_pairs={{1,2},{2,1},{3,4},{4,3},{5,6},{6,5},{9,10},{10,9},{11,12},{12,11},... | collective-permute-start | bytes 56 | tf_op jit(solution)/shard_map/ppermute | solution.py:27
  4.1 4.7 %collective-permute-start.1 = (s32[4]{0:T(128)}, s32[4]{0:T(128)S(1)}, u32[]{:S(2)}, u32[]{:S(2)}) collective-permute-start(s32[4]{0:T(128)} %bitcast.29), channel_id=1, source_target_pairs={{0,1},{1,0},{2,3},{3,2},{4,5},{5,4},{6,7},{7,6},{8,9},{9,8},{10,11... | collective-permute-start | bytes 56 | tf_op jit(solution)/shard_map/ppermute | solution.py:27
  5.8 3.7 %collective-permute-start.2 = (s32[4]{0:T(128)}, s32[4]{0:T(128)S(1)}, u32[]{:S(2)}, u32[]{:S(2)}) collective-permute-start(s32[4]{0:T(128)} %bitcast.30), channel_id=1, source_target_pairs={{0,2},{1,3},{2,0},{3,1},{4,6},{5,7},{6,4},{7,5},{8,10},{9,11},{10,... | collective-permute-start | bytes 56 | tf_op jit(solution)/shard_map/ppermute | solution.py:27
  5.8 5.6 %collective-permute-start.3 = (s32[4]{0:T(128)}, s32[4]{0:T(128)S(1)}, u32[]{:S(2)}, u32[]{:S(2)}) collective-permute-start(s32[4]{0:T(128)} %bitcast.31), channel_id=1, source_target_pairs={{2,4},{3,5},{4,2},{5,3},{10,12},{11,13},{12,10},{13,11},{18,20},{1... | collective-permute-start | bytes 56 | tf_op jit(solution)/shard_map/ppermute | solution.py:27
  13.4 15.1 %collective-permute-start.4 = (f32[128,1024]{1,0:T(8,128)S(1)}, f32[128,1024]{1,0:T(8,128)S(1)}, u32[]{:S(2)}, u32[]{:S(2)}) collective-permute-start(f32[128,1024]{1,0:T(8,128)S(1)} %get-tuple-element.24.refs_10_), channel_id=1, source_target_pairs={{0,1},{1,0},{2,3},{3,2},{4,5},{5,4},{6,7},{7,6},{8,9},{9,8},{10,11... | collective-permute-start | bytes 1572872 | tf_op jit(solution)/shard_map/ppermute | solution.py:27
  15.4 14.9 %collective-permute-start.5 = (f32[128,1024]{1,0:T(8,128)S(1)}, f32[128,1024]{1,0:T(8,128)S(1)}, u32[]{:S(2)}, u32[]{:S(2)}) collective-permute-start(f32[128,1024]{1,0:T(8,128)S(1)} %get-tuple-element.27), channel_id=1, source_target_pairs={{0,2},{1,3},{2,0},{3,1},{4,6},{5,7},{6,4},{7,5},{8,10},{9,11},{10,... | collective-permute-start | bytes 1572872 | tf_op jit(solution)/shard_map/ppermute | solution.py:27
  15.4 14.9 %collective-permute-start.6 = (f32[128,1024]{1,0:T(8,128)S(1)}, f32[128,1024]{1,0:T(8,128)S(1)}, u32[]{:S(2)}, u32[]{:S(2)}) collective-permute-start(f32[128,1024]{1,0:T(8,128)S(1)} %get-tuple-element.28), channel_id=1, source_target_pairs={{2,4},{3,5},{4,2},{5,3},{10,12},{11,13},{12,10},{13,11},{18,20},{1... | collective-permute-start | bytes 1572872 | tf_op jit(solution)/shard_map/ppermute | solution.py:27
  20.7 19.0 %collective-permute-start.7 = (f32[128,1024]{1,0:T(8,128)S(1)}, f32[128,1024]{1,0:T(8,128)S(1)}, u32[]{:S(2)}, u32[]{:S(2)}) collective-permute-start(f32[128,1024]{1,0:T(8,128)S(1)} %get-tuple-element.31), channel_id=1, source_target_pairs={{1,2},{2,1},{3,4},{4,3},{5,6},{6,5},{9,10},{10,9},{11,12},{12,11},... | collective-permute-start | bytes 1572872 | tf_op jit(solution)/shard_map/ppermute | solution.py:27
  24.2 22.5 %collective-permute-start.8 = (f32[512,512]{1,0:T(8,128)S(1)}, f32[512,512]{1,0:T(8,128)S(1)}, u32[]{:S(2)}, u32[]{:S(2)}) collective-permute-start(f32[512,512]{1,0:T(8,128)S(1)} %get-tuple-element.29.refs_11_), channel_id=1, source_target_pairs={{0,8},{8,16},{16,24},{24,0},{1,9},{9,17},{17,25},{25,1},{2,10},{10... | collective-permute-start | bytes 3145736 | tf_op jit(solution)/shard_map/ppermute | solution.py:32
  24.2 6.0 %copy-start = (f32[1,1024,1024]{2,1,0:T(8,128)S(1)}, f32[1,1024,1024]{2,1,0:T(8,128)}, u32[]{:S(2)}) copy-start(f32[1,1024,1024]{2,1,0:T(8,128)} %param.11) | copy-start | bytes 12582916
  42.7 14.3 %collective-permute-start.9 = (f32[512,512]{1,0:T(8,128)S(1)}, f32[512,512]{1,0:T(8,128)S(1)}, u32[]{:S(2)}, u32[]{:S(2)}) collective-permute-start(f32[512,512]{1,0:T(8,128)S(1)} %get-tuple-element.36), channel_id=1, source_target_pairs={{0,8},{8,16},{16,24},{24,0},{1,9},{9,17},{17,25},{25,1},{2,10},{10... | collective-permute-start | bytes 3145736 | tf_op jit(solution)/shard_map/ppermute | solution.py:32
  42.8 8.8 %collective-permute-start.11 = (f32[128,512]{1,0:T(8,128)S(1)}, f32[128,512]{1,0:T(8,128)S(1)}, u32[]{:S(2)}, u32[]{:S(2)}) collective-permute-start(f32[128,512]{1,0:T(8,128)S(1)} %get-tuple-element.39), channel_id=1, source_target_pairs={{0,1},{1,0},{2,3},{3,2},{4,5},{5,4},{6,7},{7,6},{8,9},{9,8},{10,11... | collective-permute-start | bytes 786440 | tf_op jit(solution)/shard_map/ppermute | solution.py:27
  42.9 8.8 %collective-permute-start.12 = (f32[128,512]{1,0:T(8,128)S(1)}, f32[128,512]{1,0:T(8,128)S(1)}, u32[]{:S(2)}, u32[]{:S(2)}) collective-permute-start(f32[128,512]{1,0:T(8,128)S(1)} %get-tuple-element.40), channel_id=1, source_target_pairs={{0,2},{1,3},{2,0},{3,1},{4,6},{5,7},{6,4},{7,5},{8,10},{9,11},{10,... | collective-permute-start | bytes 786440 | tf_op jit(solution)/shard_map/ppermute | solution.py:27
  42.9 10.7 %collective-permute-start.13 = (f32[128,512]{1,0:T(8,128)S(1)}, f32[128,512]{1,0:T(8,128)S(1)}, u32[]{:S(2)}, u32[]{:S(2)}) collective-permute-start(f32[128,512]{1,0:T(8,128)S(1)} %get-tuple-element.41), channel_id=1, source_target_pairs={{2,4},{3,5},{4,2},{5,3},{10,12},{11,13},{12,10},{13,11},{18,20},{1... | collective-permute-start | bytes 786440 | tf_op jit(solution)/shard_map/ppermute | solution.py:27
  46.7 14.0 %collective-permute-start.14 = (f32[128,512]{1,0:T(8,128)S(1)}, f32[128,512]{1,0:T(8,128)S(1)}, u32[]{:S(2)}, u32[]{:S(2)}) collective-permute-start(f32[128,512]{1,0:T(8,128)S(1)} %get-tuple-element.42), channel_id=1, source_target_pairs={{1,2},{2,1},{3,4},{4,3},{5,6},{6,5},{9,10},{10,9},{11,12},{12,11},... | collective-permute-start | bytes 786440 | tf_op jit(solution)/shard_map/ppermute | solution.py:27
  61.2 14.3 %collective-permute-start.15 = (f32[512,512]{1,0:T(8,128)S(1)}, f32[512,512]{1,0:T(8,128)S(1)}, u32[]{:S(2)}, u32[]{:S(2)}) collective-permute-start(f32[512,512]{1,0:T(8,128)S(1)} %shard_map.104), channel_id=1, source_target_pairs={{0,8},{8,16},{16,24},{24,0},{1,9},{9,17},{17,25},{25,1},{2,10},{10... | collective-permute-start | bytes 3145736 | tf_op jit(solution)/shard_map/ppermute | solution.py:32
  61.3 9.0 %collective-permute-start.10 = (f32[128,512]{1,0:T(8,128)S(1)}, f32[128,512]{1,0:T(8,128)S(1)}, u32[]{:S(2)}, u32[]{:S(2)}) collective-permute-start(f32[128,512]{1,0:T(8,128)S(1)} %get-tuple-element.37.refs_4_), channel_id=1, source_target_pairs={{0,1},{1,0},{2,3},{3,2},{4,5},{5,4},{6,7},{7,6},{8,9},{9,8},{10,11... | collective-permute-start | bytes 786440 | tf_op jit(solution)/shard_map/ppermute | solution.py:27
  61.3 16.0 %collective-permute-start.16 = (f32[128,512]{1,0:T(8,128)S(1)}, f32[128,512]{1,0:T(8,128)S(1)}, u32[]{:S(2)}, u32[]{:S(2)}) collective-permute-start(f32[128,512]{1,0:T(8,128)S(1)} %get-tuple-element.43), channel_id=1, source_target_pairs={{0,2},{1,3},{2,0},{3,1},{4,6},{5,7},{6,4},{7,5},{8,10},{9,11},{10,... | collective-permute-start | bytes 786440 | tf_op jit(solution)/shard_map/ppermute | solution.py:27
  61.4 15.9 %collective-permute-start.17 = (f32[128,512]{1,0:T(8,128)S(1)}, f32[128,512]{1,0:T(8,128)S(1)}, u32[]{:S(2)}, u32[]{:S(2)}) collective-permute-start(f32[128,512]{1,0:T(8,128)S(1)} %get-tuple-element.44), channel_id=1, source_target_pairs={{2,4},{3,5},{4,2},{5,3},{10,12},{11,13},{12,10},{13,11},{18,20},{1... | collective-permute-start | bytes 786440 | tf_op jit(solution)/shard_map/ppermute | solution.py:27
  65.2 14.5 %collective-permute-start.18 = (f32[128,512]{1,0:T(8,128)S(1)}, f32[128,512]{1,0:T(8,128)S(1)}, u32[]{:S(2)}, u32[]{:S(2)}) collective-permute-start(f32[128,512]{1,0:T(8,128)S(1)} %get-tuple-element.45), channel_id=1, source_target_pairs={{1,2},{2,1},{3,4},{4,3},{5,6},{6,5},{9,10},{10,9},{11,12},{12,11},... | collective-permute-start | bytes 786440 | tf_op jit(solution)/shard_map/ppermute | solution.py:27
